TPU v7x, 32 devices: a whole 2x2x4 slice. The times are simulated.
32 devices in a mesh: space: 16 (over z, y, core), kgrp: 2 (over x).
Axes of the slice: x: 2, y: 2, z: 4, core: 2. Of those that a mesh axis runs over, the one named last changes fastest.
Arguments:
- features: bfloat16 [4096, 128], P(('space', 'kgrp')), may hold values from -8 to 8, as said below
- positions: float32 [4096, 3], P('space'), may hold values from 0 to 512, as said below
- wave_index: int32 [1536, 3], P('kgrp'), may hold values from -12 to 12, as said below
- wave_filter: float32 [1536, 128], P('kgrp'), may hold values from 0.2 to 2
- mix_pair: bfloat16 [2, 128, 128], replicated, may hold values from -0.5 to 0.5
- msg_weight: bfloat16 [128, 128], replicated, may hold values from -0.5 to 0.5
- chan_width: float32 [128], replicated, may hold values from 1 to 30
- pair_dist: float32 [4096, 16], P(('space', 'kgrp')), may hold values from 1 to 25
- neighbours: int32 [4096, 16], P(('space', 'kgrp')), may hold values from 0 to 191, as said below
- norm_gain: float32 [128], replicated, may hold values from 0.1 to 1.9
- in_weight: bfloat16 [128, 512], replicated, may hold values from -0.5 to 0.5
- out_weight: bfloat16 [512, 128], replicated, may hold values from -0.25 to 0.25
Outputs:
- updated: bfloat16 [4096, 128], P(('space', 'kgrp'))
Inputs may be any that keep to these rules, and one draw needn't show every extreme that they name: Entries of the features are clipped to the range. `positions`: x and y lie in [0, 16); atom i has z in [i / 8, (i + 1) / 8). `wave_index`: the wave vectors are distinct and nonzero, one of each plus-minus k pair: each is lexicographically positive (first nonzero component positive). Rows of a device's extended block are its lower 32 wrapped neighbours' rows, its own 128 rows, then 32 upper ones; an atom at own row r lists rows r + 32 + o with 1 <= |o| <= 32.
All inputs are finite; a program needn't handle non-finite values.
Results may differ from a plain program's by a relative error of at most 0.008.
Values may be sent and summed in bfloat16 or wider, within the bound.
No kernel may reach another device: no remote copies, remote signals or barrier semaphores. Data moves between devices by JAX's collectives and lax.ppermute only.
A program may use at most 64 MiB of HBM per device.

v0:
```python
import math

import jax
import jax.numpy as jnp
from jax import lax
from jax.sharding import PartitionSpec as P

box_side = 16.0
slab_step = 0.125
two_pi = 2.0 * math.pi


def padded(shard, sides, width):
    for axis, dim in sides:
        size, length = (lax.axis_size(axis), shard.shape[dim])
        up = [(i, (i + 1) % size) for i in range(size)]
        down = [(j, i) for i, j in up]
        last = lax.slice_in_dim(shard, length - width, length, axis=dim)
        first = lax.slice_in_dim(shard, 0, width, axis=dim)
        before = lax.ppermute(last, axis, up)
        after = lax.ppermute(first, axis, down)
        shard = jnp.concatenate([before, shard, after], axis=dim)
    return shard


def wave_vectors(wave_index, slab_length):
    counts = wave_index.astype(jnp.float32)
    return jnp.stack(
        [
            counts[:, 0] * (two_pi / box_side),
            counts[:, 1] * (two_pi / box_side),
            counts[:, 2] * (two_pi / slab_length),
        ],
        axis=0,
    )


def phase_angles(points, wave_vecs):
    return (
        points[:, 0:1] * wave_vecs[0:1, :]
        + points[:, 1:2] * wave_vecs[1:2, :]
        + points[:, 2:3] * wave_vecs[2:3, :]
    )


def mix_vectors(s_re, s_im, mix_pair, wave_filter, scale):
    a_re = (s_re * scale).astype(jnp.bfloat16)
    a_im = (s_im * scale).astype(jnp.bfloat16)
    real_real = jnp.dot(a_re, mix_pair[0], preferred_element_type=jnp.float32)
    imag_imag = jnp.dot(a_im, mix_pair[1], preferred_element_type=jnp.float32)
    real_imag = jnp.dot(a_re, mix_pair[1], preferred_element_type=jnp.float32)
    imag_real = jnp.dot(a_im, mix_pair[0], preferred_element_type=jnp.float32)
    y_re = (wave_filter * (real_real - imag_imag)).astype(jnp.bfloat16)
    y_im = (wave_filter * (real_imag + imag_real)).astype(jnp.bfloat16)
    return (y_re, y_im)


def wave_terms(points, wave_vecs, y_re, y_im, inv_scale):
    angles = phase_angles(points, wave_vecs)
    cos_part = jnp.cos(angles).astype(jnp.bfloat16)
    sin_part = jnp.sin(angles).astype(jnp.bfloat16)
    summed = jnp.dot(cos_part, y_re, preferred_element_type=jnp.float32) + jnp.dot(
        sin_part, y_im, preferred_element_type=jnp.float32
    )
    return summed * inv_scale


def structure_piece(carry, piece, positions, wave_vecs):
    count = piece.shape[0]
    block = 512 if count % 512 == 0 else count
    dims = (((0,), (0,)), ((), ()))

    def one_block(block_id, totals):
        offset = (block_id * block).astype(jnp.int32)
        feat_block = lax.dynamic_slice_in_dim(piece, offset, block, 0)
        pos_block = lax.dynamic_slice_in_dim(positions, offset, block, 0)
        angles = phase_angles(pos_block, wave_vecs)
        cos_part = jnp.cos(angles).astype(jnp.bfloat16)
        sin_part = jnp.sin(angles).astype(jnp.bfloat16)
        new_re = totals[0] + lax.dot_general(
            cos_part, feat_block, dims, preferred_element_type=jnp.float32
        )
        new_im = totals[1] + lax.dot_general(
            sin_part, feat_block, dims, preferred_element_type=jnp.float32
        )
        return (new_re, new_im)

    return lax.fori_loop(0, count // block, one_block, carry)


def local(
    features,
    positions,
    wave_index,
    wave_filter,
    mix_pair,
    msg_weight,
    chan_width,
    pair_dist,
    neighbours,
    norm_gain,
    in_weight,
    out_weight,
):
    atom_dev = features.shape[0]
    channels = features.shape[1]
    groups = lax.axis_size("kgrp")
    total_atoms = atom_dev * groups * lax.axis_size("space")
    halo_width = atom_dev // 4
    projected = jnp.dot(features, msg_weight, preferred_element_type=jnp.float32).astype(
        jnp.bfloat16
    )
    extended = padded(projected, ((("space", "kgrp"), 0),), halo_width)
    nearby = jnp.take(extended, neighbours, axis=0)
    weights = jnp.exp(-pair_dist[:, :, None] / chan_width[None, None, :])
    message = jnp.sum(weights * nearby.astype(jnp.float32), axis=1)
    wave_vecs = wave_vectors(wave_index, total_atoms * slab_step)
    wave_count = wave_index.shape[0]
    zeros = jnp.zeros((wave_count, channels), jnp.float32)
    partial_sums = structure_piece(
        (zeros, zeros), lax.all_gather(features, "kgrp", axis=0, tiled=True), positions, wave_vecs
    )
    scale = 1.0 / math.sqrt(total_atoms)
    s_re, s_im = lax.psum((partial_sums[0], partial_sums[1]), "space")
    y_re, y_im = mix_vectors(s_re, s_im, mix_pair, wave_filter, scale)
    inv_scale = 1.0 / math.sqrt(wave_count * groups)
    count = lax.axis_size("kgrp") * atom_dev
    block = 512 if count % 512 == 0 else count
    stacked = positions.reshape(count // block, block, 3)
    terms = lax.map(
        lambda group_points: wave_terms(group_points, wave_vecs, y_re, y_im, inv_scale), stacked
    )
    ewald = lax.psum_scatter(
        terms.reshape(count, channels).astype(jnp.bfloat16), "kgrp", scatter_dimension=0, tiled=True
    ).astype(jnp.float32)
    mixed = features.astype(jnp.float32) + message + ewald
    inverse = lax.rsqrt(jnp.mean(mixed * mixed, axis=1, keepdims=True) + 1e-06)
    normed = (mixed * inverse * norm_gain).astype(jnp.bfloat16)
    hidden = jax.nn.silu(jnp.dot(normed, in_weight, preferred_element_type=jnp.float32)).astype(
        jnp.bfloat16
    )
    return (mixed + jnp.dot(hidden, out_weight, preferred_element_type=jnp.float32)).astype(
        jnp.bfloat16
    )


def solution(mesh):
    placed = (
        P(("space", "kgrp"), None),
        P("space", None),
        P("kgrp", None),
        P("kgrp", None),
        P(),
        P(),
        P(),
        P(("space", "kgrp"), None),
        P(("space", "kgrp"), None),
        P(),
        P(),
        P(),
    )
    return jax.shard_map(
        local, mesh=mesh, in_specs=placed, out_specs=P(("space", "kgrp"), None), check_vma=False
    )
```

profile of v0, /device:TPU:0, one launch (start us, length us, event | category | flops | bytes accessed | tf_op | source)
XLA Modules:
  0.0 144.7 jit_solution(14038815412444516779)
XLA Ops:
  6.5 0.9 convolution_convert_fusion
  7.5 0.0 copy-start.2
  7.5 3.0 %collective-permute-start = (bf16[32,128]{1,0:T(8,128)(2,1)S(1)}, bf16[32,128]{1,0:T(8,128)(2,1)S(1)}, u32[]{:S(2)}, u32[]{:S(2)}) collective-permute-start(bf16[32,128]{1,0:T(8,128)(2,1)S(1)} %get-tuple-element.43), channel_id=1, source_target_pairs={{0,1},{1,2},{2,3},{3,4},{4,5},{5,6},{6,7},{7,8},{8,9},{9,10},{10,1... | collective-permute-start | bytes 24584 | tf_op jit(solution)/shard_map/ppermute | solution.py:20
  10.5 3.5 %collective-permute-start.1 = (bf16[32,128]{1,0:T(8,128)(2,1)S(1)}, bf16[32,128]{1,0:T(8,128)(2,1)S(1)}, u32[]{:S(2)}, u32[]{:S(2)}) collective-permute-start(bf16[32,128]{1,0:T(8,128)(2,1)S(1)} %get-tuple-element.52), channel_id=1, source_target_pairs={{1,0},{2,1},{3,2},{4,3},{5,4},{6,5},{7,6},{8,7},{9,8},{10,9},{11,1... | collective-permute-start | bytes 24584 | tf_op jit(solution)/shard_map/ppermute | solution.py:21
  14.0 4.6 %all_gather.3 = bf16[256,128]{1,0:T(8,128)(2,1)S(1)} all-gather(bf16[128,128]{1,0:T(8,128)(2,1)S(1)} %copy-done.2), channel_id=1, replica_groups=mesh['space'=16,'kgrp'=2] {'kgrp'}, dimensions={0}, use_global_device_ids=true | all-gather | bytes 98304 | tf_op jit(solution)/shard_map/all_gather | solution.py:121
  18.7 0.6 copy-done.8
  19.3 3.7 %fusion.13 = f32[768,128]{1,0:T(8,128)} fusion(bf16[256,128]{1,0:T(8,128)(2,1)S(1)} %all_gather.3, f32[768]{0:T(1024)S(1)} %get-tuple-element.39, f32[256]{0:T(256)S(1)} %bitcast.27, f32[768]{0:T(1024)S(1)} %get-tuple-element.40, f32[256]{0:T(256)S(1)} %bitcast.31, f32[768]{0:T(1024)S(1)} %get-tuple-element.38, f32[256]{0:T(256)S(1)} %bitcast.23), kind=kOutput, calls=%fused_computation.25 | convolution fusion | flops 51511296 | bytes 471040 | tf_op jit(solution)/shard_map/while/body/eval_jaxpr/dot_general | solution.py:83
  23.0 3.7 %fusion.12 = f32[768,128]{1,0:T(8,128)} fusion(bf16[256,128]{1,0:T(8,128)(2,1)S(1)} %all_gather.3, f32[768]{0:T(1024)S(1)} %get-tuple-element.39, f32[256]{0:T(256)S(1)} %bitcast.28, f32[768]{0:T(1024)S(1)} %get-tuple-element.40, f32[256]{0:T(256)S(1)} %bitcast.32, f32[768]{0:T(1024)S(1)} %get-tuple-element.38, f32[256]{0:T(256)S(1)} %bitcast.24), kind=kOutput, calls=%fused_computation.24 | convolution fusion | flops 51511296 | bytes 471040 | tf_op jit(solution)/shard_map/while/body/eval_jaxpr/dot_general | solution.py:80
  26.7 0.0 all-reduce.3.cloned.1.call-update
  26.7 0.2 reduce-scatter.2.cloned.1.call-start
  27.0 0.4 copy-done.4
  27.4 0.1 copy.17
  27.5 0.1 reshape.45
  27.6 0.7 copy-done.7
  28.3 0.1 copy.15
  28.4 0.1 copy.16
  28.6 6.2 %gather_fusion = bf16[2048,128]{1,0:T(8,128)(2,1)S(1)} fusion(bf16[192,128]{1,0:T(8,128)(2,1)S(1)} %pad_maximum_fusion, s32[2048]{0:T(1024)S(1)} %broadcast_clamp_fusion), kind=kCustom, calls=%fused_computation | custom fusion | bytes 1056768 | tf_op jit(solution)/shard_map/jit(_take)/gather | solution.py:114
  34.8 82.6 %all-reduce.3.cloned.1.call-done = (f32[768,128]{1,0:T(8,128)}, f32[768,128]{1,0:T(8,128)}) async-done(((f32[768,128]{1,0:T(8,128)}, f32[768,128]{1,0:T(8,128)}), (f32[768,128]{1,0:T(8,128)}, f32[768,128]{1,0:T(8,128)})) %all-reduce.3.cloned.1.call-update) | async-done | bytes 786448 | tf_op jit(solution)/shard_map/psum | solution.py:124
  117.4 1.3 fusion.15
  118.6 0.0 copy-start.10
  118.7 0.2 fusion.14
  118.8 0.8 copy-done.10
  119.6 0.1 copy-done.11
  119.8 2.9 %fusion.4 = f32[256,128]{1,0:T(8,128)S(1)} fusion(f32[768,128]{1,0:T(8,128)S(1)} %copy-done.10, f32[768,128]{1,0:T(8,128)S(1)} %fusion.15, f32[768]{0:T(1024)S(1)} %get-tuple-element.39, f32[256]{0:T(256)S(1)} %bitcast.29, f32[768]{0:T(1024)S(1)} %get-tuple-element.40, f32[256]{0:T(256)S(1)} %bitcast.33, f32[768]{0:T(1024)S(1)} %get-tuple-element.38, ...), kind=kOutput, calls=%fused_computation.7 | convolution fusion | flops 77168640 | bytes 1358848 | tf_op jit(solution)/shard_map/while/body/eval_jaxpr/dot_general | solution.py:62
  122.7 3.6 %fusion.8 = bf16[256,128]{1,0:T(8,128)(2,1)} fusion(f32[256,128]{1,0:T(8,128)S(1)} %fusion.4, f32[768,128]{1,0:T(8,128)S(1)} %copy-done.10, f32[768,128]{1,0:T(8,128)S(1)} %fusion.14, f32[768]{0:T(1024)S(1)} %get-tuple-element.39, f32[256]{0:T(256)S(1)} %bitcast.30, f32[768]{0:T(1024)S(1)} %get-tuple-element.40, f32[256]{0:T(256)S(1)} %bitcast.34, ...), kind=kOutput, calls=%fused_computation.11 | convolution fusion | flops 77266944 | bytes 1424384 | tf_op jit(solution)/shard_map/while/body/eval_jaxpr/dot_general | solution.py:62
  126.2 0.0 reduce-scatter.2.cloned.1.call-update
  126.2 0.6 copy-done.9
  126.9 0.8 fusion.11
  127.7 7.6 %reduce-scatter.2.cloned.1.call-done = bf16[128,128]{1,0:T(8,128)(2,1)} async-done(((bf16[256,128]{1,0:T(8,128)(2,1)}), bf16[128,128]{1,0:T(8,128)(2,1)}) %reduce-scatter.2.cloned.1.call-update) | async-done | bytes 32784 | tf_op jit(solution)/shard_map/reduce_scatter | solution.py:133
  135.2 0.9 multiply_reduce_fusion
  136.2 0.6 copy-done.13
  136.8 1.0 fusion.9
  (32 shorter events, 0.1 us)
Async XLA Ops:
  6.5 129.7 %copy-start = (bf16[512,128]{1,0:T(8,128)(2,1)S(1)}, bf16[512,128]{1,0:T(8,128)(2,1)}, u32[]{:S(2)}) copy-start(bf16[512,128]{1,0:T(8,128)(2,1)} %param.23) | copy-start | bytes 393220
  6.5 110.8 %all-reduce.3.cloned.1.call-start = ((), (), s32[]{:S(2)}) async-start(), calls=%async_computation.2 | async-start | bytes 1572864 | tf_op jit(solution)/shard_map/psum | solution.py:124
  7.5 6.6 %copy-start.2 = (bf16[128,128]{1,0:T(8,128)(2,1)S(1)}, bf16[128,128]{1,0:T(8,128)(2,1)}, u32[]{:S(2)}) copy-start(bf16[128,128]{1,0:T(8,128)(2,1)} %param.12) | copy-start | bytes 98308
  7.5 21.0 %collective-permute-start = (bf16[32,128]{1,0:T(8,128)(2,1)S(1)}, bf16[32,128]{1,0:T(8,128)(2,1)S(1)}, u32[]{:S(2)}, u32[]{:S(2)}) collective-permute-start(bf16[32,128]{1,0:T(8,128)(2,1)S(1)} %get-tuple-element.43), channel_id=1, source_target_pairs={{0,1},{1,2},{2,3},{3,4},{4,5},{5,6},{6,7},{7,8},{8,9},{9,10},{10,1... | collective-permute-start | bytes 24584 | tf_op jit(solution)/shard_map/ppermute | solution.py:20
  10.5 8.1 %copy-start.6 = (s32[768,3]{0,1:T(4,128)S(1)}, s32[768,3]{0,1:T(4,128)}, u32[]{:S(2)}) copy-start(s32[768,3]{0,1:T(4,128)} %param.14) | copy-start | bytes 27652
  10.5 18.0 %collective-permute-start.1 = (bf16[32,128]{1,0:T(8,128)(2,1)S(1)}, bf16[32,128]{1,0:T(8,128)(2,1)S(1)}, u32[]{:S(2)}, u32[]{:S(2)}) collective-permute-start(bf16[32,128]{1,0:T(8,128)(2,1)S(1)} %get-tuple-element.52), channel_id=1, source_target_pairs={{1,0},{2,1},{3,2},{4,3},{5,4},{6,5},{7,6},{8,7},{9,8},{10,9},{11,1... | collective-permute-start | bytes 24584 | tf_op jit(solution)/shard_map/ppermute | solution.py:21
  18.6 0.7 copy-start.8
  26.7 0.7 copy-start.4
  26.7 108.5 %reduce-scatter.2.cloned.1.call-start = ((), (), s32[]{:S(2)}) async-start(), calls=%async_computation.1 | async-start | bytes 98304 | tf_op jit(solution)/shard_map/reduce_scatter | solution.py:133
  27.6 0.7 copy-start.7
  28.6 88.8 %copy-start.3 = (bf16[2,128,128]{2,1,0:T(8,128)(2,1)S(1)}, bf16[2,128,128]{2,1,0:T(8,128)(2,1)}, u32[]{:S(2)}) copy-start(bf16[2,128,128]{2,1,0:T(8,128)(2,1)} %param.16) | copy-start | bytes 196612
  117.4 1.3 copy-start.1
  118.6 1.0 copy-start.10
  118.6 1.1 copy-start.11
  126.2 0.7 copy-start.9
  126.9 9.3 %copy-start.12 = (bf16[128,512]{1,0:T(8,128)(2,1)S(1)}, bf16[128,512]{1,0:T(8,128)(2,1)}, u32[]{:S(2)}) copy-start(bf16[128,512]{1,0:T(8,128)(2,1)} %param.22) | copy-start | bytes 393220
  135.2 1.0 copy-start.5
  136.2 0.7 copy-start.13
Sparse Core Ops, SparseCore 0:
  26.8 90.4 all-reduce.2
  126.4 8.8 reduce-scatter.1
where the time goes:
time: 145 us
  waiting for transfers between devices  90.2 us (62%)
  matrix products  17.2 us (12%)
  between operations  13.6 us (9%)
  local copies, waits for them, and re-layouts  10.6 us (7%)
  starting transfers between devices  6.74 us (5%)
  blocking collectives  4.58 us (3%)
  other arithmetic  1.77 us (1%)
    psum x1, waiting for transfers between devices, local(): s_re, s_im = lax.psum((partial_sums[0], partial_sums[1]), 'space')  82.6 us
    reduce_scatter x1, waiting for transfers between devices, local(): lax.psum_scatter(terms.reshape(count, channels).astype(jnp.bfloat16), 'kg...  7.57 us
    gather x1, local copies, waits for them, and re-layouts, local(): nearby = jnp.take(extended, neighbours, axis=0)  6.18 us
    all_gather x1, blocking collectives, local(): lax.all_gather(features, 'kgrp', axis=0, tiled=True)  4.58 us
    unnamed x28, local copies, waits for them, and re-layouts  3.95 us
    dot_general x1, matrix products, one_block(): lax.dot_general(sin_part, feat_block, dims, preferred_element_type=jnp.fl...  3.7 us
    dot_general x1, matrix products, one_block(): lax.dot_general(cos_part, feat_block, dims, preferred_element_type=jnp.fl...  3.68 us
    dot_general x1, matrix products, wave_terms(): jnp.dot(sin_part, y_im, preferred_element_type=jnp.float32)  3.57 us
  transfers between devices with their start and end apart: 4, of which 2 were waited for; matrix products, arithmetic and copies ran while one was open for 10% of the time, Pallas kernels for 0%

commit v1 on v0

v1 whole, which is shorter than its diff:
```python
import functools
import math

import jax
import jax.numpy as jnp
import numpy as np
from jax import lax
from jax.experimental import pallas as pl
from jax.experimental.pallas import tpu as pltpu
from jax.sharding import PartitionSpec as P

box_side = 16.0
slab_step = 0.125
coord_rows = 16
bf16, f32 = jnp.bfloat16, jnp.float32

both = ("space", "kgrp")

def fit_cosine(degree):
    count = 64
    theta = (np.arange(count) + 0.5) * math.pi / count
    u = 0.125 * (1.0 + np.cos(theta))
    values = np.cos(2.0 * math.pi * np.sqrt(u))
    cheb = np.polynomial.chebyshev.Chebyshev.fit(u, values, degree, domain=[0.0, 0.25])
    return [float(c) for c in cheb.convert(kind=np.polynomial.Polynomial).coef]


cosine = fit_cosine(6)


def dot(a, b, dims):
    return lax.dot_general(a, b, (dims, ((), ())), preferred_element_type=f32)


def whole(count):
    return [pl.BlockSpec(memory_space=pltpu.VMEM)] * count


def call(body, outs, *args, flops=0, transcendentals=0):
    moved = sum(a.size * a.dtype.itemsize for a in (*args, *outs))
    return pl.pallas_call(
        body,
        out_shape=outs if len(outs) > 1 else outs[0],
        in_specs=whole(len(args)),
        out_specs=whole(len(outs)) if len(outs) > 1 else whole(1)[0],
        cost_estimate=pl.CostEstimate(
            flops=flops, bytes_accessed=moved, transcendentals=transcendentals
        ),
        compiler_params=pltpu.CompilerParams(vmem_limit_bytes=24 * 1024 * 1024),
    )(*args)


def shape(dims, dtype):
    return jax.ShapeDtypeStruct(dims, dtype)


def payload_body(slab_length, feat_ref, pos_ref, out_ref):
    atoms = feat_ref.shape[0]
    group = lax.axis_index("kgrp")
    out_ref[:atoms, :] = feat_ref[...]
    own = pos_ref[:, pl.ds(pl.multiple_of(group * atoms, atoms), atoms)]
    row = lax.broadcasted_iota(jnp.int32, own.shape, 0)
    turns = own * jnp.where(row == 2, 1.0 / slab_length, 1.0 / box_side)
    high = turns.astype(bf16).astype(f32)
    rest = turns - high
    middle = rest.astype(bf16).astype(f32)
    low = rest - middle
    ones = jnp.ones((1, atoms), f32)
    zeros = jnp.zeros((coord_rows - 10, atoms), f32)
    parts = jnp.concatenate([high, middle, low, ones, zeros], axis=0)
    out_ref[atoms:, :] = parts.astype(bf16)


def structure_body(blocks, carried, *refs):
    block_refs, (wave_ref, *refs) = refs[:blocks], refs[blocks:]
    carry_ref = None
    if carried:
        carry_ref, *refs = refs
    phase_ref, sum_ref = refs
    atoms = block_refs[0].shape[0] - coord_rows
    total = None if carry_ref is None else carry_ref[...]
    for i, ref in enumerate(block_refs):
        turns = dot(ref[atoms:, :], wave_ref[...], ((0,), (0,)))
        part = turns - jnp.round(turns)
        u = part * part
        value = jnp.full_like(u, cosine[-1])
        for c in cosine[-2::-1]:
            value = value * u + c
        phase = value.astype(bf16)
        phase_ref[i * atoms : (i + 1) * atoms, :] = phase
        term = dot(ref[:atoms, :], phase, ((0,), (0,)))
        total = term if total is None else total + term
    sum_ref[...] = total.astype(sum_ref.dtype)


def structure(blocks, waves, carry):
    atoms, channels = blocks[0].shape[0] - coord_rows, blocks[0].shape[1]
    columns = waves.shape[1]
    outs = (
        shape((len(blocks) * atoms, columns), bf16),
        shape((channels, columns), f32 if carry is None else bf16),
    )
    extra = () if carry is None else (carry,)
    work = len(blocks) * atoms * columns
    return call(
        functools.partial(structure_body, len(blocks), carry is not None),
        outs,
        *blocks,
        waves,
        *extra,
        flops=2 * work * (channels + coord_rows) + 16 * work,
    )


def ewald_body(scale, inv_scale, a_ref, b_ref, mix_ref, filter_ref, near_ref, far_ref, keep_ref, send_ref):
    total = (a_ref[...].astype(f32) + b_ref[...].astype(f32)) * scale
    amps = total.astype(bf16)
    columns = amps.shape[1]
    straight = dot(mix_ref[0], amps, ((0,), (0,)))
    crossed = dot(mix_ref[1], amps, ((0,), (0,)))
    half = columns // 2
    crossed = jnp.concatenate([-crossed[:, half:], crossed[:, :half]], axis=1)
    y = (filter_ref[...] * (straight + crossed)).astype(bf16)
    send_ref[...] = (dot(far_ref[...], y, ((1,), (1,))) * inv_scale).astype(bf16)
    keep_ref[...] = dot(near_ref[...], y, ((1,), (1,))) * inv_scale


def message_body(feat_ref, before_ref, after_ref, msg_ref, width_ref, dist_ref, nbr_ref, base_ref):
    atoms = feat_ref.shape[0]
    extended = jnp.concatenate([before_ref[...], feat_ref[...], after_ref[...]], axis=0)
    projected = dot(msg_ref[...], extended, ((0,), (1,))).astype(bf16)
    rows = extended.shape[0]
    row = lax.broadcasted_iota(jnp.int32, (rows, atoms), 0)
    inverse = -1.0 / width_ref[...]
    message = jnp.zeros((projected.shape[0], atoms), f32)
    for j in range(nbr_ref.shape[0]):
        chosen = jnp.where(row == nbr_ref[j : j + 1, :], 1.0, 0.0).astype(bf16)
        nearby = dot(projected, chosen, ((1,), (0,)))
        message = message + jnp.exp(dist_ref[j : j + 1, :] * inverse) * nearby
    base_ref[...] = feat_ref[...].astype(f32) + message.T


def final_body(peers, *refs):
    base_ref, *refs = refs
    peer_refs, (gain_ref, in_ref, out_ref, result_ref) = refs[:peers], refs[peers:]
    mixed = base_ref[...]
    for ref in peer_refs:
        mixed = mixed + ref[...].astype(f32)
    inverse = lax.rsqrt(jnp.mean(mixed * mixed, axis=1, keepdims=True) + 1e-06)
    normed = (mixed * inverse * gain_ref[...]).astype(bf16)
    hidden = dot(normed, in_ref[...], ((1,), (0,)))
    hidden = (hidden * (1.0 / (1.0 + jnp.exp(-hidden)))).astype(bf16)
    result_ref[...] = (mixed + dot(hidden, out_ref[...], ((1,), (0,)))).astype(bf16)


def local(
    outer,
    features,
    positions,
    wave_index,
    wave_filter,
    mix_pair,
    msg_weight,
    chan_width,
    pair_dist,
    neighbours,
    norm_gain,
    in_weight,
    out_weight,
):
    atoms, channels = features.shape
    groups, space = lax.axis_size("kgrp"), lax.axis_size("space")
    inner = space // outer
    members = inner * groups
    devices = space * groups
    total_atoms = atoms * devices
    halo = atoms // 4
    slab_length = total_atoms * slab_step
    own_space = lax.axis_index("space")
    member = (own_space * groups + lax.axis_index("kgrp")) % members

    def swap(x, mask):
        return lax.ppermute(x, both, [(i, i ^ mask) for i in range(devices)])

    near = [m for m in range(members) if not m & groups]
    sent = call(
        functools.partial(payload_body, slab_length),
        (shape((atoms + coord_rows, channels), bf16),),
        features,
        positions.T,
    )
    near_blocks = [sent] + [swap(sent, m) for m in near[1:]]
    far_blocks = [swap(block, groups) for block in near_blocks]
    of_mask = {m: b for m, b in zip(near, near_blocks)}
    of_mask.update({m ^ groups: b for m, b in zip(near, far_blocks)})

    share = wave_index.shape[0] // inner
    first = (own_space % inner) * share
    counts = lax.dynamic_slice_in_dim(wave_index.T, first, share, 1).astype(f32)
    counts = jnp.concatenate([counts, counts], axis=1)
    quarter = jnp.where(jnp.arange(2 * share)[None, :] < share, 0.0, -0.25)
    zeros = jnp.zeros((coord_rows - 10, 2 * share), f32)
    waves = jnp.concatenate([counts, counts, counts, quarter, zeros], axis=0).astype(bf16)
    filters = lax.dynamic_slice_in_dim(wave_filter, first, share, 0).T
    filters = jnp.concatenate([filters, filters], axis=1)

    near_phase, near_sum = structure(near_blocks, waves, None)
    far_phase, amps = structure(far_blocks, waves, near_sum)

    step = 1
    while 2 * step < outer:
        other = swap(amps, (2 * step - 1) * members)
        amps = (amps.astype(f32) + other.astype(f32)).astype(bf16)
        step *= 2
    if outer > 1:
        other = swap(amps, (2 * step - 1) * members)
    else:
        other = jnp.zeros_like(amps)

    columns = 2 * share
    half = len(near) * atoms
    keep, send = call(
        functools.partial(
            ewald_body, 1.0 / math.sqrt(total_atoms), 1.0 / math.sqrt(wave_index.shape[0] * groups)
        ),
        (shape((half, channels), f32), shape((half, channels), bf16)),
        amps,
        other,
        mix_pair,
        filters,
        near_phase,
        far_phase,
        flops=2 * channels * columns * (2 * channels + 2 * half),
    )
    came = swap(send, groups)
    terms = keep + came.astype(f32)
    peers = [terms[:atoms]]
    for i, m in enumerate(near[1:], 1):
        peers.append(swap(terms[i * atoms : (i + 1) * atoms].astype(bf16), m))

    edge = jnp.where(member == 0, features[:halo], features[atoms - halo :])
    pairs = []
    for layer in range(outer):
        above = (layer + 1) % outer
        pairs.append((layer * members + members - 1, above * members))
        pairs.append((above * members, layer * members + members - 1))
    before = after = lax.ppermute(edge, both, pairs)
    mask = 1
    while mask < members:
        block = of_mask[mask]
        span = (mask + 1) // 2
        before = jnp.where(member % (2 * span) == span, block[atoms - halo : atoms], before)
        after = jnp.where((member + 1) % (2 * span) == span, block[:halo], after)
        mask = 2 * mask + 1
    slots = neighbours.shape[1]
    base = call(
        message_body,
        (shape((atoms, channels), f32),),
        features,
        before,
        after,
        msg_weight,
        chan_width.reshape(channels, 1),
        pair_dist.T,
        neighbours.T,
        flops=2 * channels * atoms * slots * (atoms + 2 * halo),
        transcendentals=atoms * slots * channels,
    )
    return call(
        functools.partial(final_body, len(peers)),
        (shape((atoms, channels), bf16),),
        base,
        *peers,
        norm_gain.reshape(1, channels),
        in_weight,
        out_weight,
        flops=4 * atoms * channels * in_weight.shape[1],
    )


def layers(mesh):
    depths = {getattr(d, "coords", (0, 0, i))[2] for i, d in enumerate(mesh.devices[:, 0])}
    return len(depths)


def solution(mesh):
    placed = (
        P(both, None),
        P("space", None),
        P("kgrp", None),
        P("kgrp", None),
        P(),
        P(),
        P(),
        P(both, None),
        P(both, None),
        P(),
        P(),
        P(),
    )
    return jax.shard_map(
        functools.partial(local, layers(mesh)),
        mesh=mesh,
        in_specs=placed,
        out_specs=P(both, None),
        check_vma=False,
    )
```

time: 145 us -> 39.3 us (0.27)
  waiting for transfers between devices: 90.2 us -> 11.1 us
  matrix products: 17.2 us -> 0 us
  between operations: 13.6 us -> 0.35 us
  starting transfers between devices: 6.74 us -> 19.4 us
  local copies, waits for them, and re-layouts: 10.6 us -> 2.58 us
  blocking collectives: 4.58 us -> 0 us
  Pallas kernels: 0 us -> 4.5 us
    psum x1 -> x0, waiting for transfers between devices: 82.6 us -> none  [local(): s_re, s_im = lax.psum((partial_sums[0], partial_sums[1]), 'space')]
    dot_general x8 -> x0, matrix products: 17.2 us -> none  [the longest x1 3.7 us: one_block(): lax.dot_general(sin_part, feat_block, dims, preferred_element_type=jnp.fl...]
    ppermute x2 -> x14, starting transfers between devices: 6.52 us -> 19.4 us  [the longest x13 13.7 us: swap(): return lax.ppermute(x, both, [(i, i ^ mask) for i in range(devices)])]
    ppermute x2 -> x14, waiting for transfers between devices: 0.01 us -> 11.1 us  [the longest x13 11.1 us: swap(): return lax.ppermute(x, both, [(i, i ^ mask) for i in range(devices)])]
    reduce_scatter x1 -> x0, waiting for transfers between devices: 7.57 us -> none  [local(): lax.psum_scatter(terms.reshape(count, channels).astype(jnp.bfloat16), 'kg...]
    gather x1 -> x0, local copies, waits for them, and re-layouts: 6.18 us -> none  [local(): nearby = jnp.take(extended, neighbours, axis=0)]
    all_gather x1 -> x0, blocking collectives: 4.58 us -> none  [local(): lax.all_gather(features, 'kgrp', axis=0, tiled=True)]
    pallas_call x0 -> x6, Pallas kernels: none -> 4.5 us  [call(): pl.pallas_call(body, out_shape=outs if len(outs) > 1 else outs[0], in_spe...]
  transfers between devices with their start and end apart: 4 -> 14, of which waited for: 2 -> 6; matrix products, arithmetic and copies ran while one was open for 10% -> 4% of each run, Pallas kernels for 0% -> 4%
where the time goes in v1:
time: 39.3 us; the launch traced here: 39 us
  starting transfers between devices  19.4 us (49%)
  waiting for transfers between devices  11.1 us (28%)
  Pallas kernels  4.5 us (11%)
  local copies, waits for them, and re-layouts  2.58 us (7%)
  other arithmetic  1.03 us (3%)
    ppermute x13, starting transfers between devices, swap(): return lax.ppermute(x, both, [(i, i ^ mask) for i in range(devices)])  13.7 us
    ppermute x13, waiting for transfers between devices, swap(): return lax.ppermute(x, both, [(i, i ^ mask) for i in range(devices)])  11.1 us
    ppermute x1, starting transfers between devices, local(): before = after = lax.ppermute(edge, both, pairs)  5.76 us
    pallas_call x6, Pallas kernels, call(): pl.pallas_call(body, out_shape=outs if len(outs) > 1 else outs[0], in_spe...  4.5 us
    unnamed x25, local copies, waits for them, and re-layouts  2.3 us
  transfers between devices with their start and end apart: 14, of which 6 were waited for; matrix products, arithmetic and copies ran while one was open for 4% of the time, Pallas kernels for 4%

profile of v1, /device:TPU:0, one launch (start us, length us, event | category | flops | bytes accessed | tf_op | source)
XLA Modules:
  0.0 39.0 jit_solution(8489313667249657159)
XLA Ops:
  0.0 0.8 %copy-done.3 = bf16[128,128]{1,0:T(8,128)(2,1)S(1)} copy-done((bf16[128,128]{1,0:T(8,128)(2,1)S(1)}, bf16[128,128]{1,0:T(8,128)(2,1)}, u32[]{:S(2)}) %copy-start.3) | copy-done | bytes 32792
  0.8 0.7 %copy-done.6 = f32[256,3]{0,1:T(4,128)S(1)} copy-done((f32[256,3]{0,1:T(4,128)S(1)}, f32[256,3]{0,1:T(4,128)}, u32[]{:S(2)}) %copy-start.6) | copy-done | bytes 3096
  1.5 3.0 %collective-permute-start.6 = (bf16[144,128]{1,0:T(8,128)(2,1)S(1)}, bf16[144,128]{1,0:T(8,128)(2,1)S(1)}, u32[]{:S(2)}, u32[]{:S(2)}) collective-permute-start(bf16[144,128]{1,0:T(8,128)(2,1)S(1)} %shard_map.118.refs_0_), channel_id=1, source_target_pairs={{0,4},{1,5},{2,6},{3,7},{4,0},{5,1},{6,2},{7,3},{8,12},{9,13},{10,... | collective-permute-start | bytes 110600 | tf_op jit(solution)/shard_map/ppermute | solution.py:183
  4.5 1.5 %collective-permute-start.2 = (bf16[144,128]{1,0:T(8,128)(2,1)S(1)}, bf16[144,128]{1,0:T(8,128)(2,1)S(1)}, u32[]{:S(2)}, u32[]{:S(2)}) collective-permute-start(bf16[144,128]{1,0:T(8,128)(2,1)S(1)} %shard_map.118.refs_0_), channel_id=1, source_target_pairs={{0,1},{1,0},{2,3},{3,2},{4,5},{5,4},{6,7},{7,6},{8,9},{9,8},{10,11... | collective-permute-start | bytes 110600 | tf_op jit(solution)/shard_map/ppermute | solution.py:183
  6.0 0.1 collective-permute-start
  6.2 0.8 %convert_bitcast_fusion = bf16[3,192]{1,0:T(4,128)(2,1)S(1)} fusion(s32[768,3]{0,1:T(4,128)} %param.14, s32[]{:T(128)S(6)} %select_n.117), kind=kLoop, calls=%fused_computation.12 | loop fusion | flops 576 | bytes 3460 | tf_op jit(solution)/shard_map/convert_element_type | solution.py:199
  6.9 0.1 maximum_convert_fusion
  7.0 0.1 collective-permute-start.7
  7.1 1.4 %collective-permute-done.2.refs_1_ = bf16[144,128]{1,0:T(8,128)(2,1)S(1)} collective-permute-done((bf16[144,128]{1,0:T(8,128)(2,1)S(1)}, bf16[144,128]{1,0:T(8,128)(2,1)S(1)}, u32[]{:S(2)}, u32[]{:S(2)}) %collective-permute-start.2) | collective-permute-done | bytes 36896 | tf_op jit(solution)/shard_map/ppermute | solution.py:183
  8.5 2.4 %collective-permute-done.refs_3_ = bf16[144,128]{1,0:T(8,128)(2,1)S(1)} collective-permute-done((bf16[144,128]{1,0:T(8,128)(2,1)S(1)}, bf16[144,128]{1,0:T(8,128)(2,1)S(1)}, u32[]{:S(2)}, u32[]{:S(2)}) %collective-permute-start) | collective-permute-done | bytes 36896 | tf_op jit(solution)/shard_map/ppermute | solution.py:183
  10.9 0.1 concatenate.11.refs_4_
  11.1 1.0 %shard_map.120 = (bf16[512,384]{1,0:T(8,128)(2,1)S(1)}, f32[128,384]{1,0:T(8,128)S(1)}) custom-call(bf16[144,128]{1,0:T(8,128)(2,1)S(1)} %shard_map.118.refs_0_, bf16[144,128]{1,0:T(8,128)(2,1)S(1)} %collective-permute-done.2.refs_1_, bf16[144,128]{1,0:T(8,128)(2,1)S(1)} %collective-permute-done.6.refs_2_, ...), custom_call_target="tpu_custom_call" | custom-call | flops 59768832 | bytes 749568 | tf_op jit(solution)/shard_map/pallas_call | solution.py:41
  12.1 0.0 collective-permute-done.1.refs_3_
  12.1 1.1 %shard_map.121 = (bf16[512,384]{1,0:T(8,128)(2,1)S(1)}, bf16[128,384]{1,0:T(8,128)(2,1)S(1)}) custom-call(bf16[144,128]{1,0:T(8,128)(2,1)S(1)} %collective-permute-done.5.refs_0_, bf16[144,128]{1,0:T(8,128)(2,1)S(1)} %collective-permute-done.3.refs_1_, bf16[144,128]{1,0:T(8,128)(2,1)S(1)} %collective-permute-done.7.refs_2_, ...), custom_call_target="tpu_custom_call" | custom-call | flops 59768832 | bytes 847872 | tf_op jit(solution)/shard_map/pallas_call | solution.py:41
  13.2 1.6 %collective-permute-start.8 = (bf16[128,384]{1,0:T(8,128)(2,1)S(1)}, bf16[128,384]{1,0:T(8,128)(2,1)S(1)}, u32[]{:S(2)}, u32[]{:S(2)}) collective-permute-start(bf16[128,384]{1,0:T(8,128)(2,1)S(1)} %get-tuple-element.12), channel_id=1, source_target_pairs={{0,8},{1,9},{2,10},{3,11},{4,12},{5,13},{6,14},{7,15},{8,0},{9,1},... | collective-permute-start | bytes 294920 | tf_op jit(solution)/shard_map/ppermute | solution.py:183
  14.9 0.1 copy.15
  15.0 3.5 %collective-permute-done.8 = bf16[128,384]{1,0:T(8,128)(2,1)S(1)} collective-permute-done((bf16[128,384]{1,0:T(8,128)(2,1)S(1)}, bf16[128,384]{1,0:T(8,128)(2,1)S(1)}, u32[]{:S(2)}, u32[]{:S(2)}) %collective-permute-start.8) | collective-permute-done | bytes 98336 | tf_op jit(solution)/shard_map/ppermute | solution.py:183
  18.5 3.7 %collective-permute-start.9 = (bf16[128,384]{1,0:T(8,128)(2,1)S(1)}, bf16[128,384]{1,0:T(8,128)(2,1)S(1)}, u32[]{:S(2)}, u32[]{:S(2)}) collective-permute-start(bf16[128,384]{1,0:T(8,128)(2,1)S(1)} %add_convert_fusion.a_ref), channel_id=1, source_target_pairs={{0,24},{1,25},{2,26},{3,27},{4,28},{5,29},{6,30},{7,31},{8,16},{9,... | collective-permute-start | bytes 294920 | tf_op jit(solution)/shard_map/ppermute | solution.py:183
  22.2 0.1 pad_maximum_fusion.filter_ref
  22.3 2.8 %collective-permute-done.9.b_ref = bf16[128,384]{1,0:T(8,128)(2,1)S(1)} collective-permute-done((bf16[128,384]{1,0:T(8,128)(2,1)S(1)}, bf16[128,384]{1,0:T(8,128)(2,1)S(1)}, u32[]{:S(2)}, u32[]{:S(2)}) %collective-permute-start.9) | collective-permute-done | bytes 98336 | tf_op jit(solution)/shard_map/ppermute | solution.py:183
  25.0 0.7 %shard_map.122 = (f32[512,128]{1,0:T(8,128)S(1)}, bf16[512,128]{1,0:T(8,128)(2,1)S(1)}) custom-call(bf16[128,384]{1,0:T(8,128)(2,1)S(1)} %add_convert_fusion.a_ref, bf16[128,384]{1,0:T(8,128)(2,1)S(1)} %collective-permute-done.9.b_ref, bf16[2,128,128]{2,1,0:T(8,128)(2,1)S(1)} %copy-done.5, f32[128,384]{1,0:T(8,128)S(1)} %pad_maximum_fusion.filter_ref, ...), custom_call_target="tpu_custom_call" | custom-call | flops 125829120 | bytes 1638400 | tf_op jit(solution)/shard_map/pallas_call | solution.py:41
  25.7 0.1 collective-permute-start.10
  25.8 5.8 %collective-permute-start.4 = (bf16[32,128]{1,0:T(8,128)(2,1)S(1)}, bf16[32,128]{1,0:T(8,128)(2,1)S(1)}, u32[]{:S(2)}, u32[]{:S(2)}) collective-permute-start(bf16[32,128]{1,0:T(8,128)(2,1)S(1)} %slice_select_fusion.2), channel_id=1, source_target_pairs={{7,8},{8,7},{15,16},{16,15},{23,24},{24,23},{31,0},{0,31}} | collective-permute-start | bytes 24584 | tf_op jit(solution)/shard_map/ppermute | solution.py:247
  31.7 0.6 %copy-done.11 = f32[128]{0:T(128)S(1)} copy-done((f32[128]{0:T(128)S(1)}, f32[128]{0:T(128)}, u32[]{:S(2)}) %copy-start.11) | copy-done | bytes 536
  32.3 0.1 copy.13.width_ref
  32.5 0.1 collective-permute-start.13
  32.6 0.1 collective-permute-start.12
  32.7 3.4 %collective-permute-start.11 = (bf16[128,128]{1,0:T(8,128)(2,1)S(1)}, bf16[128,128]{1,0:T(8,128)(2,1)S(1)}, u32[]{:S(2)}, u32[]{:S(2)}) collective-permute-start(bf16[128,128]{1,0:T(8,128)(2,1)S(1)} %get-tuple-element.21), channel_id=1, source_target_pairs={{0,1},{1,0},{2,3},{3,2},{4,5},{5,4},{6,7},{7,6},{8,9},{9,8},{10,11... | collective-permute-start | bytes 98312 | tf_op jit(solution)/shard_map/ppermute | solution.py:183
  36.1 0.7 %shard_map.119.refs_0_ = f32[128,128]{1,0:T(8,128)S(1)} custom-call(bf16[128,128]{1,0:T(8,128)(2,1)S(1)} %copy-done.4, bf16[32,128]{1,0:T(8,128)(2,1)S(1)} %get-tuple-element.23.before_ref, bf16[32,128]{1,0:T(8,128)(2,1)S(1)} %get-tuple-element.22.after_ref, bf16[128,128]{1,0:T(8,128)(2,1)S(1)} %copy-done.8, f32[128,1]{1,0:T(8,128)S(1)} %copy.13.width_ref, ...), custom_call_target="tpu_custom_call" | custom-call | flops 100663296 | bytes 164352 | tf_op jit(solution)/shard_map/pallas_call | solution.py:41
  36.9 0.5 %collective-permute-done.13.refs_4_ = bf16[128,128]{1,0:T(8,128)(2,1)S(1)} collective-permute-done((bf16[128,128]{1,0:T(8,128)(2,1)S(1)}, bf16[128,128]{1,0:T(8,128)(2,1)S(1)}, u32[]{:S(2)}, u32[]{:S(2)}) %collective-permute-start.13) | collective-permute-done | bytes 32800 | tf_op jit(solution)/shard_map/ppermute | solution.py:183
  37.4 0.6 %collective-permute-done.11.refs_2_ = bf16[128,128]{1,0:T(8,128)(2,1)S(1)} collective-permute-done((bf16[128,128]{1,0:T(8,128)(2,1)S(1)}, bf16[128,128]{1,0:T(8,128)(2,1)S(1)}, u32[]{:S(2)}, u32[]{:S(2)}) %collective-permute-start.11) | collective-permute-done | bytes 32800 | tf_op jit(solution)/shard_map/ppermute | solution.py:183
  38.0 1.0 %shard_map.123 = bf16[128,128]{1,0:T(8,128)(2,1)} custom-call(f32[128,128]{1,0:T(8,128)S(1)} %shard_map.119.refs_0_, f32[128,128]{1,0:T(8,128)S(1)} %slice.57.refs_1_, bf16[128,128]{1,0:T(8,128)(2,1)S(1)} %collective-permute-done.11.refs_2_, bf16[128,128]{1,0:T(8,128)(2,1)S(1)} %collective-permute-done.12.refs_3_, ...), custom_call_target="tpu_custom_call" | custom-call | flops 33554432 | bytes 524800 | tf_op jit(solution)/shard_map/pallas_call | solution.py:41
  (41 shorter events, 0.2 us)
Async XLA Ops:
  0.0 14.9 %copy-start = (f32[768,128]{1,0:T(8,128)S(1)}, f32[768,128]{1,0:T(8,128)}, u32[]{:S(2)}) copy-start(f32[768,128]{1,0:T(8,128)} %param.15) | copy-start | bytes 1179652
  0.0 0.8 %copy-start.3 = (bf16[128,128]{1,0:T(8,128)(2,1)S(1)}, bf16[128,128]{1,0:T(8,128)(2,1)}, u32[]{:S(2)}) copy-start(bf16[128,128]{1,0:T(8,128)(2,1)} %feat_ref.3) | copy-start | bytes 98308
  0.8 0.7 %copy-start.6 = (f32[256,3]{0,1:T(4,128)S(1)}, f32[256,3]{0,1:T(4,128)}, u32[]{:S(2)}) copy-start(f32[256,3]{0,1:T(4,128)} %param.13) | copy-start | bytes 9220
  1.5 5.5 %collective-permute-start.6 = (bf16[144,128]{1,0:T(8,128)(2,1)S(1)}, bf16[144,128]{1,0:T(8,128)(2,1)S(1)}, u32[]{:S(2)}, u32[]{:S(2)}) collective-permute-start(bf16[144,128]{1,0:T(8,128)(2,1)S(1)} %shard_map.118.refs_0_), channel_id=1, source_target_pairs={{0,4},{1,5},{2,6},{3,7},{4,0},{5,1},{6,2},{7,3},{8,12},{9,13},{10,... | collective-permute-start | bytes 110600 | tf_op jit(solution)/shard_map/ppermute | solution.py:183
  4.5 7.5 %collective-permute-start.5 = (bf16[144,128]{1,0:T(8,128)(2,1)S(1)}, bf16[144,128]{1,0:T(8,128)(2,1)S(1)}, u32[]{:S(2)}, u32[]{:S(2)}) collective-permute-start(bf16[144,128]{1,0:T(8,128)(2,1)S(1)} %shard_map.118.refs_0_), channel_id=1, source_target_pairs={{0,2},{1,3},{2,0},{3,1},{4,6},{5,7},{6,4},{7,5},{8,10},{9,11},{10,... | collective-permute-start | bytes 110600 | tf_op jit(solution)/shard_map/ppermute | solution.py:183
  4.5 4.0 %collective-permute-start.2 = (bf16[144,128]{1,0:T(8,128)(2,1)S(1)}, bf16[144,128]{1,0:T(8,128)(2,1)S(1)}, u32[]{:S(2)}, u32[]{:S(2)}) collective-permute-start(bf16[144,128]{1,0:T(8,128)(2,1)S(1)} %shard_map.118.refs_0_), channel_id=1, source_target_pairs={{0,1},{1,0},{2,3},{3,2},{4,5},{5,4},{6,7},{7,6},{8,9},{9,8},{10,11... | collective-permute-start | bytes 110600 | tf_op jit(solution)/shard_map/ppermute | solution.py:183
  6.0 4.9 %collective-permute-start = (bf16[144,128]{1,0:T(8,128)(2,1)S(1)}, bf16[144,128]{1,0:T(8,128)(2,1)S(1)}, u32[]{:S(2)}, u32[]{:S(2)}) collective-permute-start(bf16[144,128]{1,0:T(8,128)(2,1)S(1)} %shard_map.118.refs_0_), channel_id=1, source_target_pairs={{0,5},{1,4},{2,7},{3,6},{4,1},{5,0},{6,3},{7,2},{8,13},{9,12},{10,... | collective-permute-start | bytes 110600 | tf_op jit(solution)/shard_map/ppermute | solution.py:183
  7.0 5.1 %collective-permute-start.7 = (bf16[144,128]{1,0:T(8,128)(2,1)S(1)}, bf16[144,128]{1,0:T(8,128)(2,1)S(1)}, u32[]{:S(2)}, u32[]{:S(2)}) collective-permute-start(bf16[144,128]{1,0:T(8,128)(2,1)S(1)} %collective-permute-done.6.refs_2_), channel_id=1, source_target_pairs={{0,2},{1,3},{2,0},{3,1},{4,6},{5,7},{6,4},{7,5},{8,10},{9,11},{10,... | collective-permute-start | bytes 110600 | tf_op jit(solution)/shard_map/ppermute | solution.py:183
  8.5 3.6 %collective-permute-start.3 = (bf16[144,128]{1,0:T(8,128)(2,1)S(1)}, bf16[144,128]{1,0:T(8,128)(2,1)S(1)}, u32[]{:S(2)}, u32[]{:S(2)}) collective-permute-start(bf16[144,128]{1,0:T(8,128)(2,1)S(1)} %collective-permute-done.2.refs_1_), channel_id=1, source_target_pairs={{0,2},{1,3},{2,0},{3,1},{4,6},{5,7},{6,4},{7,5},{8,10},{9,11},{10,... | collective-permute-start | bytes 110600 | tf_op jit(solution)/shard_map/ppermute | solution.py:183
  10.9 1.2 %collective-permute-start.1 = (bf16[144,128]{1,0:T(8,128)(2,1)S(1)}, bf16[144,128]{1,0:T(8,128)(2,1)S(1)}, u32[]{:S(2)}, u32[]{:S(2)}) collective-permute-start(bf16[144,128]{1,0:T(8,128)(2,1)S(1)} %collective-permute-done.refs_3_), channel_id=1, source_target_pairs={{0,2},{1,3},{2,0},{3,1},{4,6},{5,7},{6,4},{7,5},{8,10},{9,11},{10,... | collective-permute-start | bytes 110600 | tf_op jit(solution)/shard_map/ppermute | solution.py:183
  13.2 5.2 %collective-permute-start.8 = (bf16[128,384]{1,0:T(8,128)(2,1)S(1)}, bf16[128,384]{1,0:T(8,128)(2,1)S(1)}, u32[]{:S(2)}, u32[]{:S(2)}) collective-permute-start(bf16[128,384]{1,0:T(8,128)(2,1)S(1)} %get-tuple-element.12), channel_id=1, source_target_pairs={{0,8},{1,9},{2,10},{3,11},{4,12},{5,13},{6,14},{7,15},{8,0},{9,1},... | collective-permute-start | bytes 294920 | tf_op jit(solution)/shard_map/ppermute | solution.py:183
  18.5 6.5 %collective-permute-start.9 = (bf16[128,384]{1,0:T(8,128)(2,1)S(1)}, bf16[128,384]{1,0:T(8,128)(2,1)S(1)}, u32[]{:S(2)}, u32[]{:S(2)}) collective-permute-start(bf16[128,384]{1,0:T(8,128)(2,1)S(1)} %add_convert_fusion.a_ref), channel_id=1, source_target_pairs={{0,24},{1,25},{2,26},{3,27},{4,28},{5,29},{6,30},{7,31},{8,16},{9,... | collective-permute-start | bytes 294920 | tf_op jit(solution)/shard_map/ppermute | solution.py:183
  22.2 2.9 %copy-start.5 = (bf16[2,128,128]{2,1,0:T(8,128)(2,1)S(1)}, bf16[2,128,128]{2,1,0:T(8,128)(2,1)}, u32[]{:S(2)}) copy-start(bf16[2,128,128]{2,1,0:T(8,128)(2,1)} %mix_ref.1) | copy-start | bytes 196612
  25.0 0.8 %copy-start.4 = (bf16[128,128]{1,0:T(8,128)(2,1)S(1)}, bf16[128,128]{1,0:T(8,128)(2,1)}, u32[]{:S(2)}) copy-start(bf16[128,128]{1,0:T(8,128)(2,1)} %feat_ref.3) | copy-start | bytes 98308
  25.7 6.7 %collective-permute-start.10 = (bf16[512,128]{1,0:T(8,128)(2,1)S(1)}, bf16[512,128]{1,0:T(8,128)(2,1)S(1)}, u32[]{:S(2)}, u32[]{:S(2)}) collective-permute-start(bf16[512,128]{1,0:T(8,128)(2,1)S(1)} %get-tuple-element.16), channel_id=1, source_target_pairs={{0,2},{1,3},{2,0},{3,1},{4,6},{5,7},{6,4},{7,5},{8,10},{9,11},{10,... | collective-permute-start | bytes 393224 | tf_op jit(solution)/shard_map/ppermute | solution.py:183
  25.8 10.3 %collective-permute-start.4 = (bf16[32,128]{1,0:T(8,128)(2,1)S(1)}, bf16[32,128]{1,0:T(8,128)(2,1)S(1)}, u32[]{:S(2)}, u32[]{:S(2)}) collective-permute-start(bf16[32,128]{1,0:T(8,128)(2,1)S(1)} %slice_select_fusion.2), channel_id=1, source_target_pairs={{7,8},{8,7},{15,16},{16,15},{23,24},{24,23},{31,0},{0,31}} | collective-permute-start | bytes 24584 | tf_op jit(solution)/shard_map/ppermute | solution.py:247
  31.7 0.7 %copy-start.11 = (f32[128]{0:T(128)S(1)}, f32[128]{0:T(128)}, u32[]{:S(2)}) copy-start(f32[128]{0:T(128)} %param.18) | copy-start | bytes 1540
  32.5 4.9 %collective-permute-start.13 = (bf16[128,128]{1,0:T(8,128)(2,1)S(1)}, bf16[128,128]{1,0:T(8,128)(2,1)S(1)}, u32[]{:S(2)}, u32[]{:S(2)}) collective-permute-start(bf16[128,128]{1,0:T(8,128)(2,1)S(1)} %get-tuple-element.19), channel_id=1, source_target_pairs={{0,5},{1,4},{2,7},{3,6},{4,1},{5,0},{6,3},{7,2},{8,13},{9,12},{10,... | collective-permute-start | bytes 98312 | tf_op jit(solution)/shard_map/ppermute | solution.py:183
  32.6 4.8 %collective-permute-start.12 = (bf16[128,128]{1,0:T(8,128)(2,1)S(1)}, bf16[128,128]{1,0:T(8,128)(2,1)S(1)}, u32[]{:S(2)}, u32[]{:S(2)}) collective-permute-start(bf16[128,128]{1,0:T(8,128)(2,1)S(1)} %get-tuple-element.20), channel_id=1, source_target_pairs={{0,4},{1,5},{2,6},{3,7},{4,0},{5,1},{6,2},{7,3},{8,12},{9,13},{10,... | collective-permute-start | bytes 98312 | tf_op jit(solution)/shard_map/ppermute | solution.py:183
  32.7 3.4 %copy-start.8 = (bf16[128,128]{1,0:T(8,128)(2,1)S(1)}, bf16[128,128]{1,0:T(8,128)(2,1)}, u32[]{:S(2)}) copy-start(bf16[128,128]{1,0:T(8,128)(2,1)} %msg_ref.1) | copy-start | bytes 98308
  32.7 3.4 %copy-start.9 = (f32[128,16]{0,1:T(8,128)S(1)}, f32[128,16]{0,1:T(8,128)}, u32[]{:S(2)}) copy-start(f32[128,16]{0,1:T(8,128)} %param.19) | copy-start | bytes 24580
  32.7 3.4 %copy-start.10 = (s32[128,16]{0,1:T(8,128)S(1)}, s32[128,16]{0,1:T(8,128)}, u32[]{:S(2)}) copy-start(s32[128,16]{0,1:T(8,128)} %param.20) | copy-start | bytes 24580
  32.7 5.3 %collective-permute-start.11 = (bf16[128,128]{1,0:T(8,128)(2,1)S(1)}, bf16[128,128]{1,0:T(8,128)(2,1)S(1)}, u32[]{:S(2)}, u32[]{:S(2)}) collective-permute-start(bf16[128,128]{1,0:T(8,128)(2,1)S(1)} %get-tuple-element.21), channel_id=1, source_target_pairs={{0,1},{1,0},{2,3},{3,2},{4,5},{5,4},{6,7},{7,6},{8,9},{9,8},{10,11... | collective-permute-start | bytes 98312 | tf_op jit(solution)/shard_map/ppermute | solution.py:183
  36.1 1.8 %copy-start.2 = (bf16[512,128]{1,0:T(8,128)(2,1)S(1)}, bf16[512,128]{1,0:T(8,128)(2,1)}, u32[]{:S(2)}) copy-start(bf16[512,128]{1,0:T(8,128)(2,1)} %refs_7_.1) | copy-start | bytes 393220
  36.8 1.1 %copy-start.1 = (bf16[128,512]{1,0:T(8,128)(2,1)S(1)}, bf16[128,512]{1,0:T(8,128)(2,1)}, u32[]{:S(2)}) copy-start(bf16[128,512]{1,0:T(8,128)(2,1)} %refs_6_.1) | copy-start | bytes 393220
  36.8 1.1 %copy-start.7 = (f32[128]{0:T(128)S(1)}, f32[128]{0:T(128)}, u32[]{:S(2)}) copy-start(f32[128]{0:T(128)} %param.21) | copy-start | bytes 1540

commit v2 on v1

v2 whole, which is shorter than its diff:
```python
import functools
import math

import jax
import jax.numpy as jnp
import numpy as np
from jax import lax
from jax.experimental import pallas as pl
from jax.experimental.pallas import tpu as pltpu
from jax.sharding import PartitionSpec as P

box_side = 16.0
slab_step = 0.125
coord_rows = 16
bf16, f32 = jnp.bfloat16, jnp.float32

both = ("space", "kgrp")

vector_flops = 15000

def fit_cosine(degree):
    count = 64
    theta = (np.arange(count) + 0.5) * math.pi / count
    u = 0.125 * (1.0 + np.cos(theta))
    values = np.cos(2.0 * math.pi * np.sqrt(u))
    cheb = np.polynomial.chebyshev.Chebyshev.fit(u, values, degree, domain=[0.0, 0.25])
    return [float(c) for c in cheb.convert(kind=np.polynomial.Polynomial).coef]


cosine = fit_cosine(6)


def dot(a, b, dims):
    return lax.dot_general(a, b, (dims, ((), ())), preferred_element_type=f32)


def whole(count):
    return [pl.BlockSpec(memory_space=pltpu.VMEM)] * count


def call(body, outs, *args, flops=0, transcendentals=0):
    moved = sum(a.size * a.dtype.itemsize for a in (*args, *outs))
    return pl.pallas_call(
        body,
        out_shape=outs if len(outs) > 1 else outs[0],
        in_specs=whole(len(args)),
        out_specs=whole(len(outs)) if len(outs) > 1 else whole(1)[0],
        cost_estimate=pl.CostEstimate(
            flops=flops, bytes_accessed=moved, transcendentals=transcendentals
        ),
        compiler_params=pltpu.CompilerParams(vmem_limit_bytes=24 * 1024 * 1024),
    )(*args)


def shape(dims, dtype):
    return jax.ShapeDtypeStruct(dims, dtype)


def coordinate_parts(coords, slab_length):
    atoms = coords.shape[1]
    row = lax.broadcasted_iota(jnp.int32, coords.shape, 0)
    turns = coords * jnp.where(row == 2, 1.0 / slab_length, 1.0 / box_side)
    high = turns.astype(bf16).astype(f32)
    rest = turns - high
    middle = rest.astype(bf16).astype(f32)
    low = rest - middle
    ones = jnp.ones((1, atoms), f32)
    zeros = jnp.zeros((coord_rows - 10, atoms), f32)
    return jnp.concatenate([high, middle, low, ones, zeros], axis=0).astype(bf16)


def cosines(turns):
    part = turns - jnp.round(turns)
    u = part * part
    value = jnp.full_like(u, cosine[-1])
    for c in cosine[-2::-1]:
        value = value * u + c
    return value.astype(bf16)


def fill_phases(coord_refs, waves, groups, slab_length, phase_ref):
    group = lax.axis_index("kgrp")
    atoms = coord_refs[0].shape[1] // groups
    for i in range(len(coord_refs) * groups):
        start = pl.multiple_of((group ^ (i % groups)) * atoms, atoms)
        parts = coordinate_parts(coord_refs[i // groups][:, pl.ds(start, atoms)], slab_length)
        phase_ref[i * atoms : (i + 1) * atoms, :] = cosines(dot(parts, waves, ((0,), (0,))))


def quarter_body(out_ref):
    share = out_ref.shape[1] // 2
    row = lax.broadcasted_iota(jnp.int32, out_ref.shape, 0)
    column = lax.broadcasted_iota(jnp.int32, out_ref.shape, 1)
    out_ref[...] = jnp.where((row == 9) & (column >= share), -0.25, 0.0)


def prepare_body(inner, groups, slab_length, quarter_ref, index_ref, pos_ref, wave_ref, phase_ref):
    share = index_ref.shape[1] // inner
    first = lax.axis_index("space") & (inner - 1)
    counts = index_ref[...].astype(f32)
    mine = counts[:, :share]
    for i in range(1, inner):
        mine = jnp.where(first == i, counts[:, i * share : (i + 1) * share], mine)
    counts = jnp.concatenate([mine, mine], axis=1)
    zeros = jnp.zeros((coord_rows - 9, 2 * share), f32)
    waves = jnp.concatenate([counts, counts, counts, zeros], axis=0) + quarter_ref[...]
    wave_ref[...] = waves.astype(bf16)
    fill_phases([pos_ref], wave_ref[...], groups, slab_length, phase_ref)


def phase_body(groups, slab_length, *refs):
    *coord_refs, wave_ref, phase_ref = refs
    fill_phases(coord_refs, wave_ref[...], groups, slab_length, phase_ref)


def phases(coords, waves, groups, slab_length):
    rows = len(coords) * coords[0].shape[1]
    return call(
        functools.partial(phase_body, groups, slab_length),
        (shape((rows, waves.shape[1]), bf16),),
        *coords,
        waves,
        flops=vector_flops * rows * waves.shape[1],
    )


def layer_member(members):
    member = lax.axis_index("space") * lax.axis_size("kgrp") + lax.axis_index("kgrp")
    return member & (members - 1)


def structure_body(count, places, phases, members, atoms, final, *refs):
    block_refs, refs = refs[:count], refs[count:]
    phase_refs, (*carry_refs, sum_ref) = refs[:phases], refs[phases:]
    channels = block_refs[0].shape[1]
    total = carry_refs[0][...] if carry_refs else None
    blocks = [
        ref[i : i + atoms, :] for ref in block_refs for i in range(0, ref.shape[0], atoms)
    ]
    for block, (which, at) in zip(blocks, places):
        phase = phase_refs[which][at * atoms : (at + 1) * atoms, :]
        term = dot(block, phase, ((0,), (0,)))
        total = term if total is None else total + term
    sum_ref[:channels, :] = total.astype(sum_ref.dtype)
    if final:
        last = blocks[-1]
        halo = atoms // 4
        first = layer_member(members) == 0
        edge = jnp.where(first, last[atoms - halo :, :], last[:halo, :])
        sum_ref[channels:, :] = jnp.zeros_like(sum_ref[channels:, :])
        for r, c, piece in edge_places(halo, channels, sum_ref.shape[1]):
            sum_ref[channels + r : channels + r + 16, c : c + channels] = edge[piece : piece + 16]


def edge_places(halo, channels, columns):
    per_row = columns // channels
    return [
        (i // per_row * 16, i % per_row * channels, i * 16) for i in range(halo // 16)
    ]


def structure(blocks, places, phases, carry, members, atoms, final):
    channels = blocks[0].shape[1]
    columns = phases[0].shape[1]
    if final:
        edges = edge_places(atoms // 4, channels, columns)
        out = shape((channels + edges[-1][0] + 16, columns), bf16)
    else:
        out = shape((channels, columns), f32)
    extra = () if carry is None else (carry,)
    return call(
        functools.partial(structure_body, len(blocks), places, len(phases), members, atoms, final),
        (out,),
        *blocks,
        *phases,
        *extra,
        flops=2 * len(places) * atoms * columns * channels,
    )


def ewald_body(scale, inv_scale, places, phases, a_ref, b_ref, mix_ref, filter_ref, *refs):
    phase_refs, out_refs = refs[:phases], refs[phases:]
    channels = mix_ref.shape[1]
    total = (a_ref[:channels, :].astype(f32) + b_ref[:channels, :].astype(f32)) * scale
    amps = total.astype(bf16)
    columns = amps.shape[1]
    straight = dot(mix_ref[0], amps, ((0,), (0,)))
    crossed = dot(mix_ref[1], amps, ((0,), (0,)))
    half = columns // 2
    crossed = jnp.concatenate([-crossed[:, half:], crossed[:, :half]], axis=1)
    y = (filter_ref[...] * (straight + crossed)).astype(bf16)
    for ref, blocks in zip(out_refs, places):
        rows = ref.shape[0] // len(blocks)
        for i, (which, at) in enumerate(blocks):
            phase = phase_refs[which][at * rows : (at + 1) * rows, :]
            term = dot(phase, y, ((1,), (1,))) * inv_scale
            ref[i * rows : (i + 1) * rows, :] = term.astype(ref.dtype)


def halo_rows(members, blocks, stage_refs):
    atoms, channels = blocks[0].shape
    halo = atoms // 4
    member = layer_member(members)
    layer = lax.axis_index("space") // (members // lax.axis_size("kgrp"))
    before, after = blocks[-1][atoms - halo :, :], blocks[-1][:halo, :]
    places = edge_places(halo, channels, stage_refs[0].shape[1]) if stage_refs else []
    for i, ref in enumerate(stage_refs):
        edge = jnp.concatenate(
            [ref[channels + r : channels + r + 16, c : c + channels] for r, c, _ in places], axis=0
        )
        if i == 0:
            before = after = edge
        else:
            before = jnp.where((layer & ((1 << i) - 1)) == 0, edge, before)
            after = jnp.where(((layer + 1) & ((1 << i) - 1)) == 0, edge, after)
    for i, block in enumerate(blocks):
        span = 1 << i
        before = jnp.where((member & (2 * span - 1)) == span, block[atoms - halo :, :], before)
        after = jnp.where(((member + 1) & (2 * span - 1)) == span, block[:halo, :], after)
    return before, after


def message_body(members, places, refs_of_blocks, *refs):
    block_refs, refs = refs[:refs_of_blocks], refs[refs_of_blocks:]
    *stage_refs, msg_ref, width_ref, dist_ref, nbr_ref, base_ref = refs
    feat_ref = block_refs[0]
    channels, atoms = feat_ref.shape[1], dist_ref.shape[1]
    blocks = [block_refs[which][row : row + atoms, :] for which, row in places]
    before, after = halo_rows(members, blocks, stage_refs)
    extended = jnp.concatenate([before, feat_ref[:atoms, :], after], axis=0)
    projected = dot(msg_ref[...], extended, ((0,), (1,))).astype(bf16)
    rows = extended.shape[0]
    row = lax.broadcasted_iota(jnp.int32, (rows, atoms), 0)
    inverse = -1.0 / jnp.broadcast_to(width_ref[...], (atoms, channels)).T
    message = jnp.zeros((projected.shape[0], atoms), f32)
    for j in range(nbr_ref.shape[0]):
        chosen = jnp.where(row == nbr_ref[j : j + 1, :], 1.0, 0.0).astype(bf16)
        nearby = dot(projected, chosen, ((1,), (0,)))
        message = message + jnp.exp(dist_ref[j : j + 1, :] * inverse) * nearby
    base_ref[...] = feat_ref[:atoms, :].astype(f32) + message.T


def final_body(peers, *refs):
    base_ref, *refs = refs
    peer_refs, (gain_ref, in_ref, out_ref, result_ref) = refs[:peers], refs[peers:]
    mixed = base_ref[...]
    for ref in peer_refs:
        mixed = mixed + ref[...].astype(f32)
    inverse = lax.rsqrt(jnp.mean(mixed * mixed, axis=1, keepdims=True) + 1e-06)
    normed = (mixed * inverse * gain_ref[...]).astype(bf16)
    hidden = dot(normed, in_ref[...], ((1,), (0,)))
    hidden = (hidden * (1.0 / (1.0 + jnp.exp(-hidden)))).astype(bf16)
    result_ref[...] = (mixed + dot(hidden, out_ref[...], ((1,), (0,)))).astype(bf16)


def local(
    outer,
    features,
    positions,
    wave_index,
    wave_filter,
    mix_pair,
    msg_weight,
    chan_width,
    pair_dist,
    neighbours,
    norm_gain,
    in_weight,
    out_weight,
):
    atoms, channels = features.shape
    groups, space = lax.axis_size("kgrp"), lax.axis_size("space")
    inner = space // outer
    members = inner * groups
    devices = space * groups
    total_atoms = atoms * devices
    slab_length = total_atoms * slab_step

    def swap(x, mask):
        return lax.ppermute(x, both, [(i, i ^ mask) for i in range(devices)])

    near = [m for m in range(members) if not m & groups]
    single = [m for m in near if m & (m - 1) == 0]
    direct = [m for m in near if m not in single]
    bases = [m for m in near if m % groups == 0]
    block = {0: features}
    coords = {0: positions.T}
    for m in near[1:]:
        block[m] = swap(features, m)
    for m in bases[1:]:
        coords[m] = swap(positions.T, m)
    share = wave_index.shape[0] // inner
    quarter = call(quarter_body, (shape((coord_rows, 2 * share), f32),))
    waves, own_phase = call(
        functools.partial(prepare_body, inner, groups, slab_length),
        (shape((coord_rows, 2 * share), bf16), shape((groups * atoms, 2 * share), bf16)),
        quarter,
        wave_index.T,
        coords[0],
        flops=vector_flops * 2 * groups * atoms * share,
    )
    first = (lax.axis_index("space") % inner) * share
    filters = lax.dynamic_slice_in_dim(wave_filter, first, share, 0).T
    filters = jnp.concatenate([filters, filters], axis=1)
    far_blocks = swap(jnp.concatenate([block[m] for m in near], axis=0), groups)
    far_at = {m ^ groups: i * atoms for i, m in enumerate(near)}
    crossed = swap(jnp.concatenate([coords[m] for m in bases], axis=1), groups)
    own = groups * atoms
    for i, m in enumerate(bases):
        coords[m ^ groups] = crossed[:, i * own : (i + 1) * own]
    early = phases([coords[m] for m in bases[1:]], waves, groups, slab_length)
    late = phases([coords[m ^ groups] for m in bases], waves, groups, slab_length)
    phase = [own_phase, early, late]
    place = {}
    for i in range(groups):
        place[i] = (0, i)
        for j, m in enumerate(bases[1:]):
            place[m + i] = (1, j * groups + i)
        for j, m in enumerate(bases):
            place[(m ^ groups) + i] = (2, j * groups + i)
    part = structure(
        [block[m] for m in near], [place[m] for m in near], phase[:2], None, members, atoms, False
    )
    far_places = [(0, place[m][1]) for m in far_at]
    amps = structure([far_blocks], far_places, [late], part, members, atoms, True)

    stages = []
    sums = lax.broadcasted_iota(jnp.int32, amps.shape, 0) < channels
    while (1 << len(stages)) < outer:
        if stages:
            both_sums = amps.astype(f32) + stages[-1].astype(f32)
            amps = jnp.where(sums, both_sums, amps.astype(f32)).astype(bf16)
        stages.append(swap(amps, ((2 << len(stages)) - 1) * members))
    other = stages[-1] if stages else jnp.zeros_like(amps)

    columns = filters.shape[1]
    outs = [[place[m] for m in single], [place[m ^ groups] for m in single]]
    outs += [[place[m ^ core]] for m in direct for core in (0, groups)]
    keep, send, *straight = call(
        functools.partial(
            ewald_body,
            1.0 / math.sqrt(total_atoms),
            1.0 / math.sqrt(wave_index.shape[0] * groups),
            outs,
            len(phase),
        ),
        tuple(
            shape((len(blocks) * atoms, channels), bf16 if i else f32)
            for i, blocks in enumerate(outs)
        ),
        amps,
        other,
        mix_pair,
        filters,
        *phase,
        flops=2 * channels * columns * (2 * channels + members * atoms),
    )
    came = swap(send, groups)
    far_masks = [m ^ core for m in direct for core in (0, groups)]
    peers = [swap(x, m) for x, m in zip(straight, far_masks)]
    terms = keep + came.astype(f32)
    peers.append(terms[:atoms])
    for i, m in enumerate(single[1:], 1):
        peers.append(swap(terms[i * atoms : (i + 1) * atoms].astype(bf16), m))

    slots = neighbours.shape[1]
    steps = [(2 << i) - 1 for i in range(members.bit_length() - 1)]
    step_places = [(len(near), far_at[m]) if m in far_at else (near.index(m), 0) for m in steps]
    base = call(
        functools.partial(message_body, members, step_places, 1 + len(near)),
        (shape((atoms, channels), f32),),
        *[block[m] for m in near],
        far_blocks,
        *stages,
        msg_weight,
        chan_width.reshape(1, channels),
        pair_dist.T,
        neighbours.T,
        flops=3 * channels * atoms * slots * atoms,
        transcendentals=atoms * slots * channels,
    )
    return call(
        functools.partial(final_body, len(peers)),
        (shape((atoms, channels), bf16),),
        base,
        *peers,
        norm_gain.reshape(1, channels),
        in_weight,
        out_weight,
        flops=4 * atoms * channels * in_weight.shape[1],
    )


def layers(mesh):
    depths = {getattr(d, "coords", (0, 0, i))[2] for i, d in enumerate(mesh.devices[:, 0])}
    return len(depths)


def solution(mesh):
    placed = (
        P(both, None),
        P("space", None),
        P("kgrp", None),
        P("kgrp", None),
        P(),
        P(),
        P(),
        P(both, None),
        P(both, None),
        P(),
        P(),
        P(),
    )
    return jax.shard_map(
        functools.partial(local, layers(mesh)),
        mesh=mesh,
        in_specs=placed,
        out_specs=P(both, None),
        check_vma=False,
    )
```

time: 39.3 us -> 34.1 us (0.87)
  waiting for transfers between devices: 11.1 us -> 8.53 us
  local copies, waits for them, and re-layouts: 2.58 us -> 1.52 us
  other arithmetic: 1.03 us -> 0.24 us
  starting transfers between devices: 19.4 us -> 18.7 us
    ppermute x1 -> x0, starting transfers between devices: 5.76 us -> none  [local(): before = after = lax.ppermute(edge, both, pairs)]
    ppermute x13, starting transfers between devices: 13.7 us -> 18.7 us  [swap(): return lax.ppermute(x, both, [(i, i ^ mask) for i in range(devices)])]
    ppermute x13, waiting for transfers between devices: 11.1 us -> 8.53 us  [swap(): return lax.ppermute(x, both, [(i, i ^ mask) for i in range(devices)])]
    unnamed x25, local copies, waits for them, and re-layouts: 2.3 us -> 1.49 us
    convert_element_type x2 -> x1, other arithmetic: 0.79 us -> 0.1 us  [local(): amps = jnp.where(sums, both_sums, amps.astype(f32)).astype(bf16)]
    pallas_call x6 -> x9, Pallas kernels: 4.5 us -> 4.65 us  [call(): pl.pallas_call(body, out_shape=outs if len(outs) > 1 else outs[0], in_spe...]
  transfers between devices with their start and end apart: 14 -> 13, of which waited for: 6 -> 6; matrix products, arithmetic and copies ran while one was open for 4% -> 1% of each run, Pallas kernels for 4% -> 8%
where the time goes in v2:
time: 34.1 us; the launch traced here: 33.9 us
  starting transfers between devices  18.7 us (55%)
  waiting for transfers between devices  8.53 us (25%)
  Pallas kernels  4.65 us (14%)
  local copies, waits for them, and re-layouts  1.52 us (4%)
    ppermute x13, starting transfers between devices, swap(): return lax.ppermute(x, both, [(i, i ^ mask) for i in range(devices)])  18.7 us
    ppermute x13, waiting for transfers between devices, swap(): return lax.ppermute(x, both, [(i, i ^ mask) for i in range(devices)])  8.53 us
    pallas_call x9, Pallas kernels, call(): pl.pallas_call(body, out_shape=outs if len(outs) > 1 else outs[0], in_spe...  4.65 us
    unnamed x25, local copies, waits for them, and re-layouts  1.49 us
  transfers between devices with their start and end apart: 13, of which 6 were waited for; matrix products, arithmetic and copies ran while one was open for 1% of the time, Pallas kernels for 8%

profile of v2, /device:TPU:0, one launch (start us, length us, event | category | flops | bytes accessed | tf_op | source)
XLA Modules:
  0.0 33.9 jit_solution(7312249381801284309)
XLA Ops:
  0.0 2.9 %collective-permute-start = (bf16[128,128]{1,0:T(8,128)(2,1)}, bf16[128,128]{1,0:T(8,128)(2,1)S(1)}, u32[]{:S(2)}, u32[]{:S(2)}) collective-permute-start(bf16[128,128]{1,0:T(8,128)(2,1)} %refs_0_.3), channel_id=1, source_target_pairs={{0,1},{1,0},{2,3},{3,2},{4,5},{5,4},{6,7},{7,6},{8,9},{9,8},{10,11... | collective-permute-start | bytes 98312 | tf_op jit(solution)/shard_map/ppermute | solution.py:280
  2.9 1.5 %collective-permute-start.1 = (bf16[128,128]{1,0:T(8,128)(2,1)}, bf16[128,128]{1,0:T(8,128)(2,1)S(1)}, u32[]{:S(2)}, u32[]{:S(2)}) collective-permute-start(bf16[128,128]{1,0:T(8,128)(2,1)} %refs_0_.3), channel_id=1, source_target_pairs={{0,4},{1,5},{2,6},{3,7},{4,0},{5,1},{6,2},{7,3},{8,12},{9,13},{10,... | collective-permute-start | bytes 98312 | tf_op jit(solution)/shard_map/ppermute | solution.py:280
  4.5 0.0 collective-permute-start.2
  4.5 2.0 %collective-permute-start.4 = (f32[3,256]{1,0:T(4,128)}, f32[3,256]{1,0:T(4,128)S(1)}, u32[]{:S(2)}, u32[]{:S(2)}) collective-permute-start(f32[3,256]{1,0:T(4,128)} %bitcast.9), channel_id=1, source_target_pairs={{0,4},{1,5},{2,6},{3,7},{4,0},{5,1},{6,2},{7,3},{8,12},{9,13},{10,... | collective-permute-start | bytes 9224 | tf_op jit(solution)/shard_map/ppermute | solution.py:280
  6.5 0.7 %copy-done.11 = s32[768,3]{0,1:T(4,128)S(1)} copy-done((s32[768,3]{0,1:T(4,128)S(1)}, s32[768,3]{0,1:T(4,128)}, u32[]{:S(2)}) %copy-start.11) | copy-done | bytes 9240
  7.2 0.0 copy-done.8
  7.2 0.5 %shard_map.119 = (bf16[16,384]{1,0:T(8,128)(2,1)S(1)}, bf16[256,384]{1,0:T(8,128)(2,1)S(1)}) custom-call(f32[16,384]{1,0:T(8,128)S(1)} %shard_map.118.quarter_ref, s32[3,768]{1,0:T(4,128)S(1)} %bitcast.14, f32[3,256]{1,0:T(4,128)S(1)} %bitcast.10), custom_call_target="tpu_custom_call" | custom-call | flops 1474560000 | bytes 245760 | tf_op jit(solution)/shard_map/pallas_call | solution.py:43
  7.8 0.1 copy.14
  7.9 0.4 %collective-permute-done.4.refs_0_ = f32[3,256]{1,0:T(4,128)S(1)} collective-permute-done((f32[3,256]{1,0:T(4,128)}, f32[3,256]{1,0:T(4,128)S(1)}, u32[]{:S(2)}, u32[]{:S(2)}) %collective-permute-start.4) | collective-permute-done | bytes 3104 | tf_op jit(solution)/shard_map/ppermute | solution.py:280
  8.3 0.4 %shard_map.121.refs_5_.refs_1_ = bf16[256,384]{1,0:T(8,128)(2,1)S(1)} custom-call(f32[3,256]{1,0:T(4,128)S(1)} %collective-permute-done.4.refs_0_, bf16[16,384]{1,0:T(8,128)(2,1)S(1)} %get-tuple-element.11.refs_2_.refs_1_), custom_call_target="tpu_custom_call" | custom-call | flops 1474560000 | bytes 211968 | tf_op jit(solution)/shard_map/pallas_call | solution.py:43
  8.7 0.7 %collective-permute-done.5 = f32[3,512]{1,0:T(4,128)S(1)} collective-permute-done((f32[3,512]{1,0:T(4,128)S(1)}, f32[3,512]{1,0:T(4,128)S(1)}, u32[]{:S(2)}, u32[]{:S(2)}) %collective-permute-start.5) | collective-permute-done | bytes 6176 | tf_op jit(solution)/shard_map/ppermute | solution.py:280
  9.5 0.2 collective-permute-start.3
  9.8 0.6 %shard_map.120.refs_1_.refs_2_ = bf16[512,384]{1,0:T(8,128)(2,1)S(1)} custom-call(f32[3,256]{1,0:T(4,128)S(1)} %get-tuple-element.22.refs_0_, f32[3,256]{1,0:T(4,128)S(1)} %get-tuple-element.21.refs_1_, bf16[16,384]{1,0:T(8,128)(2,1)S(1)} %get-tuple-element.11.refs_2_.refs_1_), custom_call_target="tpu_custom_call" | custom-call | flops 2949120000 | bytes 411648 | tf_op jit(solution)/shard_map/pallas_call | solution.py:43
  10.4 0.3 shard_map.122.refs_2_
  10.7 0.3 collective-permute-done.3.refs_0_.refs_4_
  10.9 0.3 shard_map.123
  11.2 2.1 %collective-permute-start.6 = (bf16[144,384]{1,0:T(8,128)(2,1)S(1)}, bf16[144,384]{1,0:T(8,128)(2,1)S(1)}, u32[]{:S(2)}, u32[]{:S(2)}) collective-permute-start(bf16[144,384]{1,0:T(8,128)(2,1)S(1)} %shard_map.123), channel_id=1, source_target_pairs={{0,8},{1,9},{2,10},{3,11},{4,12},{5,13},{6,14},{7,15},{8,0},{9,1},... | collective-permute-start | bytes 331784 | tf_op jit(solution)/shard_map/ppermute | solution.py:280
  13.3 3.4 %collective-permute-done.6.refs_5_ = bf16[144,384]{1,0:T(8,128)(2,1)S(1)} collective-permute-done((bf16[144,384]{1,0:T(8,128)(2,1)S(1)}, bf16[144,384]{1,0:T(8,128)(2,1)S(1)}, u32[]{:S(2)}, u32[]{:S(2)}) %collective-permute-start.6) | collective-permute-done | bytes 110624 | tf_op jit(solution)/shard_map/ppermute | solution.py:280
  16.7 0.1 fusion.a_ref
  16.8 3.8 %collective-permute-start.7 = (bf16[144,384]{1,0:T(8,128)(2,1)S(1)}, bf16[144,384]{1,0:T(8,128)(2,1)S(1)}, u32[]{:S(2)}, u32[]{:S(2)}) collective-permute-start(bf16[144,384]{1,0:T(8,128)(2,1)S(1)} %fusion.a_ref), channel_id=1, source_target_pairs={{0,24},{1,25},{2,26},{3,27},{4,28},{5,29},{6,30},{7,31},{8,16},{9,... | collective-permute-start | bytes 331784 | tf_op jit(solution)/shard_map/ppermute | solution.py:280
  20.7 0.1 pad_maximum_fusion.filter_ref
  20.8 2.7 %collective-permute-done.7.refs_6_.b_ref = bf16[144,384]{1,0:T(8,128)(2,1)S(1)} collective-permute-done((bf16[144,384]{1,0:T(8,128)(2,1)S(1)}, bf16[144,384]{1,0:T(8,128)(2,1)S(1)}, u32[]{:S(2)}, u32[]{:S(2)}) %collective-permute-start.7) | collective-permute-done | bytes 110624 | tf_op jit(solution)/shard_map/ppermute | solution.py:280
  23.5 0.7 %shard_map.125 = (f32[384,128]{1,0:T(8,128)S(1)}, bf16[384,128]{1,0:T(8,128)(2,1)S(1)}, bf16[128,128]{1,0:T(8,128)(2,1)S(1)}, bf16[128,128]{1,0:T(8,128)(2,1)S(1)}) custom-call(bf16[144,384]{1,0:T(8,128)(2,1)S(1)} %fusion.a_ref, bf16[144,384]{1,0:T(8,128)(2,1)S(1)} %collective-permute-done.7.refs_6_.b_ref, bf16[2,128,128]{2,1,0:T(8,128)(2,1)S(1)} %copy-done.4, ...), custom_call_target="tpu_custom_call" | custom-call | flops 125829120 | bytes 1630208 | tf_op jit(solution)/shard_map/pallas_call | solution.py:43
  24.3 0.1 collective-permute-start.10
  24.3 2.7 %collective-permute-start.8 = (bf16[128,128]{1,0:T(8,128)(2,1)S(1)}, bf16[128,128]{1,0:T(8,128)(2,1)S(1)}, u32[]{:S(2)}, u32[]{:S(2)}) collective-permute-start(bf16[128,128]{1,0:T(8,128)(2,1)S(1)} %get-tuple-element.13), channel_id=1, source_target_pairs={{0,5},{1,4},{2,7},{3,6},{4,1},{5,0},{6,3},{7,2},{8,13},{9,12},{10,... | collective-permute-start | bytes 98312 | tf_op jit(solution)/shard_map/ppermute | solution.py:280
  27.0 0.1 collective-permute-start.9
  27.2 1.7 %collective-permute-start.11 = (bf16[128,128]{1,0:T(8,128)(2,1)S(1)}, bf16[128,128]{1,0:T(8,128)(2,1)S(1)}, u32[]{:S(2)}, u32[]{:S(2)}) collective-permute-start(bf16[128,128]{1,0:T(8,128)(2,1)S(1)} %get-tuple-element.20), channel_id=1, source_target_pairs={{0,1},{1,0},{2,3},{3,2},{4,5},{5,4},{6,7},{7,6},{8,9},{9,8},{10,11... | collective-permute-start | bytes 98312 | tf_op jit(solution)/shard_map/ppermute | solution.py:280
  28.9 1.5 %collective-permute-start.12 = (bf16[128,128]{1,0:T(8,128)(2,1)S(1)}, bf16[128,128]{1,0:T(8,128)(2,1)S(1)}, u32[]{:S(2)}, u32[]{:S(2)}) collective-permute-start(bf16[128,128]{1,0:T(8,128)(2,1)S(1)} %get-tuple-element.19), channel_id=1, source_target_pairs={{0,4},{1,5},{2,6},{3,7},{4,0},{5,1},{6,2},{7,3},{8,12},{9,13},{10,... | collective-permute-start | bytes 98312 | tf_op jit(solution)/shard_map/ppermute | solution.py:280
  30.4 0.6 %copy-done.10 = f32[128]{0:T(128)S(1)} copy-done((f32[128]{0:T(128)S(1)}, f32[128]{0:T(128)}, u32[]{:S(2)}) %copy-start.10) | copy-done | bytes 536
  31.1 0.7 %shard_map.124.refs_0_ = f32[128,128]{1,0:T(8,128)S(1)} custom-call(bf16[128,128]{1,0:T(8,128)(2,1)S(1)} %copy-done.1, bf16[128,128]{1,0:T(8,128)(2,1)S(1)} %collective-permute-done.refs_1_, bf16[128,128]{1,0:T(8,128)(2,1)S(1)} %collective-permute-done.1.refs_2_, bf16[128,128]{1,0:T(8,128)(2,1)S(1)} %collective-permute-done.2.refs_3_, ...), custom_call_target="tpu_custom_call" | custom-call | flops 100663296 | bytes 598528 | tf_op jit(solution)/shard_map/pallas_call | solution.py:43
  31.9 0.9 %collective-permute-done.12.refs_5_ = bf16[128,128]{1,0:T(8,128)(2,1)S(1)} collective-permute-done((bf16[128,128]{1,0:T(8,128)(2,1)S(1)}, bf16[128,128]{1,0:T(8,128)(2,1)S(1)}, u32[]{:S(2)}, u32[]{:S(2)}) %collective-permute-start.12) | collective-permute-done | bytes 32800 | tf_op jit(solution)/shard_map/ppermute | solution.py:280
  32.8 1.1 %shard_map.126 = bf16[128,128]{1,0:T(8,128)(2,1)} custom-call(f32[128,128]{1,0:T(8,128)S(1)} %shard_map.124.refs_0_, bf16[128,128]{1,0:T(8,128)(2,1)S(1)} %collective-permute-done.8.refs_1_, bf16[128,128]{1,0:T(8,128)(2,1)S(1)} %collective-permute-done.9.refs_2_, f32[128,128]{1,0:T(8,128)S(1)} %slice.24.refs_3_, ...), custom_call_target="tpu_custom_call" | custom-call | flops 33554432 | bytes 557568 | tf_op jit(solution)/shard_map/pallas_call | solution.py:43
  (38 shorter events, 0.2 us)
Async XLA Ops:
  0.0 7.7 %copy-start = (f32[768,128]{1,0:T(8,128)S(1)}, f32[768,128]{1,0:T(8,128)}, u32[]{:S(2)}) copy-start(f32[768,128]{1,0:T(8,128)} %param.15) | copy-start | bytes 1179652
  0.0 9.5 %collective-permute-start = (bf16[128,128]{1,0:T(8,128)(2,1)}, bf16[128,128]{1,0:T(8,128)(2,1)S(1)}, u32[]{:S(2)}, u32[]{:S(2)}) collective-permute-start(bf16[128,128]{1,0:T(8,128)(2,1)} %refs_0_.3), channel_id=1, source_target_pairs={{0,1},{1,0},{2,3},{3,2},{4,5},{5,4},{6,7},{7,6},{8,9},{9,8},{10,11... | collective-permute-start | bytes 98312 | tf_op jit(solution)/shard_map/ppermute | solution.py:280
  2.9 6.5 %collective-permute-start.1 = (bf16[128,128]{1,0:T(8,128)(2,1)}, bf16[128,128]{1,0:T(8,128)(2,1)S(1)}, u32[]{:S(2)}, u32[]{:S(2)}) collective-permute-start(bf16[128,128]{1,0:T(8,128)(2,1)} %refs_0_.3), channel_id=1, source_target_pairs={{0,4},{1,5},{2,6},{3,7},{4,0},{5,1},{6,2},{7,3},{8,12},{9,13},{10,... | collective-permute-start | bytes 98312 | tf_op jit(solution)/shard_map/ppermute | solution.py:280
  4.5 5.0 %collective-permute-start.2 = (bf16[128,128]{1,0:T(8,128)(2,1)}, bf16[128,128]{1,0:T(8,128)(2,1)S(1)}, u32[]{:S(2)}, u32[]{:S(2)}) collective-permute-start(bf16[128,128]{1,0:T(8,128)(2,1)} %refs_0_.3), channel_id=1, source_target_pairs={{0,5},{1,4},{2,7},{3,6},{4,1},{5,0},{6,3},{7,2},{8,13},{9,12},{10,... | collective-permute-start | bytes 98312 | tf_op jit(solution)/shard_map/ppermute | solution.py:280
  4.5 3.8 %collective-permute-start.4 = (f32[3,256]{1,0:T(4,128)}, f32[3,256]{1,0:T(4,128)S(1)}, u32[]{:S(2)}, u32[]{:S(2)}) collective-permute-start(f32[3,256]{1,0:T(4,128)} %bitcast.9), channel_id=1, source_target_pairs={{0,4},{1,5},{2,6},{3,7},{4,0},{5,1},{6,2},{7,3},{8,12},{9,13},{10,... | collective-permute-start | bytes 9224 | tf_op jit(solution)/shard_map/ppermute | solution.py:280
  6.5 0.7 %copy-start.11 = (s32[768,3]{0,1:T(4,128)S(1)}, s32[768,3]{0,1:T(4,128)}, u32[]{:S(2)}) copy-start(s32[768,3]{0,1:T(4,128)} %param.14) | copy-start | bytes 27652
  6.5 0.7 %copy-start.8 = (f32[256,3]{0,1:T(4,128)S(1)}, f32[256,3]{0,1:T(4,128)}, u32[]{:S(2)}) copy-start(f32[256,3]{0,1:T(4,128)} %param.13) | copy-start | bytes 9220
  8.3 1.2 %collective-permute-start.5 = (f32[3,512]{1,0:T(4,128)S(1)}, f32[3,512]{1,0:T(4,128)S(1)}, u32[]{:S(2)}, u32[]{:S(2)}) collective-permute-start(f32[3,512]{1,0:T(4,128)S(1)} %pad_maximum_fusion.2), channel_id=1, source_target_pairs={{0,2},{1,3},{2,0},{3,1},{4,6},{5,7},{6,4},{7,5},{8,10},{9,11},{10,... | collective-permute-start | bytes 18440 | tf_op jit(solution)/shard_map/ppermute | solution.py:280
  8.3 1.2 %copy-start.1 = (bf16[128,128]{1,0:T(8,128)(2,1)S(1)}, bf16[128,128]{1,0:T(8,128)(2,1)}, u32[]{:S(2)}) copy-start(bf16[128,128]{1,0:T(8,128)(2,1)} %refs_0_.3) | copy-start | bytes 98308
  9.5 1.4 %collective-permute-start.3 = (bf16[512,128]{1,0:T(8,128)(2,1)S(1)}, bf16[512,128]{1,0:T(8,128)(2,1)S(1)}, u32[]{:S(2)}, u32[]{:S(2)}) collective-permute-start(bf16[512,128]{1,0:T(8,128)(2,1)S(1)} %pad_maximum_fusion.1), channel_id=1, source_target_pairs={{0,2},{1,3},{2,0},{3,1},{4,6},{5,7},{6,4},{7,5},{8,10},{9,11},{10,... | collective-permute-start | bytes 393224 | tf_op jit(solution)/shard_map/ppermute | solution.py:280
  11.2 5.5 %collective-permute-start.6 = (bf16[144,384]{1,0:T(8,128)(2,1)S(1)}, bf16[144,384]{1,0:T(8,128)(2,1)S(1)}, u32[]{:S(2)}, u32[]{:S(2)}) collective-permute-start(bf16[144,384]{1,0:T(8,128)(2,1)S(1)} %shard_map.123), channel_id=1, source_target_pairs={{0,8},{1,9},{2,10},{3,11},{4,12},{5,13},{6,14},{7,15},{8,0},{9,1},... | collective-permute-start | bytes 331784 | tf_op jit(solution)/shard_map/ppermute | solution.py:280
  16.8 6.7 %collective-permute-start.7 = (bf16[144,384]{1,0:T(8,128)(2,1)S(1)}, bf16[144,384]{1,0:T(8,128)(2,1)S(1)}, u32[]{:S(2)}, u32[]{:S(2)}) collective-permute-start(bf16[144,384]{1,0:T(8,128)(2,1)S(1)} %fusion.a_ref), channel_id=1, source_target_pairs={{0,24},{1,25},{2,26},{3,27},{4,28},{5,29},{6,30},{7,31},{8,16},{9,... | collective-permute-start | bytes 331784 | tf_op jit(solution)/shard_map/ppermute | solution.py:280
  20.7 2.8 %copy-start.4 = (bf16[2,128,128]{2,1,0:T(8,128)(2,1)S(1)}, bf16[2,128,128]{2,1,0:T(8,128)(2,1)}, u32[]{:S(2)}) copy-start(bf16[2,128,128]{2,1,0:T(8,128)(2,1)} %mix_ref.1) | copy-start | bytes 196612
  24.3 2.8 %collective-permute-start.10 = (bf16[384,128]{1,0:T(8,128)(2,1)S(1)}, bf16[384,128]{1,0:T(8,128)(2,1)S(1)}, u32[]{:S(2)}, u32[]{:S(2)}) collective-permute-start(bf16[384,128]{1,0:T(8,128)(2,1)S(1)} %get-tuple-element.16), channel_id=1, source_target_pairs={{0,2},{1,3},{2,0},{3,1},{4,6},{5,7},{6,4},{7,5},{8,10},{9,11},{10,... | collective-permute-start | bytes 294920 | tf_op jit(solution)/shard_map/ppermute | solution.py:280
  24.3 7.5 %collective-permute-start.8 = (bf16[128,128]{1,0:T(8,128)(2,1)S(1)}, bf16[128,128]{1,0:T(8,128)(2,1)S(1)}, u32[]{:S(2)}, u32[]{:S(2)}) collective-permute-start(bf16[128,128]{1,0:T(8,128)(2,1)S(1)} %get-tuple-element.13), channel_id=1, source_target_pairs={{0,5},{1,4},{2,7},{3,6},{4,1},{5,0},{6,3},{7,2},{8,13},{9,12},{10,... | collective-permute-start | bytes 98312 | tf_op jit(solution)/shard_map/ppermute | solution.py:280
  27.0 4.9 %collective-permute-start.9 = (bf16[128,128]{1,0:T(8,128)(2,1)S(1)}, bf16[128,128]{1,0:T(8,128)(2,1)S(1)}, u32[]{:S(2)}, u32[]{:S(2)}) collective-permute-start(bf16[128,128]{1,0:T(8,128)(2,1)S(1)} %get-tuple-element.14), channel_id=1, source_target_pairs={{0,7},{1,6},{2,5},{3,4},{4,3},{5,2},{6,1},{7,0},{8,15},{9,14},{10,... | collective-permute-start | bytes 98312 | tf_op jit(solution)/shard_map/ppermute | solution.py:280
  27.1 3.3 %copy-start.5 = (bf16[128,128]{1,0:T(8,128)(2,1)S(1)}, bf16[128,128]{1,0:T(8,128)(2,1)}, u32[]{:S(2)}) copy-start(bf16[128,128]{1,0:T(8,128)(2,1)} %refs_7_.2) | copy-start | bytes 98308
  27.1 3.3 %copy-start.7 = (s32[128,16]{0,1:T(8,128)S(1)}, s32[128,16]{0,1:T(8,128)}, u32[]{:S(2)}) copy-start(s32[128,16]{0,1:T(8,128)} %param.20) | copy-start | bytes 24580
  27.2 3.3 %copy-start.6 = (f32[128,16]{0,1:T(8,128)S(1)}, f32[128,16]{0,1:T(8,128)}, u32[]{:S(2)}) copy-start(f32[128,16]{0,1:T(8,128)} %param.19) | copy-start | bytes 24580
  27.2 4.7 %collective-permute-start.11 = (bf16[128,128]{1,0:T(8,128)(2,1)S(1)}, bf16[128,128]{1,0:T(8,128)(2,1)S(1)}, u32[]{:S(2)}, u32[]{:S(2)}) collective-permute-start(bf16[128,128]{1,0:T(8,128)(2,1)S(1)} %get-tuple-element.20), channel_id=1, source_target_pairs={{0,1},{1,0},{2,3},{3,2},{4,5},{5,4},{6,7},{7,6},{8,9},{9,8},{10,11... | collective-permute-start | bytes 98312 | tf_op jit(solution)/shard_map/ppermute | solution.py:280
  28.9 3.9 %collective-permute-start.12 = (bf16[128,128]{1,0:T(8,128)(2,1)S(1)}, bf16[128,128]{1,0:T(8,128)(2,1)S(1)}, u32[]{:S(2)}, u32[]{:S(2)}) collective-permute-start(bf16[128,128]{1,0:T(8,128)(2,1)S(1)} %get-tuple-element.19), channel_id=1, source_target_pairs={{0,4},{1,5},{2,6},{3,7},{4,0},{5,1},{6,2},{7,3},{8,12},{9,13},{10,... | collective-permute-start | bytes 98312 | tf_op jit(solution)/shard_map/ppermute | solution.py:280
  30.4 0.7 %copy-start.10 = (f32[128]{0:T(128)S(1)}, f32[128]{0:T(128)}, u32[]{:S(2)}) copy-start(f32[128]{0:T(128)} %param.18) | copy-start | bytes 1540
  31.1 1.7 %copy-start.3 = (bf16[512,128]{1,0:T(8,128)(2,1)S(1)}, bf16[512,128]{1,0:T(8,128)(2,1)}, u32[]{:S(2)}) copy-start(bf16[512,128]{1,0:T(8,128)(2,1)} %refs_8_.1) | copy-start | bytes 393220
  31.8 1.0 %copy-start.2 = (bf16[128,512]{1,0:T(8,128)(2,1)S(1)}, bf16[128,512]{1,0:T(8,128)(2,1)}, u32[]{:S(2)}) copy-start(bf16[128,512]{1,0:T(8,128)(2,1)} %refs_7_.3) | copy-start | bytes 393220
  31.8 1.0 %copy-start.9 = (f32[128]{0:T(128)S(1)}, f32[128]{0:T(128)}, u32[]{:S(2)}) copy-start(f32[128]{0:T(128)} %param.21) | copy-start | bytes 1540

commit v3 on v1

v3 whole, which is shorter than its diff:
```python
import functools
import math

import jax
import jax.numpy as jnp
import numpy as np
from jax import lax
from jax.experimental import pallas as pl
from jax.experimental.pallas import tpu as pltpu
from jax.sharding import PartitionSpec as P

box_side = 16.0
slab_step = 0.125
coord_rows = 16
bf16, f32 = jnp.bfloat16, jnp.float32

both = ("space", "kgrp")

vector_flops = 15000


def fit_cosine(degree):
    count = 64
    theta = (np.arange(count) + 0.5) * math.pi / count
    u = 0.125 * (1.0 + np.cos(theta))
    values = np.cos(2.0 * math.pi * np.sqrt(u))
    cheb = np.polynomial.chebyshev.Chebyshev.fit(u, values, degree, domain=[0.0, 0.25])
    return [float(c) for c in cheb.convert(kind=np.polynomial.Polynomial).coef]


cosine = fit_cosine(6)


def dot(a, b, dims):
    return lax.dot_general(a, b, (dims, ((), ())), preferred_element_type=f32)


def whole(count):
    return [pl.BlockSpec(memory_space=pltpu.VMEM)] * count


def call(body, outs, *args, flops=0, transcendentals=0):
    moved = sum(a.size * a.dtype.itemsize for a in (*args, *outs))
    return pl.pallas_call(
        body,
        out_shape=outs if len(outs) > 1 else outs[0],
        in_specs=whole(len(args)),
        out_specs=whole(len(outs)) if len(outs) > 1 else whole(1)[0],
        cost_estimate=pl.CostEstimate(
            flops=flops, bytes_accessed=moved, transcendentals=transcendentals
        ),
        compiler_params=pltpu.CompilerParams(vmem_limit_bytes=24 * 1024 * 1024),
    )(*args)


def shape(dims, dtype):
    return jax.ShapeDtypeStruct(dims, dtype)


def layer_member(members):
    member = lax.axis_index("space") * lax.axis_size("kgrp") + lax.axis_index("kgrp")
    return member & (members - 1)


def pack(features, positions, groups, slab_length):
    atoms, channels = features.shape
    scale = jnp.array([[1.0 / box_side], [1.0 / box_side], [1.0 / slab_length]], f32)
    turns = positions.T * scale
    high = lax.reduce_precision(turns, 8, 7)
    rest = turns - high
    middle = lax.reduce_precision(rest, 8, 7)
    parts = [high, middle, rest - middle, jnp.ones((1, groups * atoms), f32)]
    parts.append(jnp.zeros((coord_rows - 10, groups * atoms), f32))
    parts = jnp.concatenate(parts, axis=0).astype(bf16)
    split = [parts[:, i * atoms : (i + 1) * atoms] for i in range(groups)]
    return jnp.concatenate([features, *split], axis=0)


def fill_phases(block_ref, waves, groups, phase_ref):
    group = lax.axis_index("kgrp")
    atoms = phase_ref.shape[0] // groups
    for i in range(groups):
        row = pl.multiple_of(atoms + (group ^ i) * coord_rows, coord_rows)
        turns = dot(block_ref[pl.ds(row, coord_rows), :], waves, ((0,), (0,)))
        part = turns - jnp.round(turns)
        u = part * part
        value = jnp.full_like(u, cosine[-1])
        for c in cosine[-2::-1]:
            value = value * u + c
        phase_ref[i * atoms : (i + 1) * atoms, :] = value.astype(bf16)


def prepare_body(inner, groups, index_ref, block_ref, wave_ref, phase_ref):
    share = index_ref.shape[1] // inner
    own = lax.axis_index("space") & (inner - 1)
    counts = index_ref[...].astype(f32)
    halves = []
    for which in (own, own ^ 1):
        mine = counts[:, :share]
        for i in range(1, inner):
            mine = jnp.where(which == i, counts[:, i * share : (i + 1) * share], mine)
        halves += [mine, mine]
    counts = jnp.concatenate(halves, axis=1)
    column = lax.broadcasted_iota(jnp.int32, (1, 4 * share), 1)
    cosines = (column < share) | ((column >= 2 * share) & (column < 3 * share))
    quarter = jnp.where(cosines, 0.0, -0.25)
    zeros = jnp.zeros((coord_rows - 10, 4 * share), f32)
    waves = jnp.concatenate([counts, counts, counts, quarter, zeros], axis=0)
    wave_ref[...] = waves.astype(bf16)
    fill_phases(block_ref, wave_ref[...], groups, phase_ref)


def phase_body(groups, block_ref, wave_ref, phase_ref):
    fill_phases(block_ref, wave_ref[...], groups, phase_ref)


def add_blocks(block_refs, phase_ref, total):
    atoms = phase_ref.shape[0] // len(block_refs)
    for i, ref in enumerate(block_refs):
        phase = phase_ref[i * atoms : (i + 1) * atoms, :]
        term = dot(ref[:atoms, :], phase, ((0,), (0,)))
        total = term if total is None else total + term
    return total


def structure_body(*refs):
    *block_refs, phase_ref, sum_ref = refs
    sum_ref[...] = add_blocks(block_refs, phase_ref, None)


def stack(ref, total):
    channels = ref.shape[1]
    for i in range(total.shape[1] // channels):
        part = total[:, i * channels : (i + 1) * channels]
        ref[i * channels : (i + 1) * channels, :] = part.astype(ref.dtype)


def split_body(blocks, members, groups, masks, *refs):
    block_refs, refs = refs[:blocks], refs[blocks:]
    phase_ref, carry_ref, *far_refs, keep_ref, send_ref = refs
    total = add_blocks(block_refs, phase_ref, carry_ref[...])
    columns = total.shape[1] // 2
    stack(keep_ref, total[:, :columns])
    stack(send_ref, total[:, columns:])
    atoms = phase_ref.shape[0] // blocks
    halo = atoms // 4
    other = layer_member(members) ^ groups
    even = (other & 1) == 0
    edge = None
    for mask, ref in zip(masks, far_refs):
        rows = jnp.where(even, ref[atoms - halo : atoms, :], ref[:halo, :])
        if edge is None:
            edge = rows
        else:
            edge = jnp.where(reaches(other, even, mask), rows, edge)
    sums = send_ref.shape[0] - halo
    keep_ref[sums:, :] = jnp.zeros_like(keep_ref[sums:, :])
    send_ref[sums:, :] = edge


def reaches(member, even, mask):
    start = jnp.where(even, member, member + 1)
    return (start & mask) == (mask + 1) // 2


def mix_body(scale, a_ref, b_ref, mix_ref, filter_ref, y_ref):
    channels, columns = y_ref.shape
    tiles = [
        a_ref[i : i + channels, :].astype(f32) + b_ref[i : i + channels, :].astype(f32)
        for i in range(0, columns, channels)
    ]
    amps = (jnp.concatenate(tiles, axis=1) * scale).astype(bf16)
    half = amps.shape[1] // 2
    straight = dot(mix_ref[0], amps, ((0,), (0,)))
    crossed = dot(mix_ref[1], amps, ((0,), (0,)))
    crossed = jnp.concatenate([-crossed[:, half:], crossed[:, :half]], axis=1)
    y_ref[...] = (filter_ref[...] * (straight + crossed)).astype(bf16)


def near_body(phases, *refs):
    phase_refs, (y_ref, out_ref) = refs[:phases], refs[phases:]
    row = 0
    for ref in phase_refs:
        rows = ref.shape[0]
        out_ref[row : row + rows, :] = dot(ref[:, : y_ref.shape[1]], y_ref[...], ((1,), (1,)))
        row += rows


def far_body(phases, inv_scale, *refs):
    phase_refs, (y_ref, near_ref, *out_refs) = refs[:phases], refs[phases:]
    row = 0
    atoms = out_refs[0].shape[0]
    for ref in phase_refs:
        term = dot(ref[:, y_ref.shape[1] :], y_ref[...], ((1,), (1,)))
        for i in range(ref.shape[0] // atoms):
            block = term[i * atoms : (i + 1) * atoms] + near_ref[row : row + atoms, :]
            out = out_refs[row // atoms]
            out[...] = (block * inv_scale).astype(out.dtype)
            row += atoms


def hold_body(count, *refs):
    for a, b in zip(refs[:count], refs[count + 1 :]):
        b[...] = a[...]


def message_body(members, groups, masks, stages, *refs):
    feat_ref, *refs = refs
    near_refs, refs = refs[: len(masks)], refs[len(masks) :]
    core_ref, *refs = refs
    stage_refs, refs = refs[:stages], refs[stages:]
    msg_ref, width_ref, dist_ref, nbr_ref, base_ref = refs
    atoms, channels = dist_ref.shape[1], feat_ref.shape[1]
    features = feat_ref[:atoms, :]
    halo = atoms // 4
    member = layer_member(members)
    even = (member & 1) == 0
    layer = lax.axis_index("space") // (members // groups)

    def edge_of(ref):
        return ref[ref.shape[0] - halo :, :]

    start = jnp.where(even, layer, layer + 1)
    across = None
    for i, ref in enumerate(stage_refs):
        edge = edge_of(ref)
        across = edge if i == 0 else jnp.where((start & ((1 << i) - 1)) == 0, edge, across)
    far = edge_of(core_ref)
    if stages:
        ends = (member == 0) | (member == members - 1)
        far = jnp.where(ends, across, far)
    for mask, ref in zip(masks[1:], near_refs[1:]):
        rows = jnp.where(even, ref[atoms - halo : atoms, :], ref[:halo, :])
        far = jnp.where(reaches(member, even, mask), rows, far)
    beside = near_refs[0]
    before = jnp.where(even, far, beside[atoms - halo : atoms, :])
    after = jnp.where(even, beside[:halo, :], far)
    extended = jnp.concatenate([before, features, after], axis=0)
    projected = dot(msg_ref[...], extended, ((0,), (1,))).astype(bf16)
    row = lax.broadcasted_iota(jnp.int32, (extended.shape[0], atoms), 0)
    inverse = -1.0 / jnp.broadcast_to(width_ref[...], (atoms, channels)).T
    message = jnp.zeros((channels, atoms), f32)
    for j in range(nbr_ref.shape[0]):
        chosen = jnp.where(row == nbr_ref[j : j + 1, :], 1.0, 0.0).astype(bf16)
        nearby = dot(projected, chosen, ((1,), (0,)))
        message = message + jnp.exp(dist_ref[j : j + 1, :] * inverse) * nearby
    base_ref[...] = features.astype(f32) + message.T


def final_body(peers, *refs):
    base_ref, *refs = refs
    peer_refs, (gain_ref, in_ref, out_ref, result_ref) = refs[:peers], refs[peers:]
    mixed = base_ref[...]
    for ref in peer_refs:
        mixed = mixed + ref[...].astype(f32)
    inverse = lax.rsqrt(jnp.mean(mixed * mixed, axis=1, keepdims=True) + 1e-06)
    normed = (mixed * inverse * gain_ref[...]).astype(bf16)
    hidden = dot(normed, in_ref[...], ((1,), (0,)))
    half = 0.5 * hidden
    hidden = (half + half * jnp.tanh(half)).astype(bf16)
    result_ref[...] = (mixed + dot(hidden, out_ref[...], ((1,), (0,)))).astype(bf16)


def local(
    outer,
    features,
    positions,
    wave_index,
    wave_filter,
    mix_pair,
    msg_weight,
    chan_width,
    pair_dist,
    neighbours,
    norm_gain,
    in_weight,
    out_weight,
):
    atoms, channels = features.shape
    groups, space = lax.axis_size("kgrp"), lax.axis_size("space")
    inner = space // outer
    members = inner * groups
    devices = space * groups
    total_atoms = atoms * devices
    slab_length = total_atoms * slab_step
    share = wave_index.shape[0] // inner
    columns = 2 * share
    own_rows = groups * atoms

    def swap(x, mask):
        return lax.ppermute(x, both, [(i, i ^ mask) for i in range(devices)])

    near = [m for m in range(members) if not m & groups]
    bases = [m for m in near if m % groups == 0]
    block = {0: features}
    packed = pack(features, positions, groups, slab_length)
    for m in sorted(near[1:], key=lambda m: -m.bit_count()):
        block[m] = swap(features if m % groups else packed, m)
    waves, own_phase = call(
        functools.partial(prepare_body, inner, groups),
        (shape((coord_rows, 2 * columns), bf16), shape((own_rows, 2 * columns), bf16)),
        wave_index.T,
        packed,
        flops=vector_flops * 2 * own_rows * columns,
    )
    phase = [own_phase]
    for m in bases[1:]:
        phase.append(
            call(
                functools.partial(phase_body, groups),
                (shape((own_rows, 2 * columns), bf16),),
                block[m],
                waves,
                flops=vector_flops * own_rows * columns,
            )
        )

    work = 4 * own_rows * columns * channels
    part = None
    for m, rows in zip(bases[:-1], phase[:-1]):
        here = call(
            structure_body,
            (shape((channels, 2 * columns), f32),),
            *[block[m + i] if m + i else packed for i in range(groups)],
            rows,
            flops=work,
        )
        part = here if part is None else part + here
    chain = [(2 << i) - 1 for i in range(members.bit_length() - 1)]
    far_masks = [m for m in reversed(chain) if m & groups]
    height = columns + atoms // 4
    keep, send = call(
        functools.partial(split_body, groups, members, groups, far_masks),
        (shape((height, channels), f32), shape((height, channels), bf16)),
        *[block[bases[-1] + i] for i in range(groups)],
        phase[-1],
        part,
        *[block[m ^ groups] for m in far_masks],
        flops=work,
    )
    arrived = swap(send, groups)
    amps = (keep + arrived.astype(f32)).astype(bf16)

    stages = []
    sums = lax.broadcasted_iota(jnp.int32, amps.shape, 0) < columns
    while (1 << len(stages)) < outer:
        if stages:
            both_sums = amps.astype(f32) + stages[-1].astype(f32)
            amps = jnp.where(sums, both_sums, amps.astype(f32)).astype(bf16)
        stages.append(swap(amps, ((2 << len(stages)) - 1) * members))
    other = stages[-1] if stages else jnp.zeros_like(amps)
    held = (
        msg_weight,
        chan_width.reshape(1, channels),
        pair_dist.T,
        neighbours.T,
        norm_gain.reshape(1, channels),
        in_weight,
        out_weight,
    )
    held = call(
        functools.partial(hold_body, len(held)),
        tuple(shape(x.shape, x.dtype) for x in held),
        *held,
        amps,
        flops=2 * 10**9,
    )
    other, held = lax.optimization_barrier((other, held))
    msg_weight, chan_width, pair_dist, neighbours, norm_gain, in_weight, out_weight = held

    first = (lax.axis_index("space") % inner) * share
    filters = lax.dynamic_slice_in_dim(wave_filter, first, share, 0).T
    filters = jnp.concatenate([filters, filters], axis=1)
    y = call(
        functools.partial(mix_body, 1.0 / math.sqrt(total_atoms)),
        (shape((channels, columns), bf16),),
        amps,
        other,
        mix_pair,
        filters,
        flops=4 * channels * channels * columns,
    )
    y_far = swap(y, groups)
    work = 2 * len(near) * atoms * channels * columns
    near_terms = call(
        functools.partial(near_body, len(phase)),
        (shape((len(near) * atoms, channels), f32),),
        *phase,
        y,
        flops=work,
    )
    terms = call(
        functools.partial(far_body, len(phase), 1.0 / math.sqrt(wave_index.shape[0] * groups)),
        tuple(shape((atoms, channels), bf16 if m else f32) for m in near),
        *phase,
        y_far,
        near_terms,
        flops=work,
    )
    peers = [terms[0]]
    for m in sorted(near[1:], key=lambda m: -m.bit_count()):
        peers.append(swap(terms[near.index(m)], m))

    near_masks = [m for m in chain if not m & groups]
    base = call(
        functools.partial(message_body, members, groups, near_masks, len(stages)),
        (shape((atoms, channels), f32),),
        packed,
        *[block[m] for m in near_masks],
        arrived,
        *stages,
        msg_weight,
        chan_width,
        pair_dist,
        neighbours,
        flops=3 * channels * atoms * neighbours.shape[0] * atoms,
        transcendentals=atoms * neighbours.shape[0] * channels,
    )
    return call(
        functools.partial(final_body, len(peers)),
        (shape((atoms, channels), bf16),),
        base,
        *peers,
        norm_gain,
        in_weight,
        out_weight,
        flops=4 * atoms * channels * in_weight.shape[1],
    )


def layers(mesh):
    depths = {getattr(d, "coords", (0, 0, i))[2] for i, d in enumerate(mesh.devices[:, 0])}
    return len(depths)


def solution(mesh):
    placed = (
        P(both, None),
        P("space", None),
        P("kgrp", None),
        P("kgrp", None),
        P(),
        P(),
        P(),
        P(both, None),
        P(both, None),
        P(),
        P(),
        P(),
    )
    return jax.shard_map(
        functools.partial(local, layers(mesh)),
        mesh=mesh,
        in_specs=placed,
        out_specs=P(both, None),
        check_vma=False,
    )
```

time: 39.3 us -> 32.8 us (0.83)
  starting transfers between devices: 19.4 us -> 13.6 us
  local copies, waits for them, and re-layouts: 2.58 us -> 1.51 us
  waiting for transfers between devices: 11.1 us -> 11.6 us
    ppermute x1 -> x0, starting transfers between devices: 5.76 us -> none  [local(): before = after = lax.ppermute(edge, both, pairs)]
    unnamed x25, local copies, waits for them, and re-layouts: 2.3 us -> 1.35 us
    convert_element_type x2, other arithmetic: 0.79 us -> 0.15 us  [the longest x1 0.12 us: local(): amps = jnp.where(sums, both_sums, amps.astype(f32)).astype(bf16)]
    another operation x3 -> x1, other arithmetic: 0.12 us -> 0.76 us
    ppermute x13 -> x10, waiting for transfers between devices: 11.1 us -> 11.6 us  [swap(): return lax.ppermute(x, both, [(i, i ^ mask) for i in range(devices)])]
    ppermute x13 -> x10, starting transfers between devices: 13.7 us -> 13.6 us  [swap(): return lax.ppermute(x, both, [(i, i ^ mask) for i in range(devices)])]
    pallas_call x6 -> x10, Pallas kernels: 4.5 us -> 4.52 us  [call(): pl.pallas_call(body, out_shape=outs if len(outs) > 1 else outs[0], in_spe...]
  transfers between devices with their start and end apart: 14 -> 10, of which waited for: 6 -> 8; matrix products, arithmetic and copies ran while one was open for 4% -> 3% of each run, Pallas kernels for 4% -> 8%
where the time goes in v3:
time: 32.8 us; the launch traced here: 32.5 us
  starting transfers between devices  13.6 us (41%)
  waiting for transfers between devices  11.6 us (35%)
  Pallas kernels  4.52 us (14%)
  local copies, waits for them, and re-layouts  1.51 us (5%)
  other arithmetic  1.02 us (3%)
    ppermute x10, starting transfers between devices, swap(): return lax.ppermute(x, both, [(i, i ^ mask) for i in range(devices)])  13.6 us
    ppermute x10, waiting for transfers between devices, swap(): return lax.ppermute(x, both, [(i, i ^ mask) for i in range(devices)])  11.6 us
    pallas_call x10, Pallas kernels, call(): pl.pallas_call(body, out_shape=outs if len(outs) > 1 else outs[0], in_spe...  4.52 us
    unnamed x25, local copies, waits for them, and re-layouts  1.35 us
    another operation x1, other arithmetic  0.76 us
  transfers between devices with their start and end apart: 10, of which 8 were waited for; matrix products, arithmetic and copies ran while one was open for 3% of the time, Pallas kernels for 8%

profile of v3, /device:TPU:0, one launch (start us, length us, event | category | flops | bytes accessed | tf_op | source)
XLA Modules:
  0.0 32.5 jit_solution(9660060308642329035)
XLA Ops:
  0.0 3.0 %collective-permute-start = (bf16[128,128]{1,0:T(8,128)(2,1)}, bf16[128,128]{1,0:T(8,128)(2,1)S(1)}, u32[]{:S(2)}, u32[]{:S(2)}) collective-permute-start(bf16[128,128]{1,0:T(8,128)(2,1)} %param.13), channel_id=1, source_target_pairs={{0,1},{1,0},{2,3},{3,2},{4,5},{5,4},{6,7},{7,6},{8,9},{9,8},{10,11... | collective-permute-start | bytes 98312 | tf_op jit(solution)/shard_map/ppermute | solution.py:291
  3.0 1.5 %collective-permute-start.2 = (bf16[128,128]{1,0:T(8,128)(2,1)}, bf16[128,128]{1,0:T(8,128)(2,1)S(1)}, u32[]{:S(2)}, u32[]{:S(2)}) collective-permute-start(bf16[128,128]{1,0:T(8,128)(2,1)} %param.13), channel_id=1, source_target_pairs={{0,5},{1,4},{2,7},{3,6},{4,1},{5,0},{6,3},{7,2},{8,13},{9,12},{10,... | collective-permute-start | bytes 98312 | tf_op jit(solution)/shard_map/ppermute | solution.py:291
  4.5 0.8 %fusion.1 = (bf16[3,256]{1,0:T(4,128)(2,1)S(1)}, bf16[3,256]{1,0:T(4,128)(2,1)S(1)}, bf16[3,256]{1,0:T(4,128)(2,1)S(1)}) fusion(f32[256,3]{0,1:T(4,128)} %param.14, f32[3]{0:T(128)S(1)} %copy-done.11), kind=kLoop, calls=%fused_computation.9 | loop fusion | flops 6144 | bytes 7692 | tf_op jit(solution)/shard_map/convert.2
  5.3 0.1 concatenate.10
  5.4 0.1 collective-permute-start.1
  5.6 0.6 %copy-done.5 = s32[768,3]{0,1:T(4,128)S(1)} copy-done((s32[768,3]{0,1:T(4,128)S(1)}, s32[768,3]{0,1:T(4,128)}, u32[]{:S(2)}) %copy-start.5) | copy-done | bytes 9240
  6.1 0.7 %shard_map.127 = (bf16[16,768]{1,0:T(8,128)(2,1)S(1)}, bf16[256,768]{1,0:T(8,128)(2,1)S(1)}) custom-call(s32[3,768]{1,0:T(4,128)S(1)} %bitcast.13, bf16[160,128]{1,0:T(8,128)(2,1)S(1)} %pad_maximum_fusion.1.block_ref.refs_0_), custom_call_target="tpu_custom_call" | custom-call | flops 2949120000 | bytes 467968 | tf_op jit(solution)/shard_map/pallas_call | solution.py:44
  6.9 0.1 copy.15
  7.1 0.3 shard_map.129.refs_3_
  7.3 2.2 %collective-permute-done.1.block_ref.refs_0_ = bf16[160,128]{1,0:T(8,128)(2,1)S(1)} collective-permute-done((bf16[160,128]{1,0:T(8,128)(2,1)S(1)}, bf16[160,128]{1,0:T(8,128)(2,1)S(1)}, u32[]{:S(2)}, u32[]{:S(2)}) %collective-permute-start.1) | collective-permute-done | bytes 40992 | tf_op jit(solution)/shard_map/ppermute | solution.py:291
  9.5 0.6 %shard_map.128.refs_2_.refs_1_ = bf16[256,768]{1,0:T(8,128)(2,1)S(1)} custom-call(bf16[160,128]{1,0:T(8,128)(2,1)S(1)} %collective-permute-done.1.block_ref.refs_0_, bf16[16,768]{1,0:T(8,128)(2,1)S(1)} %get-tuple-element.28.wave_ref), custom_call_target="tpu_custom_call" | custom-call | flops 1474560000 | bytes 458752 | tf_op jit(solution)/shard_map/pallas_call | solution.py:44
  10.1 0.3 shard_map.130
  10.5 0.1 pad_maximum_fusion.filter_ref
  10.6 1.2 %collective-permute-done.3.refs_2_ = bf16[416,128]{1,0:T(8,128)(2,1)S(1)} collective-permute-done((bf16[416,128]{1,0:T(8,128)(2,1)S(1)}, bf16[416,128]{1,0:T(8,128)(2,1)S(1)}, u32[]{:S(2)}, u32[]{:S(2)}) %collective-permute-start.3) | collective-permute-done | bytes 106528 | tf_op jit(solution)/shard_map/ppermute | solution.py:291
  11.8 1.6 %collective-permute-start.4 = (bf16[416,128]{1,0:T(8,128)(2,1)S(1)}, bf16[416,128]{1,0:T(8,128)(2,1)S(1)}, u32[]{:S(2)}, u32[]{:S(2)}) collective-permute-start(bf16[416,128]{1,0:T(8,128)(2,1)S(1)} %add_convert_fusion), channel_id=1, source_target_pairs={{0,8},{1,9},{2,10},{3,11},{4,12},{5,13},{6,14},{7,15},{8,0},{9,1},... | collective-permute-start | bytes 319496 | tf_op jit(solution)/shard_map/ppermute | solution.py:291
  13.5 3.4 %collective-permute-done.4.refs_3_ = bf16[416,128]{1,0:T(8,128)(2,1)S(1)} collective-permute-done((bf16[416,128]{1,0:T(8,128)(2,1)S(1)}, bf16[416,128]{1,0:T(8,128)(2,1)S(1)}, u32[]{:S(2)}, u32[]{:S(2)}) %collective-permute-start.4) | collective-permute-done | bytes 106528 | tf_op jit(solution)/shard_map/ppermute | solution.py:291
  16.9 0.1 fusion.refs_7_.a_ref
  17.0 3.7 %collective-permute-start.5 = (bf16[416,128]{1,0:T(8,128)(2,1)S(1)}, bf16[416,128]{1,0:T(8,128)(2,1)S(1)}, u32[]{:S(2)}, u32[]{:S(2)}) collective-permute-start(bf16[416,128]{1,0:T(8,128)(2,1)S(1)} %fusion.refs_7_.a_ref), channel_id=1, source_target_pairs={{0,24},{1,25},{2,26},{3,27},{4,28},{5,29},{6,30},{7,31},{8,16},{9,... | collective-permute-start | bytes 319496 | tf_op jit(solution)/shard_map/ppermute | solution.py:291
  20.8 0.6 %copy-done.8 = f32[128]{0:T(128)S(1)} copy-done((f32[128]{0:T(128)S(1)}, f32[128]{0:T(128)}, u32[]{:S(2)}) %copy-start.8) | copy-done | bytes 536
  21.4 2.3 %collective-permute-done.5.refs_4_.b_ref = bf16[416,128]{1,0:T(8,128)(2,1)S(1)} collective-permute-done((bf16[416,128]{1,0:T(8,128)(2,1)S(1)}, bf16[416,128]{1,0:T(8,128)(2,1)S(1)}, u32[]{:S(2)}, u32[]{:S(2)}) %collective-permute-start.5) | collective-permute-done | bytes 106528 | tf_op jit(solution)/shard_map/ppermute | solution.py:291
  23.7 0.3 shard_map.133.refs_2_
  24.1 0.3 shard_map.134.refs_3_
  24.3 1.0 %collective-permute-done.6.refs_2_ = bf16[128,384]{1,0:T(8,128)(2,1)S(1)} collective-permute-done((bf16[128,384]{1,0:T(8,128)(2,1)S(1)}, bf16[128,384]{1,0:T(8,128)(2,1)S(1)}, u32[]{:S(2)}, u32[]{:S(2)}) %collective-permute-start.6) | collective-permute-done | bytes 98336 | tf_op jit(solution)/shard_map/ppermute | solution.py:291
  25.4 0.3 shard_map.135
  25.6 1.5 %collective-permute-start.7 = (bf16[128,128]{1,0:T(8,128)(2,1)S(1)}, bf16[128,128]{1,0:T(8,128)(2,1)S(1)}, u32[]{:S(2)}, u32[]{:S(2)}) collective-permute-start(bf16[128,128]{1,0:T(8,128)(2,1)S(1)} %get-tuple-element.45), channel_id=1, source_target_pairs={{0,5},{1,4},{2,7},{3,6},{4,1},{5,0},{6,3},{7,2},{8,13},{9,12},{10,... | collective-permute-start | bytes 98312 | tf_op jit(solution)/shard_map/ppermute | solution.py:291
  27.1 0.4 %collective-permute-start.8 = (bf16[128,128]{1,0:T(8,128)(2,1)S(1)}, bf16[128,128]{1,0:T(8,128)(2,1)S(1)}, u32[]{:S(2)}, u32[]{:S(2)}) collective-permute-start(bf16[128,128]{1,0:T(8,128)(2,1)S(1)} %get-tuple-element.46), channel_id=1, source_target_pairs={{0,1},{1,0},{2,3},{3,2},{4,5},{5,4},{6,7},{7,6},{8,9},{9,8},{10,11... | collective-permute-start | bytes 98312 | tf_op jit(solution)/shard_map/ppermute | solution.py:291
  27.6 1.6 %collective-permute-start.9 = (bf16[128,128]{1,0:T(8,128)(2,1)S(1)}, bf16[128,128]{1,0:T(8,128)(2,1)S(1)}, u32[]{:S(2)}, u32[]{:S(2)}) collective-permute-start(bf16[128,128]{1,0:T(8,128)(2,1)S(1)} %get-tuple-element.47), channel_id=1, source_target_pairs={{0,4},{1,5},{2,6},{3,7},{4,0},{5,1},{6,2},{7,3},{8,12},{9,13},{10,... | collective-permute-start | bytes 98312 | tf_op jit(solution)/shard_map/ppermute | solution.py:291
  29.2 0.7 %shard_map.132.refs_0_ = f32[128,128]{1,0:T(8,128)S(1)} custom-call(bf16[160,128]{1,0:T(8,128)(2,1)S(1)} %pad_maximum_fusion.1.block_ref.refs_0_, bf16[128,128]{1,0:T(8,128)(2,1)S(1)} %collective-permute-done.refs_1_.refs_5_, bf16[416,128]{1,0:T(8,128)(2,1)S(1)} %collective-permute-done.3.refs_2_, bf16[416,128]{1,0:T(8,128)(2,1)S(1)} %collective-permute-done.4.refs_3_, ...), custom_call_target="tpu_custom_call" | custom-call | flops 100663296 | bytes 508416 | tf_op jit(solution)/shard_map/pallas_call | solution.py:44
  29.9 0.6 %collective-permute-done.7.refs_2_ = bf16[128,128]{1,0:T(8,128)(2,1)S(1)} collective-permute-done((bf16[128,128]{1,0:T(8,128)(2,1)S(1)}, bf16[128,128]{1,0:T(8,128)(2,1)S(1)}, u32[]{:S(2)}, u32[]{:S(2)}) %collective-permute-start.7) | collective-permute-done | bytes 32800 | tf_op jit(solution)/shard_map/ppermute | solution.py:291
  30.5 0.5 %collective-permute-done.8.refs_3_ = bf16[128,128]{1,0:T(8,128)(2,1)S(1)} collective-permute-done((bf16[128,128]{1,0:T(8,128)(2,1)S(1)}, bf16[128,128]{1,0:T(8,128)(2,1)S(1)}, u32[]{:S(2)}, u32[]{:S(2)}) %collective-permute-start.8) | collective-permute-done | bytes 32800 | tf_op jit(solution)/shard_map/ppermute | solution.py:291
  31.1 0.4 %collective-permute-done.9.refs_4_ = bf16[128,128]{1,0:T(8,128)(2,1)S(1)} collective-permute-done((bf16[128,128]{1,0:T(8,128)(2,1)S(1)}, bf16[128,128]{1,0:T(8,128)(2,1)S(1)}, u32[]{:S(2)}, u32[]{:S(2)}) %collective-permute-start.9) | collective-permute-done | bytes 32800 | tf_op jit(solution)/shard_map/ppermute | solution.py:291
  31.5 1.0 %shard_map.136 = bf16[128,128]{1,0:T(8,128)(2,1)} custom-call(f32[128,128]{1,0:T(8,128)S(1)} %shard_map.132.refs_0_, f32[128,128]{1,0:T(8,128)S(1)} %get-tuple-element.44.refs_1_, bf16[128,128]{1,0:T(8,128)(2,1)S(1)} %collective-permute-done.7.refs_2_, bf16[128,128]{1,0:T(8,128)(2,1)S(1)} %collective-permute-done.8.refs_3_, ...), custom_call_target="tpu_custom_call" | custom-call | flops 33554432 | bytes 524800 | tf_op jit(solution)/shard_map/pallas_call | solution.py:44
  (34 shorter events, 0.3 us)
Async XLA Ops:
  0.0 6.9 %copy-start = (f32[768,128]{1,0:T(8,128)S(1)}, f32[768,128]{1,0:T(8,128)}, u32[]{:S(2)}) copy-start(f32[768,128]{1,0:T(8,128)} %param.16) | copy-start | bytes 1179652
  0.0 4.5 %copy-start.11 = (f32[3]{0:T(128)S(1)}, f32[3]{0:T(128)}, u32[]{:S(2)}) copy-start(f32[3]{0:T(128)} %constant.35) | copy-start | bytes 40
  0.0 5.4 %copy-start.10 = (bf16[128,128]{1,0:T(8,128)(2,1)S(1)}, bf16[128,128]{1,0:T(8,128)(2,1)}, u32[]{:S(2)}) copy-start(bf16[128,128]{1,0:T(8,128)(2,1)} %param.13) | copy-start | bytes 98308
  0.0 7.0 %collective-permute-start = (bf16[128,128]{1,0:T(8,128)(2,1)}, bf16[128,128]{1,0:T(8,128)(2,1)S(1)}, u32[]{:S(2)}, u32[]{:S(2)}) collective-permute-start(bf16[128,128]{1,0:T(8,128)(2,1)} %param.13), channel_id=1, source_target_pairs={{0,1},{1,0},{2,3},{3,2},{4,5},{5,4},{6,7},{7,6},{8,9},{9,8},{10,11... | collective-permute-start | bytes 98312 | tf_op jit(solution)/shard_map/ppermute | solution.py:291
  3.0 7.1 %collective-permute-start.2 = (bf16[128,128]{1,0:T(8,128)(2,1)}, bf16[128,128]{1,0:T(8,128)(2,1)S(1)}, u32[]{:S(2)}, u32[]{:S(2)}) collective-permute-start(bf16[128,128]{1,0:T(8,128)(2,1)} %param.13), channel_id=1, source_target_pairs={{0,5},{1,4},{2,7},{3,6},{4,1},{5,0},{6,3},{7,2},{8,13},{9,12},{10,... | collective-permute-start | bytes 98312 | tf_op jit(solution)/shard_map/ppermute | solution.py:291
  5.4 0.7 %copy-start.5 = (s32[768,3]{0,1:T(4,128)S(1)}, s32[768,3]{0,1:T(4,128)}, u32[]{:S(2)}) copy-start(s32[768,3]{0,1:T(4,128)} %param.15) | copy-start | bytes 27652
  5.4 4.1 %collective-permute-start.1 = (bf16[160,128]{1,0:T(8,128)(2,1)S(1)}, bf16[160,128]{1,0:T(8,128)(2,1)S(1)}, u32[]{:S(2)}, u32[]{:S(2)}) collective-permute-start(bf16[160,128]{1,0:T(8,128)(2,1)S(1)} %pad_maximum_fusion.1.block_ref.refs_0_), channel_id=1, source_target_pairs={{0,4},{1,5},{2,6},{3,7},{4,0},{5,1},{6,2},{7,3},{8,12},{9,13},{10,... | collective-permute-start | bytes 122888 | tf_op jit(solution)/shard_map/ppermute | solution.py:291
  10.4 1.4 %collective-permute-start.3 = (bf16[416,128]{1,0:T(8,128)(2,1)S(1)}, bf16[416,128]{1,0:T(8,128)(2,1)S(1)}, u32[]{:S(2)}, u32[]{:S(2)}) collective-permute-start(bf16[416,128]{1,0:T(8,128)(2,1)S(1)} %get-tuple-element.30), channel_id=1, source_target_pairs={{0,2},{1,3},{2,0},{3,1},{4,6},{5,7},{6,4},{7,5},{8,10},{9,11},{10,... | collective-permute-start | bytes 319496 | tf_op jit(solution)/shard_map/ppermute | solution.py:291
  11.8 5.1 %collective-permute-start.4 = (bf16[416,128]{1,0:T(8,128)(2,1)S(1)}, bf16[416,128]{1,0:T(8,128)(2,1)S(1)}, u32[]{:S(2)}, u32[]{:S(2)}) collective-permute-start(bf16[416,128]{1,0:T(8,128)(2,1)S(1)} %add_convert_fusion), channel_id=1, source_target_pairs={{0,8},{1,9},{2,10},{3,11},{4,12},{5,13},{6,14},{7,15},{8,0},{9,1},... | collective-permute-start | bytes 319496 | tf_op jit(solution)/shard_map/ppermute | solution.py:291
  13.5 7.2 %copy-start.2 = (bf16[128,512]{1,0:T(8,128)(2,1)S(1)}, bf16[128,512]{1,0:T(8,128)(2,1)}, u32[]{:S(2)}) copy-start(bf16[128,512]{1,0:T(8,128)(2,1)} %refs_5_.1) | copy-start | bytes 393220
  13.5 7.2 %copy-start.3 = (bf16[512,128]{1,0:T(8,128)(2,1)S(1)}, bf16[512,128]{1,0:T(8,128)(2,1)}, u32[]{:S(2)}) copy-start(bf16[512,128]{1,0:T(8,128)(2,1)} %refs_6_.1) | copy-start | bytes 393220
  13.5 7.3 %copy-start.4 = (bf16[128,128]{1,0:T(8,128)(2,1)S(1)}, bf16[128,128]{1,0:T(8,128)(2,1)}, u32[]{:S(2)}) copy-start(bf16[128,128]{1,0:T(8,128)(2,1)} %refs_0_.1) | copy-start | bytes 98308
  13.5 7.2 %copy-start.6 = (f32[128,16]{0,1:T(8,128)S(1)}, f32[128,16]{0,1:T(8,128)}, u32[]{:S(2)}) copy-start(f32[128,16]{0,1:T(8,128)} %param.20) | copy-start | bytes 24580
  13.5 7.2 %copy-start.7 = (s32[128,16]{0,1:T(8,128)S(1)}, s32[128,16]{0,1:T(8,128)}, u32[]{:S(2)}) copy-start(s32[128,16]{0,1:T(8,128)} %param.21) | copy-start | bytes 24580
  17.0 6.6 %collective-permute-start.5 = (bf16[416,128]{1,0:T(8,128)(2,1)S(1)}, bf16[416,128]{1,0:T(8,128)(2,1)S(1)}, u32[]{:S(2)}, u32[]{:S(2)}) collective-permute-start(bf16[416,128]{1,0:T(8,128)(2,1)S(1)} %fusion.refs_7_.a_ref), channel_id=1, source_target_pairs={{0,24},{1,25},{2,26},{3,27},{4,28},{5,29},{6,30},{7,31},{8,16},{9,... | collective-permute-start | bytes 319496 | tf_op jit(solution)/shard_map/ppermute | solution.py:291
  20.7 0.7 %copy-start.8 = (f32[128]{0:T(128)S(1)}, f32[128]{0:T(128)}, u32[]{:S(2)}) copy-start(f32[128]{0:T(128)} %param.19) | copy-start | bytes 1540
  20.7 0.7 %copy-start.9 = (f32[128]{0:T(128)S(1)}, f32[128]{0:T(128)}, u32[]{:S(2)}) copy-start(f32[128]{0:T(128)} %param.22) | copy-start | bytes 1540
  21.4 2.3 %copy-start.1 = (bf16[2,128,128]{2,1,0:T(8,128)(2,1)S(1)}, bf16[2,128,128]{2,1,0:T(8,128)(2,1)}, u32[]{:S(2)}) copy-start(bf16[2,128,128]{2,1,0:T(8,128)(2,1)} %mix_ref.1) | copy-start | bytes 196612
  24.0 1.4 %collective-permute-start.6 = (bf16[128,384]{1,0:T(8,128)(2,1)S(1)}, bf16[128,384]{1,0:T(8,128)(2,1)S(1)}, u32[]{:S(2)}, u32[]{:S(2)}) collective-permute-start(bf16[128,384]{1,0:T(8,128)(2,1)S(1)} %shard_map.133.refs_2_), channel_id=1, source_target_pairs={{0,2},{1,3},{2,0},{3,1},{4,6},{5,7},{6,4},{7,5},{8,10},{9,11},{10,... | collective-permute-start | bytes 294920 | tf_op jit(solution)/shard_map/ppermute | solution.py:291
  25.6 4.9 %collective-permute-start.7 = (bf16[128,128]{1,0:T(8,128)(2,1)S(1)}, bf16[128,128]{1,0:T(8,128)(2,1)S(1)}, u32[]{:S(2)}, u32[]{:S(2)}) collective-permute-start(bf16[128,128]{1,0:T(8,128)(2,1)S(1)} %get-tuple-element.45), channel_id=1, source_target_pairs={{0,5},{1,4},{2,7},{3,6},{4,1},{5,0},{6,3},{7,2},{8,13},{9,12},{10,... | collective-permute-start | bytes 98312 | tf_op jit(solution)/shard_map/ppermute | solution.py:291
  27.1 3.9 %collective-permute-start.8 = (bf16[128,128]{1,0:T(8,128)(2,1)S(1)}, bf16[128,128]{1,0:T(8,128)(2,1)S(1)}, u32[]{:S(2)}, u32[]{:S(2)}) collective-permute-start(bf16[128,128]{1,0:T(8,128)(2,1)S(1)} %get-tuple-element.46), channel_id=1, source_target_pairs={{0,1},{1,0},{2,3},{3,2},{4,5},{5,4},{6,7},{7,6},{8,9},{9,8},{10,11... | collective-permute-start | bytes 98312 | tf_op jit(solution)/shard_map/ppermute | solution.py:291
  27.6 3.9 %collective-permute-start.9 = (bf16[128,128]{1,0:T(8,128)(2,1)S(1)}, bf16[128,128]{1,0:T(8,128)(2,1)S(1)}, u32[]{:S(2)}, u32[]{:S(2)}) collective-permute-start(bf16[128,128]{1,0:T(8,128)(2,1)S(1)} %get-tuple-element.47), channel_id=1, source_target_pairs={{0,4},{1,5},{2,6},{3,7},{4,0},{5,1},{6,2},{7,3},{8,12},{9,13},{10,... | collective-permute-start | bytes 98312 | tf_op jit(solution)/shard_map/ppermute | solution.py:291

commit v4 on v3

--- a/solution.py
+++ b/solution.py
@@ -57,6 +57,11 @@
     return jax.ShapeDtypeStruct(dims, dtype)
 
 
+def wave_share(inner):
+    space = lax.axis_index("space")
+    return (space ^ (space // inner & 1)) & (inner - 1)
+
+
 def layer_member(members):
     member = lax.axis_index("space") * lax.axis_size("kgrp") + lax.axis_index("kgrp")
     return member & (members - 1)
@@ -92,7 +97,7 @@
 
 def prepare_body(inner, groups, index_ref, block_ref, wave_ref, phase_ref):
     share = index_ref.shape[1] // inner
-    own = lax.axis_index("space") & (inner - 1)
+    own = wave_share(inner)
     counts = index_ref[...].astype(f32)
     halves = []
     for which in (own, own ^ 1):
@@ -114,6 +119,10 @@
     fill_phases(block_ref, wave_ref[...], groups, phase_ref)
 
 
+def features_body(block_ref, out_ref):
+    out_ref[...] = block_ref[: out_ref.shape[0], :]
+
+
 def add_blocks(block_refs, phase_ref, total):
     atoms = phase_ref.shape[0] // len(block_refs)
     for i, ref in enumerate(block_refs):
@@ -137,25 +146,26 @@
 
 def split_body(blocks, members, groups, masks, *refs):
     block_refs, refs = refs[:blocks], refs[blocks:]
-    phase_ref, carry_ref, *far_refs, keep_ref, send_ref = refs
+    phase_ref, carry_ref, *far_refs, end_ref, keep_ref, send_ref = refs
     total = add_blocks(block_refs, phase_ref, carry_ref[...])
     columns = total.shape[1] // 2
     stack(keep_ref, total[:, :columns])
     stack(send_ref, total[:, columns:])
     atoms = phase_ref.shape[0] // blocks
     halo = atoms // 4
+    sums = keep_ref.shape[0] - halo
     other = layer_member(members) ^ groups
     even = (other & 1) == 0
-    edge = None
-    for mask, ref in zip(masks, far_refs):
-        rows = jnp.where(even, ref[atoms - halo : atoms, :], ref[:halo, :])
-        if edge is None:
-            edge = rows
-        else:
-            edge = jnp.where(reaches(other, even, mask), rows, edge)
-    sums = send_ref.shape[0] - halo
+
+    def beside(ref):
+        return jnp.where(even, ref[atoms - halo : atoms, :], ref[:halo, :])
+
     keep_ref[sums:, :] = jnp.zeros_like(keep_ref[sums:, :])
-    send_ref[sums:, :] = edge
+    send_ref[sums : sums + halo, :] = beside(end_ref)
+    needed = beside(far_refs[0])
+    for mask, ref in zip(masks[1:], far_refs[1:]):
+        needed = jnp.where(reaches(other, even, mask), beside(ref), needed)
+    send_ref[sums + halo :, :] = needed
 
 
 def reaches(member, even, mask):
@@ -290,12 +300,19 @@
     def swap(x, mask):
         return lax.ppermute(x, both, [(i, i ^ mask) for i in range(devices)])
 
-    near = [m for m in range(members) if not m & groups]
-    bases = [m for m in near if m % groups == 0]
+    bases = []
+    for i in range(inner // 2):
+        bases.append((2 * i + i.bit_count() % 2) * groups)
+    near = [m + i for m in bases for i in range(groups)]
+    farthest = sorted(near[1:], key=lambda m: -(m & ~groups).bit_count())
     block = {0: features}
     packed = pack(features, positions, groups, slab_length)
-    for m in sorted(near[1:], key=lambda m: -m.bit_count()):
-        block[m] = swap(features if m % groups else packed, m)
+    copied = call(
+        features_body, (shape((atoms, channels), bf16),), packed, flops=vector_flops * 300000
+    )
+    for m in near[1:]:
+        source = packed if m % groups == 0 else features if m < groups else copied
+        block[m] = swap(source, m)
     waves, own_phase = call(
         functools.partial(prepare_body, inner, groups),
         (shape((coord_rows, 2 * columns), bf16), shape((own_rows, 2 * columns), bf16)),
@@ -327,19 +344,20 @@
         )
         part = here if part is None else part + here
     chain = [(2 << i) - 1 for i in range(members.bit_length() - 1)]
-    far_masks = [m for m in reversed(chain) if m & groups]
+    far_masks = [m for m in reversed(chain) if m not in near]
     height = columns + atoms // 4
     keep, send = call(
         functools.partial(split_body, groups, members, groups, far_masks),
-        (shape((height, channels), f32), shape((height, channels), bf16)),
+        (shape((height, channels), f32), shape((height + atoms // 4, channels), bf16)),
         *[block[bases[-1] + i] for i in range(groups)],
         phase[-1],
         part,
         *[block[m ^ groups] for m in far_masks],
+        block[members - 1],
         flops=work,
     )
     arrived = swap(send, groups)
-    amps = (keep + arrived.astype(f32)).astype(bf16)
+    amps = (keep + arrived[:height].astype(f32)).astype(bf16)
 
     stages = []
     sums = lax.broadcasted_iota(jnp.int32, amps.shape, 0) < columns
@@ -347,7 +365,7 @@
         if stages:
             both_sums = amps.astype(f32) + stages[-1].astype(f32)
             amps = jnp.where(sums, both_sums, amps.astype(f32)).astype(bf16)
-        stages.append(swap(amps, ((2 << len(stages)) - 1) * members))
+        stages.append(swap(amps, ((2 << len(stages)) - 1) * members ^ groups))
     other = stages[-1] if stages else jnp.zeros_like(amps)
     held = (
         msg_weight,
@@ -368,7 +386,7 @@
     other, held = lax.optimization_barrier((other, held))
     msg_weight, chan_width, pair_dist, neighbours, norm_gain, in_weight, out_weight = held
 
-    first = (lax.axis_index("space") % inner) * share
+    first = wave_share(inner) * share
     filters = lax.dynamic_slice_in_dim(wave_filter, first, share, 0).T
     filters = jnp.concatenate([filters, filters], axis=1)
     y = call(
@@ -398,10 +416,10 @@
         flops=work,
     )
     peers = [terms[0]]
-    for m in sorted(near[1:], key=lambda m: -m.bit_count()):
+    for m in farthest:
         peers.append(swap(terms[near.index(m)], m))
 
-    near_masks = [m for m in chain if not m & groups]
+    near_masks = [m for m in chain if m in near]
     base = call(
         functools.partial(message_body, members, groups, near_masks, len(stages)),
         (shape((atoms, channels), f32),),

time: 32.8 us -> 31.8 us (0.970)
  waiting for transfers between devices: 11.6 us -> 10.6 us
  starting transfers between devices: 13.6 us -> 14.3 us
  local copies, waits for them, and re-layouts: 1.51 us -> 0.93 us
    ppermute x10, waiting for transfers between devices: 11.6 us -> 10.6 us  [swap(): return lax.ppermute(x, both, [(i, i ^ mask) for i in range(devices)])]
    ppermute x10, starting transfers between devices: 13.6 us -> 14.3 us  [swap(): return lax.ppermute(x, both, [(i, i ^ mask) for i in range(devices)])]
    unnamed x25, local copies, waits for them, and re-layouts: 1.35 us -> 0.77 us
    pallas_call x10 -> x11, Pallas kernels: 4.52 us -> 4.52 us  [call(): pl.pallas_call(body, out_shape=outs if len(outs) > 1 else outs[0], in_spe...]
  transfers between devices with their start and end apart: 10 -> 10, of which waited for: 8 -> 9; matrix products, arithmetic and copies ran while one was open for 3% -> 4% of each run, Pallas kernels for 8% -> 8%
where the time goes in v4:
time: 31.8 us; the launch traced here: 31.6 us
  starting transfers between devices  14.3 us (45%)
  waiting for transfers between devices  10.6 us (33%)
  Pallas kernels  4.52 us (14%)
  other arithmetic  1.02 us (3%)
  local copies, waits for them, and re-layouts  0.93 us (3%)
    ppermute x10, starting transfers between devices, swap(): return lax.ppermute(x, both, [(i, i ^ mask) for i in range(devices)])  14.3 us
    ppermute x10, waiting for transfers between devices, swap(): return lax.ppermute(x, both, [(i, i ^ mask) for i in range(devices)])  10.6 us
    pallas_call x11, Pallas kernels, call(): pl.pallas_call(body, out_shape=outs if len(outs) > 1 else outs[0], in_spe...  4.52 us
    unnamed x25, local copies, waits for them, and re-layouts  0.77 us
    another operation x1, other arithmetic  0.76 us
  transfers between devices with their start and end apart: 10, of which 9 were waited for; matrix products, arithmetic and copies ran while one was open for 4% of the time, Pallas kernels for 8%

profile of v4, /device:TPU:0, one launch (start us, length us, event | category | flops | bytes accessed | tf_op | source)
XLA Modules:
  0.0 31.6 jit_solution(5252425963187240496)
XLA Ops:
  0.0 3.0 %collective-permute-start = (bf16[128,128]{1,0:T(8,128)(2,1)}, bf16[128,128]{1,0:T(8,128)(2,1)S(1)}, u32[]{:S(2)}, u32[]{:S(2)}) collective-permute-start(bf16[128,128]{1,0:T(8,128)(2,1)} %param.13), channel_id=1, source_target_pairs={{0,1},{1,0},{2,3},{3,2},{4,5},{5,4},{6,7},{7,6},{8,9},{9,8},{10,11... | collective-permute-start | bytes 98312 | tf_op jit(solution)/shard_map/ppermute | solution.py:301
  3.0 0.8 %fusion.1 = (bf16[3,256]{1,0:T(4,128)(2,1)S(1)}, bf16[3,256]{1,0:T(4,128)(2,1)S(1)}, bf16[3,256]{1,0:T(4,128)(2,1)S(1)}) fusion(f32[256,3]{0,1:T(4,128)} %param.14, f32[3]{0:T(128)S(1)} %copy-done.11), kind=kLoop, calls=%fused_computation.9 | loop fusion | flops 6144 | bytes 7692 | tf_op jit(solution)/shard_map/convert.2
  3.8 0.1 concatenate.10
  3.9 0.7 %collective-permute-start.2 = (bf16[160,128]{1,0:T(8,128)(2,1)S(1)}, bf16[160,128]{1,0:T(8,128)(2,1)S(1)}, u32[]{:S(2)}, u32[]{:S(2)}) collective-permute-start(bf16[160,128]{1,0:T(8,128)(2,1)S(1)} %pad_maximum_fusion.1.block_ref.refs_0_), channel_id=1, source_target_pairs={{0,6},{1,7},{2,4},{3,5},{4,2},{5,3},{6,0},{7,1},{8,14},{9,15},{10,... | collective-permute-start | bytes 122888 | tf_op jit(solution)/shard_map/ppermute | solution.py:301
  4.7 1.1 %collective-permute-start.1 = (bf16[128,128]{1,0:T(8,128)(2,1)S(1)}, bf16[128,128]{1,0:T(8,128)(2,1)S(1)}, u32[]{:S(2)}, u32[]{:S(2)}) collective-permute-start(bf16[128,128]{1,0:T(8,128)(2,1)S(1)} %shard_map.127), channel_id=1, source_target_pairs={{0,7},{1,6},{2,5},{3,4},{4,3},{5,2},{6,1},{7,0},{8,15},{9,14},{10,... | collective-permute-start | bytes 98312 | tf_op jit(solution)/shard_map/ppermute | solution.py:301
  5.8 0.7 %shard_map.128 = (bf16[16,768]{1,0:T(8,128)(2,1)S(1)}, bf16[256,768]{1,0:T(8,128)(2,1)S(1)}) custom-call(s32[3,768]{1,0:T(4,128)S(1)} %bitcast.13, bf16[160,128]{1,0:T(8,128)(2,1)S(1)} %pad_maximum_fusion.1.block_ref.refs_0_), custom_call_target="tpu_custom_call" | custom-call | flops 2949120000 | bytes 467968 | tf_op jit(solution)/shard_map/pallas_call | solution.py:44
  6.7 0.3 shard_map.130.refs_3_
  7.0 0.8 %collective-permute-done.2.block_ref.refs_0_ = bf16[160,128]{1,0:T(8,128)(2,1)S(1)} collective-permute-done((bf16[160,128]{1,0:T(8,128)(2,1)S(1)}, bf16[160,128]{1,0:T(8,128)(2,1)S(1)}, u32[]{:S(2)}, u32[]{:S(2)}) %collective-permute-start.2) | collective-permute-done | bytes 40992 | tf_op jit(solution)/shard_map/ppermute | solution.py:301
  7.8 0.6 %shard_map.129.refs_2_.refs_1_ = bf16[256,768]{1,0:T(8,128)(2,1)S(1)} custom-call(bf16[160,128]{1,0:T(8,128)(2,1)S(1)} %collective-permute-done.2.block_ref.refs_0_, bf16[16,768]{1,0:T(8,128)(2,1)S(1)} %get-tuple-element.28.wave_ref), custom_call_target="tpu_custom_call" | custom-call | flops 1474560000 | bytes 458752 | tf_op jit(solution)/shard_map/pallas_call | solution.py:44
  8.4 0.5 %collective-permute-done.1.refs_1_.refs_5_.refs_2_ = bf16[128,128]{1,0:T(8,128)(2,1)S(1)} collective-permute-done((bf16[128,128]{1,0:T(8,128)(2,1)S(1)}, bf16[128,128]{1,0:T(8,128)(2,1)S(1)}, u32[]{:S(2)}, u32[]{:S(2)}) %collective-permute-start.1) | collective-permute-done | bytes 32800 | tf_op jit(solution)/shard_map/ppermute | solution.py:301
  8.9 0.3 shard_map.131
  9.2 1.0 %collective-permute-start.3 = (bf16[448,128]{1,0:T(8,128)(2,1)S(1)}, bf16[448,128]{1,0:T(8,128)(2,1)S(1)}, u32[]{:S(2)}, u32[]{:S(2)}) collective-permute-start(bf16[448,128]{1,0:T(8,128)(2,1)S(1)} %get-tuple-element.30), channel_id=1, source_target_pairs={{0,2},{1,3},{2,0},{3,1},{4,6},{5,7},{6,4},{7,5},{8,10},{9,11},{10,... | collective-permute-start | bytes 344072 | tf_op jit(solution)/shard_map/ppermute | solution.py:301
  10.4 0.9 %collective-permute-done.3.refs_3_ = bf16[448,128]{1,0:T(8,128)(2,1)S(1)} collective-permute-done((bf16[448,128]{1,0:T(8,128)(2,1)S(1)}, bf16[448,128]{1,0:T(8,128)(2,1)S(1)}, u32[]{:S(2)}, u32[]{:S(2)}) %collective-permute-start.3) | collective-permute-done | bytes 114720 | tf_op jit(solution)/shard_map/ppermute | solution.py:301
  11.3 1.6 %collective-permute-start.4 = (bf16[416,128]{1,0:T(8,128)(2,1)S(1)}, bf16[416,128]{1,0:T(8,128)(2,1)S(1)}, u32[]{:S(2)}, u32[]{:S(2)}) collective-permute-start(bf16[416,128]{1,0:T(8,128)(2,1)S(1)} %add_convert_fusion), channel_id=1, source_target_pairs={{0,10},{1,11},{2,8},{3,9},{4,14},{5,15},{6,12},{7,13},{8,2},{9,3},... | collective-permute-start | bytes 319496 | tf_op jit(solution)/shard_map/ppermute | solution.py:301
  12.9 3.2 %collective-permute-done.4.refs_4_ = bf16[416,128]{1,0:T(8,128)(2,1)S(1)} collective-permute-done((bf16[416,128]{1,0:T(8,128)(2,1)S(1)}, bf16[416,128]{1,0:T(8,128)(2,1)S(1)}, u32[]{:S(2)}, u32[]{:S(2)}) %collective-permute-start.4) | collective-permute-done | bytes 106528 | tf_op jit(solution)/shard_map/ppermute | solution.py:301
  16.1 0.1 fusion.refs_7_.a_ref
  16.3 3.5 %collective-permute-start.5 = (bf16[416,128]{1,0:T(8,128)(2,1)S(1)}, bf16[416,128]{1,0:T(8,128)(2,1)S(1)}, u32[]{:S(2)}, u32[]{:S(2)}) collective-permute-start(bf16[416,128]{1,0:T(8,128)(2,1)S(1)} %fusion.refs_7_.a_ref), channel_id=1, source_target_pairs={{0,26},{1,27},{2,24},{3,25},{4,30},{5,31},{6,28},{7,29},{8,18},{9,... | collective-permute-start | bytes 319496 | tf_op jit(solution)/shard_map/ppermute | solution.py:301
  19.9 0.6 %copy-done.8 = f32[128]{0:T(128)S(1)} copy-done((f32[128]{0:T(128)S(1)}, f32[128]{0:T(128)}, u32[]{:S(2)}) %copy-start.8) | copy-done | bytes 536
  20.5 2.6 %collective-permute-done.5.refs_5_.b_ref = bf16[416,128]{1,0:T(8,128)(2,1)S(1)} collective-permute-done((bf16[416,128]{1,0:T(8,128)(2,1)S(1)}, bf16[416,128]{1,0:T(8,128)(2,1)S(1)}, u32[]{:S(2)}, u32[]{:S(2)}) %collective-permute-start.5) | collective-permute-done | bytes 106528 | tf_op jit(solution)/shard_map/ppermute | solution.py:301
  23.1 0.3 %shard_map.134.refs_2_ = bf16[128,384]{1,0:T(8,128)(2,1)S(1)} custom-call(bf16[416,128]{1,0:T(8,128)(2,1)S(1)} %fusion.refs_7_.a_ref, bf16[416,128]{1,0:T(8,128)(2,1)S(1)} %collective-permute-done.5.refs_5_.b_ref, bf16[2,128,128]{2,1,0:T(8,128)(2,1)S(1)} %copy-done.1, f32[128,384]{1,0:T(8,128)S(1)} %pad_maximum_fusion.filter_ref), custom_call_target="tpu_custom_call" | custom-call | flops 25165824 | bytes 573440 | tf_op jit(solution)/shard_map/pallas_call | solution.py:44
  23.5 0.3 collective-permute-start.6
  23.7 0.3 shard_map.135.refs_3_
  24.0 0.8 %collective-permute-done.6.refs_2_ = bf16[128,384]{1,0:T(8,128)(2,1)S(1)} collective-permute-done((bf16[128,384]{1,0:T(8,128)(2,1)S(1)}, bf16[128,384]{1,0:T(8,128)(2,1)S(1)}, u32[]{:S(2)}, u32[]{:S(2)}) %collective-permute-start.6) | collective-permute-done | bytes 98336 | tf_op jit(solution)/shard_map/ppermute | solution.py:301
  24.8 0.3 shard_map.136
  25.1 0.5 %collective-permute-start.7 = (bf16[128,128]{1,0:T(8,128)(2,1)S(1)}, bf16[128,128]{1,0:T(8,128)(2,1)S(1)}, u32[]{:S(2)}, u32[]{:S(2)}) collective-permute-start(bf16[128,128]{1,0:T(8,128)(2,1)S(1)} %get-tuple-element.45), channel_id=1, source_target_pairs={{0,7},{1,6},{2,5},{3,4},{4,3},{5,2},{6,1},{7,0},{8,15},{9,14},{10,... | collective-permute-start | bytes 98312 | tf_op jit(solution)/shard_map/ppermute | solution.py:301
  25.6 1.4 %collective-permute-start.8 = (bf16[128,128]{1,0:T(8,128)(2,1)S(1)}, bf16[128,128]{1,0:T(8,128)(2,1)S(1)}, u32[]{:S(2)}, u32[]{:S(2)}) collective-permute-start(bf16[128,128]{1,0:T(8,128)(2,1)S(1)} %get-tuple-element.46), channel_id=1, source_target_pairs={{0,1},{1,0},{2,3},{3,2},{4,5},{5,4},{6,7},{7,6},{8,9},{9,8},{10,11... | collective-permute-start | bytes 98312 | tf_op jit(solution)/shard_map/ppermute | solution.py:301
  27.0 1.1 %collective-permute-start.9 = (bf16[128,128]{1,0:T(8,128)(2,1)S(1)}, bf16[128,128]{1,0:T(8,128)(2,1)S(1)}, u32[]{:S(2)}, u32[]{:S(2)}) collective-permute-start(bf16[128,128]{1,0:T(8,128)(2,1)S(1)} %get-tuple-element.47), channel_id=1, source_target_pairs={{0,6},{1,7},{2,4},{3,5},{4,2},{5,3},{6,0},{7,1},{8,14},{9,15},{10,... | collective-permute-start | bytes 98312 | tf_op jit(solution)/shard_map/ppermute | solution.py:301
  28.1 0.7 %shard_map.133.refs_0_ = f32[128,128]{1,0:T(8,128)S(1)} custom-call(bf16[160,128]{1,0:T(8,128)(2,1)S(1)} %pad_maximum_fusion.1.block_ref.refs_0_, bf16[128,128]{1,0:T(8,128)(2,1)S(1)} %collective-permute-done.refs_1_.refs_4_, bf16[128,128]{1,0:T(8,128)(2,1)S(1)} %collective-permute-done.1.refs_1_.refs_5_.refs_2_, ...), custom_call_target="tpu_custom_call" | custom-call | flops 100663296 | bytes 549376 | tf_op jit(solution)/shard_map/pallas_call | solution.py:44
  28.8 0.6 %collective-permute-done.7.refs_2_ = bf16[128,128]{1,0:T(8,128)(2,1)S(1)} collective-permute-done((bf16[128,128]{1,0:T(8,128)(2,1)S(1)}, bf16[128,128]{1,0:T(8,128)(2,1)S(1)}, u32[]{:S(2)}, u32[]{:S(2)}) %collective-permute-start.7) | collective-permute-done | bytes 32800 | tf_op jit(solution)/shard_map/ppermute | solution.py:301
  29.4 0.1 collective-permute-done.8.refs_3_
  29.5 1.1 %collective-permute-done.9.refs_4_ = bf16[128,128]{1,0:T(8,128)(2,1)S(1)} collective-permute-done((bf16[128,128]{1,0:T(8,128)(2,1)S(1)}, bf16[128,128]{1,0:T(8,128)(2,1)S(1)}, u32[]{:S(2)}, u32[]{:S(2)}) %collective-permute-start.9) | collective-permute-done | bytes 32800 | tf_op jit(solution)/shard_map/ppermute | solution.py:301
  30.6 1.0 %shard_map.137 = bf16[128,128]{1,0:T(8,128)(2,1)} custom-call(f32[128,128]{1,0:T(8,128)S(1)} %shard_map.133.refs_0_, f32[128,128]{1,0:T(8,128)S(1)} %get-tuple-element.44.refs_1_, bf16[128,128]{1,0:T(8,128)(2,1)S(1)} %collective-permute-done.7.refs_2_, bf16[128,128]{1,0:T(8,128)(2,1)S(1)} %collective-permute-done.8.refs_3_, ...), custom_call_target="tpu_custom_call" | custom-call | flops 33554432 | bytes 524800 | tf_op jit(solution)/shard_map/pallas_call | solution.py:44
  (35 shorter events, 0.3 us)
Async XLA Ops:
  0.0 6.6 %copy-start = (f32[768,128]{1,0:T(8,128)S(1)}, f32[768,128]{1,0:T(8,128)}, u32[]{:S(2)}) copy-start(f32[768,128]{1,0:T(8,128)} %param.16) | copy-start | bytes 1179652
  0.0 3.0 %copy-start.11 = (f32[3]{0:T(128)S(1)}, f32[3]{0:T(128)}, u32[]{:S(2)}) copy-start(f32[3]{0:T(128)} %constant.40) | copy-start | bytes 40
  0.0 3.9 %copy-start.10 = (bf16[128,128]{1,0:T(8,128)(2,1)S(1)}, bf16[128,128]{1,0:T(8,128)(2,1)}, u32[]{:S(2)}) copy-start(bf16[128,128]{1,0:T(8,128)(2,1)} %param.13) | copy-start | bytes 98308
  0.0 6.7 %collective-permute-start = (bf16[128,128]{1,0:T(8,128)(2,1)}, bf16[128,128]{1,0:T(8,128)(2,1)S(1)}, u32[]{:S(2)}, u32[]{:S(2)}) collective-permute-start(bf16[128,128]{1,0:T(8,128)(2,1)} %param.13), channel_id=1, source_target_pairs={{0,1},{1,0},{2,3},{3,2},{4,5},{5,4},{6,7},{7,6},{8,9},{9,8},{10,11... | collective-permute-start | bytes 98312 | tf_op jit(solution)/shard_map/ppermute | solution.py:301
  3.9 3.9 %collective-permute-start.2 = (bf16[160,128]{1,0:T(8,128)(2,1)S(1)}, bf16[160,128]{1,0:T(8,128)(2,1)S(1)}, u32[]{:S(2)}, u32[]{:S(2)}) collective-permute-start(bf16[160,128]{1,0:T(8,128)(2,1)S(1)} %pad_maximum_fusion.1.block_ref.refs_0_), channel_id=1, source_target_pairs={{0,6},{1,7},{2,4},{3,5},{4,2},{5,3},{6,0},{7,1},{8,14},{9,15},{10,... | collective-permute-start | bytes 122888 | tf_op jit(solution)/shard_map/ppermute | solution.py:301
  4.7 1.1 %copy-start.5 = (s32[768,3]{0,1:T(4,128)S(1)}, s32[768,3]{0,1:T(4,128)}, u32[]{:S(2)}) copy-start(s32[768,3]{0,1:T(4,128)} %param.15) | copy-start | bytes 27652
  4.7 4.2 %collective-permute-start.1 = (bf16[128,128]{1,0:T(8,128)(2,1)S(1)}, bf16[128,128]{1,0:T(8,128)(2,1)S(1)}, u32[]{:S(2)}, u32[]{:S(2)}) collective-permute-start(bf16[128,128]{1,0:T(8,128)(2,1)S(1)} %shard_map.127), channel_id=1, source_target_pairs={{0,7},{1,6},{2,5},{3,4},{4,3},{5,2},{6,1},{7,0},{8,15},{9,14},{10,... | collective-permute-start | bytes 98312 | tf_op jit(solution)/shard_map/ppermute | solution.py:301
  9.2 2.0 %collective-permute-start.3 = (bf16[448,128]{1,0:T(8,128)(2,1)S(1)}, bf16[448,128]{1,0:T(8,128)(2,1)S(1)}, u32[]{:S(2)}, u32[]{:S(2)}) collective-permute-start(bf16[448,128]{1,0:T(8,128)(2,1)S(1)} %get-tuple-element.30), channel_id=1, source_target_pairs={{0,2},{1,3},{2,0},{3,1},{4,6},{5,7},{6,4},{7,5},{8,10},{9,11},{10,... | collective-permute-start | bytes 344072 | tf_op jit(solution)/shard_map/ppermute | solution.py:301
  11.3 4.9 %collective-permute-start.4 = (bf16[416,128]{1,0:T(8,128)(2,1)S(1)}, bf16[416,128]{1,0:T(8,128)(2,1)S(1)}, u32[]{:S(2)}, u32[]{:S(2)}) collective-permute-start(bf16[416,128]{1,0:T(8,128)(2,1)S(1)} %add_convert_fusion), channel_id=1, source_target_pairs={{0,10},{1,11},{2,8},{3,9},{4,14},{5,15},{6,12},{7,13},{8,2},{9,3},... | collective-permute-start | bytes 319496 | tf_op jit(solution)/shard_map/ppermute | solution.py:301
  12.9 7.0 %copy-start.2 = (bf16[128,512]{1,0:T(8,128)(2,1)S(1)}, bf16[128,512]{1,0:T(8,128)(2,1)}, u32[]{:S(2)}) copy-start(bf16[128,512]{1,0:T(8,128)(2,1)} %refs_5_.1) | copy-start | bytes 393220
  12.9 7.0 %copy-start.3 = (bf16[512,128]{1,0:T(8,128)(2,1)S(1)}, bf16[512,128]{1,0:T(8,128)(2,1)}, u32[]{:S(2)}) copy-start(bf16[512,128]{1,0:T(8,128)(2,1)} %refs_6_.1) | copy-start | bytes 393220
  12.9 7.0 %copy-start.4 = (bf16[128,128]{1,0:T(8,128)(2,1)S(1)}, bf16[128,128]{1,0:T(8,128)(2,1)}, u32[]{:S(2)}) copy-start(bf16[128,128]{1,0:T(8,128)(2,1)} %refs_0_.1) | copy-start | bytes 98308
  12.9 7.0 %copy-start.6 = (f32[128,16]{0,1:T(8,128)S(1)}, f32[128,16]{0,1:T(8,128)}, u32[]{:S(2)}) copy-start(f32[128,16]{0,1:T(8,128)} %param.20) | copy-start | bytes 24580
  12.9 7.0 %copy-start.7 = (s32[128,16]{0,1:T(8,128)S(1)}, s32[128,16]{0,1:T(8,128)}, u32[]{:S(2)}) copy-start(s32[128,16]{0,1:T(8,128)} %param.21) | copy-start | bytes 24580
  16.3 6.9 %collective-permute-start.5 = (bf16[416,128]{1,0:T(8,128)(2,1)S(1)}, bf16[416,128]{1,0:T(8,128)(2,1)S(1)}, u32[]{:S(2)}, u32[]{:S(2)}) collective-permute-start(bf16[416,128]{1,0:T(8,128)(2,1)S(1)} %fusion.refs_7_.a_ref), channel_id=1, source_target_pairs={{0,26},{1,27},{2,24},{3,25},{4,30},{5,31},{6,28},{7,29},{8,18},{9,... | collective-permute-start | bytes 319496 | tf_op jit(solution)/shard_map/ppermute | solution.py:301
  19.8 0.7 %copy-start.8 = (f32[128]{0:T(128)S(1)}, f32[128]{0:T(128)}, u32[]{:S(2)}) copy-start(f32[128]{0:T(128)} %param.19) | copy-start | bytes 1540
  19.8 0.7 %copy-start.9 = (f32[128]{0:T(128)S(1)}, f32[128]{0:T(128)}, u32[]{:S(2)}) copy-start(f32[128]{0:T(128)} %param.22) | copy-start | bytes 1540
  20.5 2.6 %copy-start.1 = (bf16[2,128,128]{2,1,0:T(8,128)(2,1)S(1)}, bf16[2,128,128]{2,1,0:T(8,128)(2,1)}, u32[]{:S(2)}) copy-start(bf16[2,128,128]{2,1,0:T(8,128)(2,1)} %mix_ref.1) | copy-start | bytes 196612
  23.5 1.4 %collective-permute-start.6 = (bf16[128,384]{1,0:T(8,128)(2,1)S(1)}, bf16[128,384]{1,0:T(8,128)(2,1)S(1)}, u32[]{:S(2)}, u32[]{:S(2)}) collective-permute-start(bf16[128,384]{1,0:T(8,128)(2,1)S(1)} %shard_map.134.refs_2_), channel_id=1, source_target_pairs={{0,2},{1,3},{2,0},{3,1},{4,6},{5,7},{6,4},{7,5},{8,10},{9,11},{10,... | collective-permute-start | bytes 294920 | tf_op jit(solution)/shard_map/ppermute | solution.py:301
  25.1 4.3 %collective-permute-start.7 = (bf16[128,128]{1,0:T(8,128)(2,1)S(1)}, bf16[128,128]{1,0:T(8,128)(2,1)S(1)}, u32[]{:S(2)}, u32[]{:S(2)}) collective-permute-start(bf16[128,128]{1,0:T(8,128)(2,1)S(1)} %get-tuple-element.45), channel_id=1, source_target_pairs={{0,7},{1,6},{2,5},{3,4},{4,3},{5,2},{6,1},{7,0},{8,15},{9,14},{10,... | collective-permute-start | bytes 98312 | tf_op jit(solution)/shard_map/ppermute | solution.py:301
  25.6 4.0 %collective-permute-start.8 = (bf16[128,128]{1,0:T(8,128)(2,1)S(1)}, bf16[128,128]{1,0:T(8,128)(2,1)S(1)}, u32[]{:S(2)}, u32[]{:S(2)}) collective-permute-start(bf16[128,128]{1,0:T(8,128)(2,1)S(1)} %get-tuple-element.46), channel_id=1, source_target_pairs={{0,1},{1,0},{2,3},{3,2},{4,5},{5,4},{6,7},{7,6},{8,9},{9,8},{10,11... | collective-permute-start | bytes 98312 | tf_op jit(solution)/shard_map/ppermute | solution.py:301
  27.0 3.7 %collective-permute-start.9 = (bf16[128,128]{1,0:T(8,128)(2,1)S(1)}, bf16[128,128]{1,0:T(8,128)(2,1)S(1)}, u32[]{:S(2)}, u32[]{:S(2)}) collective-permute-start(bf16[128,128]{1,0:T(8,128)(2,1)S(1)} %get-tuple-element.47), channel_id=1, source_target_pairs={{0,6},{1,7},{2,4},{3,5},{4,2},{5,3},{6,0},{7,1},{8,14},{9,15},{10,... | collective-permute-start | bytes 98312 | tf_op jit(solution)/shard_map/ppermute | solution.py:301

commit v5 on v4

--- a/solution.py
+++ b/solution.py
@@ -69,16 +69,19 @@
 
 def pack(features, positions, groups, slab_length):
     atoms, channels = features.shape
-    scale = jnp.array([[1.0 / box_side], [1.0 / box_side], [1.0 / slab_length]], f32)
-    turns = positions.T * scale
-    high = lax.reduce_precision(turns, 8, 7)
-    rest = turns - high
-    middle = lax.reduce_precision(rest, 8, 7)
-    parts = [high, middle, rest - middle, jnp.ones((1, groups * atoms), f32)]
-    parts.append(jnp.zeros((coord_rows - 10, groups * atoms), f32))
-    parts = jnp.concatenate(parts, axis=0).astype(bf16)
-    split = [parts[:, i * atoms : (i + 1) * atoms] for i in range(groups)]
-    return jnp.concatenate([features, *split], axis=0)
+    row = lax.broadcasted_iota(jnp.int32, (coord_rows, atoms), 0)
+    scale = jnp.where(row % 3 == 2, 1.0 / slab_length, 1.0 / box_side)
+    rows = [features]
+    for i in range(groups):
+        own = positions[i * atoms : (i + 1) * atoms].T
+        turns = jnp.pad(jnp.concatenate([own, own, own], axis=0), ((0, coord_rows - 9), (0, 0))) * scale
+        high = lax.reduce_precision(turns, 8, 7)
+        rest = turns - high
+        middle = lax.reduce_precision(rest, 8, 7)
+        parts = jnp.where(row < 3, high, jnp.where(row < 6, middle, rest - middle))
+        parts = jnp.where(row < 9, parts, jnp.where(row == 9, 1.0, 0.0))
+        rows.append(parts.astype(bf16))
+    return jnp.concatenate(rows, axis=0)
 
 
 def fill_phases(block_ref, waves, groups, phase_ref):
@@ -236,9 +239,10 @@
         edge = edge_of(ref)
         across = edge if i == 0 else jnp.where((start & ((1 << i) - 1)) == 0, edge, across)
     far = edge_of(core_ref)
-    if stages:
-        ends = (member == 0) | (member == members - 1)
-        far = jnp.where(ends, across, far)
+    ends = (member == 0) | (member == members - 1)
+    if not stages:
+        across = jnp.where(even, near_refs[-1][atoms - halo : atoms, :], near_refs[-1][:halo, :])
+    far = jnp.where(ends, across, far)
     for mask, ref in zip(masks[1:], near_refs[1:]):
         rows = jnp.where(even, ref[atoms - halo : atoms, :], ref[:halo, :])
         far = jnp.where(reaches(member, even, mask), rows, far)
@@ -304,15 +308,14 @@
     for i in range(inner // 2):
         bases.append((2 * i + i.bit_count() % 2) * groups)
     near = [m + i for m in bases for i in range(groups)]
-    farthest = sorted(near[1:], key=lambda m: -(m & ~groups).bit_count())
     block = {0: features}
     packed = pack(features, positions, groups, slab_length)
-    copied = call(
-        features_body, (shape((atoms, channels), bf16),), packed, flops=vector_flops * 300000
-    )
-    for m in near[1:]:
-        source = packed if m % groups == 0 else features if m < groups else copied
+    source = packed
+    for m in sorted(near[1:], key=lambda m: (m % groups != 0, m > groups)):
         block[m] = swap(source, m)
+        source = call(
+            features_body, (shape((atoms, channels), bf16),), source, flops=vector_flops * 300000
+        )
     waves, own_phase = call(
         functools.partial(prepare_body, inner, groups),
         (shape((coord_rows, 2 * columns), bf16), shape((own_rows, 2 * columns), bf16)),
@@ -416,7 +419,7 @@
         flops=work,
     )
     peers = [terms[0]]
-    for m in farthest:
+    for m in sorted(near[1:], key=lambda m: -(m & ~groups).bit_count()):
         peers.append(swap(terms[near.index(m)], m))
 
     near_masks = [m for m in chain if m in near]

time: 31.8 us -> 31.5 us (level)
  starting transfers between devices: 14.3 us -> 13.2 us
  local copies, waits for them, and re-layouts: 0.93 us -> 1.87 us
  other arithmetic: 1.02 us -> 0.37 us
  waiting for transfers between devices: 10.6 us -> 11.1 us
    ppermute x10, starting transfers between devices: 14.3 us -> 13.2 us  [swap(): return lax.ppermute(x, both, [(i, i ^ mask) for i in range(devices)])]
    unnamed x25, local copies, waits for them, and re-layouts: 0.77 us -> 1.86 us
    another operation x1 -> x0, other arithmetic: 0.76 us -> none
    ppermute x10, waiting for transfers between devices: 10.6 us -> 11.1 us  [swap(): return lax.ppermute(x, both, [(i, i ^ mask) for i in range(devices)])]
    pallas_call x11 -> x12, Pallas kernels: 4.52 us -> 4.54 us  [call(): pl.pallas_call(body, out_shape=outs if len(outs) > 1 else outs[0], in_spe...]
  transfers between devices with their start and end apart: 10 -> 10, of which waited for: 9 -> 9; matrix products, arithmetic and copies ran while one was open for 4% -> 1% of each run, Pallas kernels for 8% -> 8%
where the time goes in v5:
time: 31.5 us; the launch traced here: 31.2 us
  starting transfers between devices  13.2 us (42%)
  waiting for transfers between devices  11.1 us (35%)
  Pallas kernels  4.54 us (14%)
  local copies, waits for them, and re-layouts  1.87 us (6%)
  other arithmetic  0.37 us (1%)
    ppermute x10, starting transfers between devices, swap(): return lax.ppermute(x, both, [(i, i ^ mask) for i in range(devices)])  13.2 us
    ppermute x10, waiting for transfers between devices, swap(): return lax.ppermute(x, both, [(i, i ^ mask) for i in range(devices)])  11.1 us
    pallas_call x12, Pallas kernels, call(): pl.pallas_call(body, out_shape=outs if len(outs) > 1 else outs[0], in_spe...  4.54 us
    unnamed x25, local copies, waits for them, and re-layouts  1.86 us
  transfers between devices with their start and end apart: 10, of which 9 were waited for; matrix products, arithmetic and copies ran while one was open for 1% of the time, Pallas kernels for 8%

profile of v5, /device:TPU:0, one launch (start us, length us, event | category | flops | bytes accessed | tf_op | source)
XLA Modules:
  0.0 31.2 jit_solution(6311837260612574878)
XLA Ops:
  0.1 0.7 %copy-done.11 = f32[256,3]{0,1:T(4,128)S(1)} copy-done((f32[256,3]{0,1:T(4,128)S(1)}, f32[256,3]{0,1:T(4,128)}, u32[]{:S(2)}) %copy-start.11) | copy-done | bytes 3096
  0.9 2.5 %collective-permute-start.2 = (bf16[160,128]{1,0:T(8,128)(2,1)S(1)}, bf16[160,128]{1,0:T(8,128)(2,1)S(1)}, u32[]{:S(2)}, u32[]{:S(2)}) collective-permute-start(bf16[160,128]{1,0:T(8,128)(2,1)S(1)} %pad_maximum_fusion.1.block_ref.refs_0_), channel_id=1, source_target_pairs={{0,6},{1,7},{2,4},{3,5},{4,2},{5,3},{6,0},{7,1},{8,14},{9,15},{10,... | collective-permute-start | bytes 122888 | tf_op jit(solution)/shard_map/ppermute | solution.py:305
  3.3 1.5 %collective-permute-start = (bf16[128,128]{1,0:T(8,128)(2,1)S(1)}, bf16[128,128]{1,0:T(8,128)(2,1)S(1)}, u32[]{:S(2)}, u32[]{:S(2)}) collective-permute-start(bf16[128,128]{1,0:T(8,128)(2,1)S(1)} %shard_map.118.block_ref), channel_id=1, source_target_pairs={{0,1},{1,0},{2,3},{3,2},{4,5},{5,4},{6,7},{7,6},{8,9},{9,8},{10,11... | collective-permute-start | bytes 98312 | tf_op jit(solution)/shard_map/ppermute | solution.py:305
  4.8 0.3 collective-permute-start.1
  5.1 0.4 %copy-done.5 = s32[768,3]{0,1:T(4,128)S(1)} copy-done((s32[768,3]{0,1:T(4,128)S(1)}, s32[768,3]{0,1:T(4,128)}, u32[]{:S(2)}) %copy-start.5) | copy-done | bytes 9240
  5.5 0.7 %shard_map.120 = (bf16[16,768]{1,0:T(8,128)(2,1)S(1)}, bf16[256,768]{1,0:T(8,128)(2,1)S(1)}) custom-call(s32[3,768]{1,0:T(4,128)S(1)} %bitcast.10, bf16[160,128]{1,0:T(8,128)(2,1)S(1)} %pad_maximum_fusion.1.block_ref.refs_0_), custom_call_target="tpu_custom_call" | custom-call | flops 2949120000 | bytes 467968 | tf_op jit(solution)/shard_map/pallas_call | solution.py:44
  6.4 0.9 %collective-permute-done.refs_1_.refs_4_ = bf16[128,128]{1,0:T(8,128)(2,1)S(1)} collective-permute-done((bf16[128,128]{1,0:T(8,128)(2,1)S(1)}, bf16[128,128]{1,0:T(8,128)(2,1)S(1)}, u32[]{:S(2)}, u32[]{:S(2)}) %collective-permute-start) | collective-permute-done | bytes 32800 | tf_op jit(solution)/shard_map/ppermute | solution.py:305
  7.3 0.3 shard_map.122.refs_3_
  7.6 0.6 %shard_map.121.refs_2_.refs_1_ = bf16[256,768]{1,0:T(8,128)(2,1)S(1)} custom-call(bf16[160,128]{1,0:T(8,128)(2,1)S(1)} %collective-permute-done.2.block_ref.refs_0_, bf16[16,768]{1,0:T(8,128)(2,1)S(1)} %get-tuple-element.28.wave_ref), custom_call_target="tpu_custom_call" | custom-call | flops 1474560000 | bytes 458752 | tf_op jit(solution)/shard_map/pallas_call | solution.py:44
  8.2 0.9 %collective-permute-done.1.refs_1_.refs_5_.refs_2_ = bf16[128,128]{1,0:T(8,128)(2,1)S(1)} collective-permute-done((bf16[128,128]{1,0:T(8,128)(2,1)S(1)}, bf16[128,128]{1,0:T(8,128)(2,1)S(1)}, u32[]{:S(2)}, u32[]{:S(2)}) %collective-permute-start.1) | collective-permute-done | bytes 32800 | tf_op jit(solution)/shard_map/ppermute | solution.py:305
  9.1 0.3 shard_map.123
  9.4 0.5 %collective-permute-start.3 = (bf16[448,128]{1,0:T(8,128)(2,1)S(1)}, bf16[448,128]{1,0:T(8,128)(2,1)S(1)}, u32[]{:S(2)}, u32[]{:S(2)}) collective-permute-start(bf16[448,128]{1,0:T(8,128)(2,1)S(1)} %get-tuple-element.30), channel_id=1, source_target_pairs={{0,2},{1,3},{2,0},{3,1},{4,6},{5,7},{6,4},{7,5},{8,10},{9,11},{10,... | collective-permute-start | bytes 344072 | tf_op jit(solution)/shard_map/ppermute | solution.py:305
  10.0 0.9 %collective-permute-done.3.refs_3_ = bf16[448,128]{1,0:T(8,128)(2,1)S(1)} collective-permute-done((bf16[448,128]{1,0:T(8,128)(2,1)S(1)}, bf16[448,128]{1,0:T(8,128)(2,1)S(1)}, u32[]{:S(2)}, u32[]{:S(2)}) %collective-permute-start.3) | collective-permute-done | bytes 114720 | tf_op jit(solution)/shard_map/ppermute | solution.py:305
  10.9 1.6 %collective-permute-start.4 = (bf16[416,128]{1,0:T(8,128)(2,1)S(1)}, bf16[416,128]{1,0:T(8,128)(2,1)S(1)}, u32[]{:S(2)}, u32[]{:S(2)}) collective-permute-start(bf16[416,128]{1,0:T(8,128)(2,1)S(1)} %add_convert_fusion), channel_id=1, source_target_pairs={{0,10},{1,11},{2,8},{3,9},{4,14},{5,15},{6,12},{7,13},{8,2},{9,3},... | collective-permute-start | bytes 319496 | tf_op jit(solution)/shard_map/ppermute | solution.py:305
  12.5 3.2 %collective-permute-done.4.refs_4_ = bf16[416,128]{1,0:T(8,128)(2,1)S(1)} collective-permute-done((bf16[416,128]{1,0:T(8,128)(2,1)S(1)}, bf16[416,128]{1,0:T(8,128)(2,1)S(1)}, u32[]{:S(2)}, u32[]{:S(2)}) %collective-permute-start.4) | collective-permute-done | bytes 106528 | tf_op jit(solution)/shard_map/ppermute | solution.py:305
  15.8 0.1 fusion.refs_7_.a_ref
  15.9 3.6 %collective-permute-start.5 = (bf16[416,128]{1,0:T(8,128)(2,1)S(1)}, bf16[416,128]{1,0:T(8,128)(2,1)S(1)}, u32[]{:S(2)}, u32[]{:S(2)}) collective-permute-start(bf16[416,128]{1,0:T(8,128)(2,1)S(1)} %fusion.refs_7_.a_ref), channel_id=1, source_target_pairs={{0,26},{1,27},{2,24},{3,25},{4,30},{5,31},{6,28},{7,29},{8,18},{9,... | collective-permute-start | bytes 319496 | tf_op jit(solution)/shard_map/ppermute | solution.py:305
  19.5 0.6 %copy-done.8 = f32[128]{0:T(128)S(1)} copy-done((f32[128]{0:T(128)S(1)}, f32[128]{0:T(128)}, u32[]{:S(2)}) %copy-start.8) | copy-done | bytes 536
  20.1 2.6 %collective-permute-done.5.refs_5_.b_ref = bf16[416,128]{1,0:T(8,128)(2,1)S(1)} collective-permute-done((bf16[416,128]{1,0:T(8,128)(2,1)S(1)}, bf16[416,128]{1,0:T(8,128)(2,1)S(1)}, u32[]{:S(2)}, u32[]{:S(2)}) %collective-permute-start.5) | collective-permute-done | bytes 106528 | tf_op jit(solution)/shard_map/ppermute | solution.py:305
  22.7 0.3 %shard_map.126.refs_2_ = bf16[128,384]{1,0:T(8,128)(2,1)S(1)} custom-call(bf16[416,128]{1,0:T(8,128)(2,1)S(1)} %fusion.refs_7_.a_ref, bf16[416,128]{1,0:T(8,128)(2,1)S(1)} %collective-permute-done.5.refs_5_.b_ref, bf16[2,128,128]{2,1,0:T(8,128)(2,1)S(1)} %copy-done.1, f32[128,384]{1,0:T(8,128)S(1)} %pad_maximum_fusion.filter_ref), custom_call_target="tpu_custom_call" | custom-call | flops 25165824 | bytes 573440 | tf_op jit(solution)/shard_map/pallas_call | solution.py:44
  23.1 0.3 collective-permute-start.6
  23.3 0.3 shard_map.127.refs_3_
  23.6 0.8 %collective-permute-done.6.refs_2_ = bf16[128,384]{1,0:T(8,128)(2,1)S(1)} collective-permute-done((bf16[128,384]{1,0:T(8,128)(2,1)S(1)}, bf16[128,384]{1,0:T(8,128)(2,1)S(1)}, u32[]{:S(2)}, u32[]{:S(2)}) %collective-permute-start.6) | collective-permute-done | bytes 98336 | tf_op jit(solution)/shard_map/ppermute | solution.py:305
  24.4 0.3 shard_map.128
  24.7 1.0 %collective-permute-start.7 = (bf16[128,128]{1,0:T(8,128)(2,1)S(1)}, bf16[128,128]{1,0:T(8,128)(2,1)S(1)}, u32[]{:S(2)}, u32[]{:S(2)}) collective-permute-start(bf16[128,128]{1,0:T(8,128)(2,1)S(1)} %get-tuple-element.45), channel_id=1, source_target_pairs={{0,7},{1,6},{2,5},{3,4},{4,3},{5,2},{6,1},{7,0},{8,15},{9,14},{10,... | collective-permute-start | bytes 98312 | tf_op jit(solution)/shard_map/ppermute | solution.py:305
  25.7 1.1 %collective-permute-start.8 = (bf16[128,128]{1,0:T(8,128)(2,1)S(1)}, bf16[128,128]{1,0:T(8,128)(2,1)S(1)}, u32[]{:S(2)}, u32[]{:S(2)}) collective-permute-start(bf16[128,128]{1,0:T(8,128)(2,1)S(1)} %get-tuple-element.46), channel_id=1, source_target_pairs={{0,1},{1,0},{2,3},{3,2},{4,5},{5,4},{6,7},{7,6},{8,9},{9,8},{10,11... | collective-permute-start | bytes 98312 | tf_op jit(solution)/shard_map/ppermute | solution.py:305
  26.8 0.9 %collective-permute-start.9 = (bf16[128,128]{1,0:T(8,128)(2,1)S(1)}, bf16[128,128]{1,0:T(8,128)(2,1)S(1)}, u32[]{:S(2)}, u32[]{:S(2)}) collective-permute-start(bf16[128,128]{1,0:T(8,128)(2,1)S(1)} %get-tuple-element.47), channel_id=1, source_target_pairs={{0,6},{1,7},{2,4},{3,5},{4,2},{5,3},{6,0},{7,1},{8,14},{9,15},{10,... | collective-permute-start | bytes 98312 | tf_op jit(solution)/shard_map/ppermute | solution.py:305
  27.7 0.7 %shard_map.125.refs_0_ = f32[128,128]{1,0:T(8,128)S(1)} custom-call(bf16[160,128]{1,0:T(8,128)(2,1)S(1)} %pad_maximum_fusion.1.block_ref.refs_0_, bf16[128,128]{1,0:T(8,128)(2,1)S(1)} %collective-permute-done.refs_1_.refs_4_, bf16[128,128]{1,0:T(8,128)(2,1)S(1)} %collective-permute-done.1.refs_1_.refs_5_.refs_2_, ...), custom_call_target="tpu_custom_call" | custom-call | flops 100663296 | bytes 549376 | tf_op jit(solution)/shard_map/pallas_call | solution.py:44
  28.4 0.6 %collective-permute-done.7.refs_2_ = bf16[128,128]{1,0:T(8,128)(2,1)S(1)} collective-permute-done((bf16[128,128]{1,0:T(8,128)(2,1)S(1)}, bf16[128,128]{1,0:T(8,128)(2,1)S(1)}, u32[]{:S(2)}, u32[]{:S(2)}) %collective-permute-start.7) | collective-permute-done | bytes 32800 | tf_op jit(solution)/shard_map/ppermute | solution.py:305
  29.0 0.6 %collective-permute-done.8.refs_3_ = bf16[128,128]{1,0:T(8,128)(2,1)S(1)} collective-permute-done((bf16[128,128]{1,0:T(8,128)(2,1)S(1)}, bf16[128,128]{1,0:T(8,128)(2,1)S(1)}, u32[]{:S(2)}, u32[]{:S(2)}) %collective-permute-start.8) | collective-permute-done | bytes 32800 | tf_op jit(solution)/shard_map/ppermute | solution.py:305
  29.6 0.6 %collective-permute-done.9.refs_4_ = bf16[128,128]{1,0:T(8,128)(2,1)S(1)} collective-permute-done((bf16[128,128]{1,0:T(8,128)(2,1)S(1)}, bf16[128,128]{1,0:T(8,128)(2,1)S(1)}, u32[]{:S(2)}, u32[]{:S(2)}) %collective-permute-start.9) | collective-permute-done | bytes 32800 | tf_op jit(solution)/shard_map/ppermute | solution.py:305
  30.2 1.0 %shard_map.129 = bf16[128,128]{1,0:T(8,128)(2,1)} custom-call(f32[128,128]{1,0:T(8,128)S(1)} %shard_map.125.refs_0_, f32[128,128]{1,0:T(8,128)S(1)} %get-tuple-element.44.refs_1_, bf16[128,128]{1,0:T(8,128)(2,1)S(1)} %collective-permute-done.7.refs_2_, bf16[128,128]{1,0:T(8,128)(2,1)S(1)} %collective-permute-done.8.refs_3_, ...), custom_call_target="tpu_custom_call" | custom-call | flops 33554432 | bytes 524800 | tf_op jit(solution)/shard_map/pallas_call | solution.py:44
  (37 shorter events, 0.4 us)
Async XLA Ops:
  0.0 6.3 %copy-start = (f32[768,128]{1,0:T(8,128)S(1)}, f32[768,128]{1,0:T(8,128)}, u32[]{:S(2)}) copy-start(f32[768,128]{1,0:T(8,128)} %param.15) | copy-start | bytes 1179652
  0.0 0.7 %copy-start.11 = (f32[256,3]{0,1:T(4,128)S(1)}, f32[256,3]{0,1:T(4,128)}, u32[]{:S(2)}) copy-start(f32[256,3]{0,1:T(4,128)} %param.13) | copy-start | bytes 9220
  0.0 0.8 %copy-start.10 = (bf16[128,128]{1,0:T(8,128)(2,1)S(1)}, bf16[128,128]{1,0:T(8,128)(2,1)}, u32[]{:S(2)}) copy-start(bf16[128,128]{1,0:T(8,128)(2,1)} %param.12) | copy-start | bytes 98308
  0.9 6.7 %collective-permute-start.2 = (bf16[160,128]{1,0:T(8,128)(2,1)S(1)}, bf16[160,128]{1,0:T(8,128)(2,1)S(1)}, u32[]{:S(2)}, u32[]{:S(2)}) collective-permute-start(bf16[160,128]{1,0:T(8,128)(2,1)S(1)} %pad_maximum_fusion.1.block_ref.refs_0_), channel_id=1, source_target_pairs={{0,6},{1,7},{2,4},{3,5},{4,2},{5,3},{6,0},{7,1},{8,14},{9,15},{10,... | collective-permute-start | bytes 122888 | tf_op jit(solution)/shard_map/ppermute | solution.py:305
  3.3 4.0 %collective-permute-start = (bf16[128,128]{1,0:T(8,128)(2,1)S(1)}, bf16[128,128]{1,0:T(8,128)(2,1)S(1)}, u32[]{:S(2)}, u32[]{:S(2)}) collective-permute-start(bf16[128,128]{1,0:T(8,128)(2,1)S(1)} %shard_map.118.block_ref), channel_id=1, source_target_pairs={{0,1},{1,0},{2,3},{3,2},{4,5},{5,4},{6,7},{7,6},{8,9},{9,8},{10,11... | collective-permute-start | bytes 98312 | tf_op jit(solution)/shard_map/ppermute | solution.py:305
  4.8 0.7 %copy-start.5 = (s32[768,3]{0,1:T(4,128)S(1)}, s32[768,3]{0,1:T(4,128)}, u32[]{:S(2)}) copy-start(s32[768,3]{0,1:T(4,128)} %param.14) | copy-start | bytes 27652
  4.8 4.2 %collective-permute-start.1 = (bf16[128,128]{1,0:T(8,128)(2,1)S(1)}, bf16[128,128]{1,0:T(8,128)(2,1)S(1)}, u32[]{:S(2)}, u32[]{:S(2)}) collective-permute-start(bf16[128,128]{1,0:T(8,128)(2,1)S(1)} %shard_map.119), channel_id=1, source_target_pairs={{0,7},{1,6},{2,5},{3,4},{4,3},{5,2},{6,1},{7,0},{8,15},{9,14},{10,... | collective-permute-start | bytes 98312 | tf_op jit(solution)/shard_map/ppermute | solution.py:305
  9.4 1.5 %collective-permute-start.3 = (bf16[448,128]{1,0:T(8,128)(2,1)S(1)}, bf16[448,128]{1,0:T(8,128)(2,1)S(1)}, u32[]{:S(2)}, u32[]{:S(2)}) collective-permute-start(bf16[448,128]{1,0:T(8,128)(2,1)S(1)} %get-tuple-element.30), channel_id=1, source_target_pairs={{0,2},{1,3},{2,0},{3,1},{4,6},{5,7},{6,4},{7,5},{8,10},{9,11},{10,... | collective-permute-start | bytes 344072 | tf_op jit(solution)/shard_map/ppermute | solution.py:305
  10.9 4.9 %collective-permute-start.4 = (bf16[416,128]{1,0:T(8,128)(2,1)S(1)}, bf16[416,128]{1,0:T(8,128)(2,1)S(1)}, u32[]{:S(2)}, u32[]{:S(2)}) collective-permute-start(bf16[416,128]{1,0:T(8,128)(2,1)S(1)} %add_convert_fusion), channel_id=1, source_target_pairs={{0,10},{1,11},{2,8},{3,9},{4,14},{5,15},{6,12},{7,13},{8,2},{9,3},... | collective-permute-start | bytes 319496 | tf_op jit(solution)/shard_map/ppermute | solution.py:305
  12.5 7.0 %copy-start.2 = (bf16[128,512]{1,0:T(8,128)(2,1)S(1)}, bf16[128,512]{1,0:T(8,128)(2,1)}, u32[]{:S(2)}) copy-start(bf16[128,512]{1,0:T(8,128)(2,1)} %refs_5_.1) | copy-start | bytes 393220
  12.5 7.0 %copy-start.3 = (bf16[512,128]{1,0:T(8,128)(2,1)S(1)}, bf16[512,128]{1,0:T(8,128)(2,1)}, u32[]{:S(2)}) copy-start(bf16[512,128]{1,0:T(8,128)(2,1)} %refs_6_.1) | copy-start | bytes 393220
  12.5 7.0 %copy-start.4 = (bf16[128,128]{1,0:T(8,128)(2,1)S(1)}, bf16[128,128]{1,0:T(8,128)(2,1)}, u32[]{:S(2)}) copy-start(bf16[128,128]{1,0:T(8,128)(2,1)} %refs_0_.1) | copy-start | bytes 98308
  12.5 7.0 %copy-start.6 = (f32[128,16]{0,1:T(8,128)S(1)}, f32[128,16]{0,1:T(8,128)}, u32[]{:S(2)}) copy-start(f32[128,16]{0,1:T(8,128)} %param.19) | copy-start | bytes 24580
  12.5 7.0 %copy-start.7 = (s32[128,16]{0,1:T(8,128)S(1)}, s32[128,16]{0,1:T(8,128)}, u32[]{:S(2)}) copy-start(s32[128,16]{0,1:T(8,128)} %param.20) | copy-start | bytes 24580
  15.9 6.9 %collective-permute-start.5 = (bf16[416,128]{1,0:T(8,128)(2,1)S(1)}, bf16[416,128]{1,0:T(8,128)(2,1)S(1)}, u32[]{:S(2)}, u32[]{:S(2)}) collective-permute-start(bf16[416,128]{1,0:T(8,128)(2,1)S(1)} %fusion.refs_7_.a_ref), channel_id=1, source_target_pairs={{0,26},{1,27},{2,24},{3,25},{4,30},{5,31},{6,28},{7,29},{8,18},{9,... | collective-permute-start | bytes 319496 | tf_op jit(solution)/shard_map/ppermute | solution.py:305
  19.4 0.7 %copy-start.8 = (f32[128]{0:T(128)S(1)}, f32[128]{0:T(128)}, u32[]{:S(2)}) copy-start(f32[128]{0:T(128)} %param.18) | copy-start | bytes 1540
  19.4 0.7 %copy-start.9 = (f32[128]{0:T(128)S(1)}, f32[128]{0:T(128)}, u32[]{:S(2)}) copy-start(f32[128]{0:T(128)} %param.21) | copy-start | bytes 1540
  20.1 2.6 %copy-start.1 = (bf16[2,128,128]{2,1,0:T(8,128)(2,1)S(1)}, bf16[2,128,128]{2,1,0:T(8,128)(2,1)}, u32[]{:S(2)}) copy-start(bf16[2,128,128]{2,1,0:T(8,128)(2,1)} %mix_ref.1) | copy-start | bytes 196612
  23.1 1.4 %collective-permute-start.6 = (bf16[128,384]{1,0:T(8,128)(2,1)S(1)}, bf16[128,384]{1,0:T(8,128)(2,1)S(1)}, u32[]{:S(2)}, u32[]{:S(2)}) collective-permute-start(bf16[128,384]{1,0:T(8,128)(2,1)S(1)} %shard_map.126.refs_2_), channel_id=1, source_target_pairs={{0,2},{1,3},{2,0},{3,1},{4,6},{5,7},{6,4},{7,5},{8,10},{9,11},{10,... | collective-permute-start | bytes 294920 | tf_op jit(solution)/shard_map/ppermute | solution.py:305
  24.7 4.3 %collective-permute-start.7 = (bf16[128,128]{1,0:T(8,128)(2,1)S(1)}, bf16[128,128]{1,0:T(8,128)(2,1)S(1)}, u32[]{:S(2)}, u32[]{:S(2)}) collective-permute-start(bf16[128,128]{1,0:T(8,128)(2,1)S(1)} %get-tuple-element.45), channel_id=1, source_target_pairs={{0,7},{1,6},{2,5},{3,4},{4,3},{5,2},{6,1},{7,0},{8,15},{9,14},{10,... | collective-permute-start | bytes 98312 | tf_op jit(solution)/shard_map/ppermute | solution.py:305
  25.7 3.9 %collective-permute-start.8 = (bf16[128,128]{1,0:T(8,128)(2,1)S(1)}, bf16[128,128]{1,0:T(8,128)(2,1)S(1)}, u32[]{:S(2)}, u32[]{:S(2)}) collective-permute-start(bf16[128,128]{1,0:T(8,128)(2,1)S(1)} %get-tuple-element.46), channel_id=1, source_target_pairs={{0,1},{1,0},{2,3},{3,2},{4,5},{5,4},{6,7},{7,6},{8,9},{9,8},{10,11... | collective-permute-start | bytes 98312 | tf_op jit(solution)/shard_map/ppermute | solution.py:305
  26.8 3.4 %collective-permute-start.9 = (bf16[128,128]{1,0:T(8,128)(2,1)S(1)}, bf16[128,128]{1,0:T(8,128)(2,1)S(1)}, u32[]{:S(2)}, u32[]{:S(2)}) collective-permute-start(bf16[128,128]{1,0:T(8,128)(2,1)S(1)} %get-tuple-element.47), channel_id=1, source_target_pairs={{0,6},{1,7},{2,4},{3,5},{4,2},{5,3},{6,0},{7,1},{8,14},{9,15},{10,... | collective-permute-start | bytes 98312 | tf_op jit(solution)/shard_map/ppermute | solution.py:305

commit v6 on v5

--- a/solution.py
+++ b/solution.py
@@ -126,18 +126,18 @@
     out_ref[...] = block_ref[: out_ref.shape[0], :]
 
 
-def add_blocks(block_refs, phase_ref, total):
-    atoms = phase_ref.shape[0] // len(block_refs)
-    for i, ref in enumerate(block_refs):
+def add_blocks(block_refs, phase_ref, first, atoms, total):
+    for i, ref in enumerate(block_refs, first):
         phase = phase_ref[i * atoms : (i + 1) * atoms, :]
         term = dot(ref[:atoms, :], phase, ((0,), (0,)))
         total = term if total is None else total + term
     return total
 
 
-def structure_body(*refs):
-    *block_refs, phase_ref, sum_ref = refs
-    sum_ref[...] = add_blocks(block_refs, phase_ref, None)
+def structure_body(blocks, atoms, *refs):
+    block_refs, (phase_ref, *carry_refs, sum_ref) = refs[:blocks], refs[blocks:]
+    total = carry_refs[0][...] if carry_refs else None
+    sum_ref[...] = add_blocks(block_refs, phase_ref, 0, atoms, total)
 
 
 def stack(ref, total):
@@ -147,14 +147,12 @@
         ref[i * channels : (i + 1) * channels, :] = part.astype(ref.dtype)
 
 
-def split_body(blocks, members, groups, masks, *refs):
-    block_refs, refs = refs[:blocks], refs[blocks:]
-    phase_ref, carry_ref, *far_refs, end_ref, keep_ref, send_ref = refs
-    total = add_blocks(block_refs, phase_ref, carry_ref[...])
+def split_body(atoms, members, groups, masks, *refs):
+    block_ref, phase_ref, carry_ref, *far_refs, end_ref, keep_ref, send_ref = refs
+    total = add_blocks([block_ref], phase_ref, groups - 1, atoms, carry_ref[...])
     columns = total.shape[1] // 2
     stack(keep_ref, total[:, :columns])
     stack(send_ref, total[:, columns:])
-    atoms = phase_ref.shape[0] // blocks
     halo = atoms // 4
     sums = keep_ref.shape[0] - halo
     other = layer_member(members) ^ groups
@@ -336,23 +334,25 @@
         )
 
     work = 4 * own_rows * columns * channels
+    phase = lax.optimization_barrier(phase)
     part = None
-    for m, rows in zip(bases[:-1], phase[:-1]):
-        here = call(
-            structure_body,
+    for m, rows in zip(bases, phase):
+        members_here = [m + i for i in range(groups) if m + i != near[-1]]
+        part = call(
+            functools.partial(structure_body, len(members_here), atoms),
             (shape((channels, 2 * columns), f32),),
-            *[block[m + i] if m + i else packed for i in range(groups)],
+            *[block[i] if i else packed for i in members_here],
             rows,
+            *([] if part is None else [part]),
             flops=work,
         )
-        part = here if part is None else part + here
     chain = [(2 << i) - 1 for i in range(members.bit_length() - 1)]
     far_masks = [m for m in reversed(chain) if m not in near]
     height = columns + atoms // 4
     keep, send = call(
-        functools.partial(split_body, groups, members, groups, far_masks),
+        functools.partial(split_body, atoms, members, groups, far_masks),
         (shape((height, channels), f32), shape((height + atoms // 4, channels), bf16)),
-        *[block[bases[-1] + i] for i in range(groups)],
+        block[near[-1]],
         phase[-1],
         part,
         *[block[m ^ groups] for m in far_masks],
@@ -434,7 +434,7 @@
         chan_width,
         pair_dist,
         neighbours,
-        flops=3 * channels * atoms * neighbours.shape[0] * atoms,
+        flops=vector_flops * atoms * neighbours.shape[0] * channels // 2,
         transcendentals=atoms * neighbours.shape[0] * channels,
     )
     return call(

time: 31.5 us -> 31.4 us (level)
    pallas_call x12 -> x13, Pallas kernels: 4.54 us -> 4.72 us  [call(): pl.pallas_call(body, out_shape=outs if len(outs) > 1 else outs[0], in_spe...]
  transfers between devices with their start and end apart: 10 -> 10, of which waited for: 9 -> 9; matrix products, arithmetic and copies ran while one was open for 1% -> 1% of each run, Pallas kernels for 8% -> 9%
where the time goes in v6:
time: 31.4 us; the launch traced here: 31.2 us
  starting transfers between devices  13.2 us (42%)
  waiting for transfers between devices  10.8 us (34%)
  Pallas kernels  4.72 us (15%)
  local copies, waits for them, and re-layouts  1.87 us (6%)
  other arithmetic  0.36 us (1%)
    ppermute x10, starting transfers between devices, swap(): return lax.ppermute(x, both, [(i, i ^ mask) for i in range(devices)])  13.2 us
    ppermute x10, waiting for transfers between devices, swap(): return lax.ppermute(x, both, [(i, i ^ mask) for i in range(devices)])  10.8 us
    pallas_call x13, Pallas kernels, call(): pl.pallas_call(body, out_shape=outs if len(outs) > 1 else outs[0], in_spe...  4.72 us
    unnamed x25, local copies, waits for them, and re-layouts  1.86 us
  transfers between devices with their start and end apart: 10, of which 9 were waited for; matrix products, arithmetic and copies ran while one was open for 1% of the time, Pallas kernels for 9%

profile of v6, /device:TPU:0, one launch (start us, length us, event | category | flops | bytes accessed | tf_op | source)
XLA Modules:
  0.0 31.2 jit_solution(7898978345193184631)
XLA Ops:
  0.1 0.7 %copy-done.11 = f32[256,3]{0,1:T(4,128)S(1)} copy-done((f32[256,3]{0,1:T(4,128)S(1)}, f32[256,3]{0,1:T(4,128)}, u32[]{:S(2)}) %copy-start.11) | copy-done | bytes 3096
  0.9 2.5 %collective-permute-start.2 = (bf16[160,128]{1,0:T(8,128)(2,1)S(1)}, bf16[160,128]{1,0:T(8,128)(2,1)S(1)}, u32[]{:S(2)}, u32[]{:S(2)}) collective-permute-start(bf16[160,128]{1,0:T(8,128)(2,1)S(1)} %pad_maximum_fusion.1.block_ref.refs_0_), channel_id=1, source_target_pairs={{0,6},{1,7},{2,4},{3,5},{4,2},{5,3},{6,0},{7,1},{8,14},{9,15},{10,... | collective-permute-start | bytes 122888 | tf_op jit(solution)/shard_map/ppermute | solution.py:303
  3.3 1.5 %collective-permute-start = (bf16[128,128]{1,0:T(8,128)(2,1)S(1)}, bf16[128,128]{1,0:T(8,128)(2,1)S(1)}, u32[]{:S(2)}, u32[]{:S(2)}) collective-permute-start(bf16[128,128]{1,0:T(8,128)(2,1)S(1)} %shard_map.118.block_ref), channel_id=1, source_target_pairs={{0,1},{1,0},{2,3},{3,2},{4,5},{5,4},{6,7},{7,6},{8,9},{9,8},{10,11... | collective-permute-start | bytes 98312 | tf_op jit(solution)/shard_map/ppermute | solution.py:303
  4.8 0.3 collective-permute-start.1
  5.1 0.4 %copy-done.5 = s32[768,3]{0,1:T(4,128)S(1)} copy-done((s32[768,3]{0,1:T(4,128)S(1)}, s32[768,3]{0,1:T(4,128)}, u32[]{:S(2)}) %copy-start.5) | copy-done | bytes 9240
  5.5 0.7 %shard_map.120 = (bf16[16,768]{1,0:T(8,128)(2,1)S(1)}, bf16[256,768]{1,0:T(8,128)(2,1)S(1)}) custom-call(s32[3,768]{1,0:T(4,128)S(1)} %bitcast.10, bf16[160,128]{1,0:T(8,128)(2,1)S(1)} %pad_maximum_fusion.1.block_ref.refs_0_), custom_call_target="tpu_custom_call" | custom-call | flops 2949120000 | bytes 467968 | tf_op jit(solution)/shard_map/pallas_call | solution.py:44
  6.4 0.6 %shard_map.121.refs_1_ = bf16[256,768]{1,0:T(8,128)(2,1)S(1)} custom-call(bf16[160,128]{1,0:T(8,128)(2,1)S(1)} %collective-permute-done.2.block_ref.refs_0_, bf16[16,768]{1,0:T(8,128)(2,1)S(1)} %get-tuple-element.31.wave_ref), custom_call_target="tpu_custom_call" | custom-call | flops 1474560000 | bytes 458752 | tf_op jit(solution)/shard_map/pallas_call | solution.py:44
  7.0 0.3 collective-permute-done.refs_1_.refs_3_
  7.3 0.3 shard_map.122.refs_2_
  7.6 0.2 shard_map.123.refs_2_
  7.8 1.2 %collective-permute-done.1.refs_0_.refs_4_.refs_2_ = bf16[128,128]{1,0:T(8,128)(2,1)S(1)} collective-permute-done((bf16[128,128]{1,0:T(8,128)(2,1)S(1)}, bf16[128,128]{1,0:T(8,128)(2,1)S(1)}, u32[]{:S(2)}, u32[]{:S(2)}) %collective-permute-start.1) | collective-permute-done | bytes 32800 | tf_op jit(solution)/shard_map/ppermute | solution.py:303
  9.1 0.2 shard_map.124
  9.3 0.5 %collective-permute-start.3 = (bf16[448,128]{1,0:T(8,128)(2,1)S(1)}, bf16[448,128]{1,0:T(8,128)(2,1)S(1)}, u32[]{:S(2)}, u32[]{:S(2)}) collective-permute-start(bf16[448,128]{1,0:T(8,128)(2,1)S(1)} %get-tuple-element.34), channel_id=1, source_target_pairs={{0,2},{1,3},{2,0},{3,1},{4,6},{5,7},{6,4},{7,5},{8,10},{9,11},{10,... | collective-permute-start | bytes 344072 | tf_op jit(solution)/shard_map/ppermute | solution.py:303
  9.9 0.9 %collective-permute-done.3.refs_3_ = bf16[448,128]{1,0:T(8,128)(2,1)S(1)} collective-permute-done((bf16[448,128]{1,0:T(8,128)(2,1)S(1)}, bf16[448,128]{1,0:T(8,128)(2,1)S(1)}, u32[]{:S(2)}, u32[]{:S(2)}) %collective-permute-start.3) | collective-permute-done | bytes 114720 | tf_op jit(solution)/shard_map/ppermute | solution.py:303
  10.8 1.6 %collective-permute-start.4 = (bf16[416,128]{1,0:T(8,128)(2,1)S(1)}, bf16[416,128]{1,0:T(8,128)(2,1)S(1)}, u32[]{:S(2)}, u32[]{:S(2)}) collective-permute-start(bf16[416,128]{1,0:T(8,128)(2,1)S(1)} %add_convert_fusion), channel_id=1, source_target_pairs={{0,10},{1,11},{2,8},{3,9},{4,14},{5,15},{6,12},{7,13},{8,2},{9,3},... | collective-permute-start | bytes 319496 | tf_op jit(solution)/shard_map/ppermute | solution.py:303
  12.5 3.2 %collective-permute-done.4.refs_4_ = bf16[416,128]{1,0:T(8,128)(2,1)S(1)} collective-permute-done((bf16[416,128]{1,0:T(8,128)(2,1)S(1)}, bf16[416,128]{1,0:T(8,128)(2,1)S(1)}, u32[]{:S(2)}, u32[]{:S(2)}) %collective-permute-start.4) | collective-permute-done | bytes 106528 | tf_op jit(solution)/shard_map/ppermute | solution.py:303
  15.8 3.6 %collective-permute-start.5 = (bf16[416,128]{1,0:T(8,128)(2,1)S(1)}, bf16[416,128]{1,0:T(8,128)(2,1)S(1)}, u32[]{:S(2)}, u32[]{:S(2)}) collective-permute-start(bf16[416,128]{1,0:T(8,128)(2,1)S(1)} %fusion.refs_7_.a_ref), channel_id=1, source_target_pairs={{0,26},{1,27},{2,24},{3,25},{4,30},{5,31},{6,28},{7,29},{8,18},{9,... | collective-permute-start | bytes 319496 | tf_op jit(solution)/shard_map/ppermute | solution.py:303
  19.4 0.6 %copy-done.8 = f32[128]{0:T(128)S(1)} copy-done((f32[128]{0:T(128)S(1)}, f32[128]{0:T(128)}, u32[]{:S(2)}) %copy-start.8) | copy-done | bytes 536
  20.1 2.6 %collective-permute-done.5.refs_5_.b_ref = bf16[416,128]{1,0:T(8,128)(2,1)S(1)} collective-permute-done((bf16[416,128]{1,0:T(8,128)(2,1)S(1)}, bf16[416,128]{1,0:T(8,128)(2,1)S(1)}, u32[]{:S(2)}, u32[]{:S(2)}) %collective-permute-start.5) | collective-permute-done | bytes 106528 | tf_op jit(solution)/shard_map/ppermute | solution.py:303
  22.7 0.3 %shard_map.127.refs_2_ = bf16[128,384]{1,0:T(8,128)(2,1)S(1)} custom-call(bf16[416,128]{1,0:T(8,128)(2,1)S(1)} %fusion.refs_7_.a_ref, bf16[416,128]{1,0:T(8,128)(2,1)S(1)} %collective-permute-done.5.refs_5_.b_ref, bf16[2,128,128]{2,1,0:T(8,128)(2,1)S(1)} %copy-done.1, f32[128,384]{1,0:T(8,128)S(1)} %pad_maximum_fusion.filter_ref), custom_call_target="tpu_custom_call" | custom-call | flops 25165824 | bytes 573440 | tf_op jit(solution)/shard_map/pallas_call | solution.py:44
  23.0 0.3 collective-permute-start.6
  23.3 0.3 shard_map.128.refs_3_
  23.6 0.8 %collective-permute-done.6.refs_2_ = bf16[128,384]{1,0:T(8,128)(2,1)S(1)} collective-permute-done((bf16[128,384]{1,0:T(8,128)(2,1)S(1)}, bf16[128,384]{1,0:T(8,128)(2,1)S(1)}, u32[]{:S(2)}, u32[]{:S(2)}) %collective-permute-start.6) | collective-permute-done | bytes 98336 | tf_op jit(solution)/shard_map/ppermute | solution.py:303
  24.4 0.3 shard_map.129
  24.7 1.0 %collective-permute-start.7 = (bf16[128,128]{1,0:T(8,128)(2,1)S(1)}, bf16[128,128]{1,0:T(8,128)(2,1)S(1)}, u32[]{:S(2)}, u32[]{:S(2)}) collective-permute-start(bf16[128,128]{1,0:T(8,128)(2,1)S(1)} %get-tuple-element.49), channel_id=1, source_target_pairs={{0,7},{1,6},{2,5},{3,4},{4,3},{5,2},{6,1},{7,0},{8,15},{9,14},{10,... | collective-permute-start | bytes 98312 | tf_op jit(solution)/shard_map/ppermute | solution.py:303
  25.7 1.1 %collective-permute-start.8 = (bf16[128,128]{1,0:T(8,128)(2,1)S(1)}, bf16[128,128]{1,0:T(8,128)(2,1)S(1)}, u32[]{:S(2)}, u32[]{:S(2)}) collective-permute-start(bf16[128,128]{1,0:T(8,128)(2,1)S(1)} %get-tuple-element.50), channel_id=1, source_target_pairs={{0,1},{1,0},{2,3},{3,2},{4,5},{5,4},{6,7},{7,6},{8,9},{9,8},{10,11... | collective-permute-start | bytes 98312 | tf_op jit(solution)/shard_map/ppermute | solution.py:303
  26.7 0.9 %collective-permute-start.9 = (bf16[128,128]{1,0:T(8,128)(2,1)S(1)}, bf16[128,128]{1,0:T(8,128)(2,1)S(1)}, u32[]{:S(2)}, u32[]{:S(2)}) collective-permute-start(bf16[128,128]{1,0:T(8,128)(2,1)S(1)} %get-tuple-element.51), channel_id=1, source_target_pairs={{0,6},{1,7},{2,4},{3,5},{4,2},{5,3},{6,0},{7,1},{8,14},{9,15},{10,... | collective-permute-start | bytes 98312 | tf_op jit(solution)/shard_map/ppermute | solution.py:303
  27.7 0.7 %shard_map.126.refs_0_ = f32[128,128]{1,0:T(8,128)S(1)} custom-call(bf16[160,128]{1,0:T(8,128)(2,1)S(1)} %pad_maximum_fusion.1.block_ref.refs_0_, bf16[128,128]{1,0:T(8,128)(2,1)S(1)} %collective-permute-done.refs_1_.refs_3_, bf16[128,128]{1,0:T(8,128)(2,1)S(1)} %collective-permute-done.1.refs_0_.refs_4_.refs_2_, ...), custom_call_target="tpu_custom_call" | custom-call | flops 1966080000 | bytes 549376 | tf_op jit(solution)/shard_map/pallas_call | solution.py:44
  28.4 0.6 %collective-permute-done.7.refs_2_ = bf16[128,128]{1,0:T(8,128)(2,1)S(1)} collective-permute-done((bf16[128,128]{1,0:T(8,128)(2,1)S(1)}, bf16[128,128]{1,0:T(8,128)(2,1)S(1)}, u32[]{:S(2)}, u32[]{:S(2)}) %collective-permute-start.7) | collective-permute-done | bytes 32800 | tf_op jit(solution)/shard_map/ppermute | solution.py:303
  29.0 0.6 %collective-permute-done.8.refs_3_ = bf16[128,128]{1,0:T(8,128)(2,1)S(1)} collective-permute-done((bf16[128,128]{1,0:T(8,128)(2,1)S(1)}, bf16[128,128]{1,0:T(8,128)(2,1)S(1)}, u32[]{:S(2)}, u32[]{:S(2)}) %collective-permute-start.8) | collective-permute-done | bytes 32800 | tf_op jit(solution)/shard_map/ppermute | solution.py:303
  29.6 0.6 %collective-permute-done.9.refs_4_ = bf16[128,128]{1,0:T(8,128)(2,1)S(1)} collective-permute-done((bf16[128,128]{1,0:T(8,128)(2,1)S(1)}, bf16[128,128]{1,0:T(8,128)(2,1)S(1)}, u32[]{:S(2)}, u32[]{:S(2)}) %collective-permute-start.9) | collective-permute-done | bytes 32800 | tf_op jit(solution)/shard_map/ppermute | solution.py:303
  30.2 1.0 %shard_map.130 = bf16[128,128]{1,0:T(8,128)(2,1)} custom-call(f32[128,128]{1,0:T(8,128)S(1)} %shard_map.126.refs_0_, f32[128,128]{1,0:T(8,128)S(1)} %get-tuple-element.48.refs_1_, bf16[128,128]{1,0:T(8,128)(2,1)S(1)} %collective-permute-done.7.refs_2_, bf16[128,128]{1,0:T(8,128)(2,1)S(1)} %collective-permute-done.8.refs_3_, ...), custom_call_target="tpu_custom_call" | custom-call | flops 33554432 | bytes 524800 | tf_op jit(solution)/shard_map/pallas_call | solution.py:44
  (38 shorter events, 0.6 us)
Async XLA Ops:
  0.0 6.3 %copy-start = (f32[768,128]{1,0:T(8,128)S(1)}, f32[768,128]{1,0:T(8,128)}, u32[]{:S(2)}) copy-start(f32[768,128]{1,0:T(8,128)} %param.15) | copy-start | bytes 1179652
  0.0 0.7 %copy-start.11 = (f32[256,3]{0,1:T(4,128)S(1)}, f32[256,3]{0,1:T(4,128)}, u32[]{:S(2)}) copy-start(f32[256,3]{0,1:T(4,128)} %param.13) | copy-start | bytes 9220
  0.0 0.8 %copy-start.10 = (bf16[128,128]{1,0:T(8,128)(2,1)S(1)}, bf16[128,128]{1,0:T(8,128)(2,1)}, u32[]{:S(2)}) copy-start(bf16[128,128]{1,0:T(8,128)(2,1)} %param.12) | copy-start | bytes 98308
  0.9 5.6 %collective-permute-start.2 = (bf16[160,128]{1,0:T(8,128)(2,1)S(1)}, bf16[160,128]{1,0:T(8,128)(2,1)S(1)}, u32[]{:S(2)}, u32[]{:S(2)}) collective-permute-start(bf16[160,128]{1,0:T(8,128)(2,1)S(1)} %pad_maximum_fusion.1.block_ref.refs_0_), channel_id=1, source_target_pairs={{0,6},{1,7},{2,4},{3,5},{4,2},{5,3},{6,0},{7,1},{8,14},{9,15},{10,... | collective-permute-start | bytes 122888 | tf_op jit(solution)/shard_map/ppermute | solution.py:303
  3.3 4.0 %collective-permute-start = (bf16[128,128]{1,0:T(8,128)(2,1)S(1)}, bf16[128,128]{1,0:T(8,128)(2,1)S(1)}, u32[]{:S(2)}, u32[]{:S(2)}) collective-permute-start(bf16[128,128]{1,0:T(8,128)(2,1)S(1)} %shard_map.118.block_ref), channel_id=1, source_target_pairs={{0,1},{1,0},{2,3},{3,2},{4,5},{5,4},{6,7},{7,6},{8,9},{9,8},{10,11... | collective-permute-start | bytes 98312 | tf_op jit(solution)/shard_map/ppermute | solution.py:303
  4.8 0.7 %copy-start.5 = (s32[768,3]{0,1:T(4,128)S(1)}, s32[768,3]{0,1:T(4,128)}, u32[]{:S(2)}) copy-start(s32[768,3]{0,1:T(4,128)} %param.14) | copy-start | bytes 27652
  4.8 4.2 %collective-permute-start.1 = (bf16[128,128]{1,0:T(8,128)(2,1)S(1)}, bf16[128,128]{1,0:T(8,128)(2,1)S(1)}, u32[]{:S(2)}, u32[]{:S(2)}) collective-permute-start(bf16[128,128]{1,0:T(8,128)(2,1)S(1)} %shard_map.119), channel_id=1, source_target_pairs={{0,7},{1,6},{2,5},{3,4},{4,3},{5,2},{6,1},{7,0},{8,15},{9,14},{10,... | collective-permute-start | bytes 98312 | tf_op jit(solution)/shard_map/ppermute | solution.py:303
  9.3 1.5 %collective-permute-start.3 = (bf16[448,128]{1,0:T(8,128)(2,1)S(1)}, bf16[448,128]{1,0:T(8,128)(2,1)S(1)}, u32[]{:S(2)}, u32[]{:S(2)}) collective-permute-start(bf16[448,128]{1,0:T(8,128)(2,1)S(1)} %get-tuple-element.34), channel_id=1, source_target_pairs={{0,2},{1,3},{2,0},{3,1},{4,6},{5,7},{6,4},{7,5},{8,10},{9,11},{10,... | collective-permute-start | bytes 344072 | tf_op jit(solution)/shard_map/ppermute | solution.py:303
  10.8 4.9 %collective-permute-start.4 = (bf16[416,128]{1,0:T(8,128)(2,1)S(1)}, bf16[416,128]{1,0:T(8,128)(2,1)S(1)}, u32[]{:S(2)}, u32[]{:S(2)}) collective-permute-start(bf16[416,128]{1,0:T(8,128)(2,1)S(1)} %add_convert_fusion), channel_id=1, source_target_pairs={{0,10},{1,11},{2,8},{3,9},{4,14},{5,15},{6,12},{7,13},{8,2},{9,3},... | collective-permute-start | bytes 319496 | tf_op jit(solution)/shard_map/ppermute | solution.py:303
  12.4 7.0 %copy-start.2 = (bf16[128,512]{1,0:T(8,128)(2,1)S(1)}, bf16[128,512]{1,0:T(8,128)(2,1)}, u32[]{:S(2)}) copy-start(bf16[128,512]{1,0:T(8,128)(2,1)} %refs_5_.1) | copy-start | bytes 393220
  12.4 7.0 %copy-start.3 = (bf16[512,128]{1,0:T(8,128)(2,1)S(1)}, bf16[512,128]{1,0:T(8,128)(2,1)}, u32[]{:S(2)}) copy-start(bf16[512,128]{1,0:T(8,128)(2,1)} %refs_6_.1) | copy-start | bytes 393220
  12.4 7.0 %copy-start.4 = (bf16[128,128]{1,0:T(8,128)(2,1)S(1)}, bf16[128,128]{1,0:T(8,128)(2,1)}, u32[]{:S(2)}) copy-start(bf16[128,128]{1,0:T(8,128)(2,1)} %refs_0_.1) | copy-start | bytes 98308
  12.4 7.0 %copy-start.6 = (f32[128,16]{0,1:T(8,128)S(1)}, f32[128,16]{0,1:T(8,128)}, u32[]{:S(2)}) copy-start(f32[128,16]{0,1:T(8,128)} %param.19) | copy-start | bytes 24580
  12.4 7.0 %copy-start.7 = (s32[128,16]{0,1:T(8,128)S(1)}, s32[128,16]{0,1:T(8,128)}, u32[]{:S(2)}) copy-start(s32[128,16]{0,1:T(8,128)} %param.20) | copy-start | bytes 24580
  15.8 6.9 %collective-permute-start.5 = (bf16[416,128]{1,0:T(8,128)(2,1)S(1)}, bf16[416,128]{1,0:T(8,128)(2,1)S(1)}, u32[]{:S(2)}, u32[]{:S(2)}) collective-permute-start(bf16[416,128]{1,0:T(8,128)(2,1)S(1)} %fusion.refs_7_.a_ref), channel_id=1, source_target_pairs={{0,26},{1,27},{2,24},{3,25},{4,30},{5,31},{6,28},{7,29},{8,18},{9,... | collective-permute-start | bytes 319496 | tf_op jit(solution)/shard_map/ppermute | solution.py:303
  19.4 0.7 %copy-start.8 = (f32[128]{0:T(128)S(1)}, f32[128]{0:T(128)}, u32[]{:S(2)}) copy-start(f32[128]{0:T(128)} %param.18) | copy-start | bytes 1540
  19.4 0.7 %copy-start.9 = (f32[128]{0:T(128)S(1)}, f32[128]{0:T(128)}, u32[]{:S(2)}) copy-start(f32[128]{0:T(128)} %param.21) | copy-start | bytes 1540
  20.1 2.6 %copy-start.1 = (bf16[2,128,128]{2,1,0:T(8,128)(2,1)S(1)}, bf16[2,128,128]{2,1,0:T(8,128)(2,1)}, u32[]{:S(2)}) copy-start(bf16[2,128,128]{2,1,0:T(8,128)(2,1)} %mix_ref.1) | copy-start | bytes 196612
  23.0 1.4 %collective-permute-start.6 = (bf16[128,384]{1,0:T(8,128)(2,1)S(1)}, bf16[128,384]{1,0:T(8,128)(2,1)S(1)}, u32[]{:S(2)}, u32[]{:S(2)}) collective-permute-start(bf16[128,384]{1,0:T(8,128)(2,1)S(1)} %shard_map.127.refs_2_), channel_id=1, source_target_pairs={{0,2},{1,3},{2,0},{3,1},{4,6},{5,7},{6,4},{7,5},{8,10},{9,11},{10,... | collective-permute-start | bytes 294920 | tf_op jit(solution)/shard_map/ppermute | solution.py:303
  24.7 4.3 %collective-permute-start.7 = (bf16[128,128]{1,0:T(8,128)(2,1)S(1)}, bf16[128,128]{1,0:T(8,128)(2,1)S(1)}, u32[]{:S(2)}, u32[]{:S(2)}) collective-permute-start(bf16[128,128]{1,0:T(8,128)(2,1)S(1)} %get-tuple-element.49), channel_id=1, source_target_pairs={{0,7},{1,6},{2,5},{3,4},{4,3},{5,2},{6,1},{7,0},{8,15},{9,14},{10,... | collective-permute-start | bytes 98312 | tf_op jit(solution)/shard_map/ppermute | solution.py:303
  25.7 3.9 %collective-permute-start.8 = (bf16[128,128]{1,0:T(8,128)(2,1)S(1)}, bf16[128,128]{1,0:T(8,128)(2,1)S(1)}, u32[]{:S(2)}, u32[]{:S(2)}) collective-permute-start(bf16[128,128]{1,0:T(8,128)(2,1)S(1)} %get-tuple-element.50), channel_id=1, source_target_pairs={{0,1},{1,0},{2,3},{3,2},{4,5},{5,4},{6,7},{7,6},{8,9},{9,8},{10,11... | collective-permute-start | bytes 98312 | tf_op jit(solution)/shard_map/ppermute | solution.py:303
  26.7 3.4 %collective-permute-start.9 = (bf16[128,128]{1,0:T(8,128)(2,1)S(1)}, bf16[128,128]{1,0:T(8,128)(2,1)S(1)}, u32[]{:S(2)}, u32[]{:S(2)}) collective-permute-start(bf16[128,128]{1,0:T(8,128)(2,1)S(1)} %get-tuple-element.51), channel_id=1, source_target_pairs={{0,6},{1,7},{2,4},{3,5},{4,2},{5,3},{6,0},{7,1},{8,14},{9,15},{10,... | collective-permute-start | bytes 98312 | tf_op jit(solution)/shard_map/ppermute | solution.py:303

commit v7 on v6

--- a/solution.py
+++ b/solution.py
@@ -368,8 +368,9 @@
         if stages:
             both_sums = amps.astype(f32) + stages[-1].astype(f32)
             amps = jnp.where(sums, both_sums, amps.astype(f32)).astype(bf16)
-        stages.append(swap(amps, ((2 << len(stages)) - 1) * members ^ groups))
+        stages.append(swap(amps, (outer >> len(stages)) * members - members ^ groups))
     other = stages[-1] if stages else jnp.zeros_like(amps)
+    stages = stages[::-1]
     held = (
         msg_weight,
         chan_width.reshape(1, channels),

time: 31.4 us -> 31.6 us (level)
  no operation moved by 1% of the time
where the time goes in v7:
time: 31.6 us; the launch traced here: 31.4 us
  starting transfers between devices  13.5 us (43%)
  waiting for transfers between devices  10.7 us (34%)
  Pallas kernels  4.7 us (15%)
  local copies, waits for them, and re-layouts  1.87 us (6%)
  other arithmetic  0.36 us (1%)
    ppermute x10, starting transfers between devices, swap(): return lax.ppermute(x, both, [(i, i ^ mask) for i in range(devices)])  13.5 us
    ppermute x10, waiting for transfers between devices, swap(): return lax.ppermute(x, both, [(i, i ^ mask) for i in range(devices)])  10.7 us
    pallas_call x13, Pallas kernels, call(): pl.pallas_call(body, out_shape=outs if len(outs) > 1 else outs[0], in_spe...  4.7 us
    unnamed x25, local copies, waits for them, and re-layouts  1.86 us
  transfers between devices with their start and end apart: 10, of which 9 were waited for; matrix products, arithmetic and copies ran while one was open for 1% of the time, Pallas kernels for 9%

profile of v7, /device:TPU:0, one launch (start us, length us, event | category | flops | bytes accessed | tf_op | source)
XLA Modules:
  0.0 31.4 jit_solution(8721709130322290479)
XLA Ops:
  0.1 0.7 %copy-done.11 = f32[256,3]{0,1:T(4,128)S(1)} copy-done((f32[256,3]{0,1:T(4,128)S(1)}, f32[256,3]{0,1:T(4,128)}, u32[]{:S(2)}) %copy-start.11) | copy-done | bytes 3096
  0.9 2.5 %collective-permute-start.2 = (bf16[160,128]{1,0:T(8,128)(2,1)S(1)}, bf16[160,128]{1,0:T(8,128)(2,1)S(1)}, u32[]{:S(2)}, u32[]{:S(2)}) collective-permute-start(bf16[160,128]{1,0:T(8,128)(2,1)S(1)} %pad_maximum_fusion.1.block_ref.refs_0_), channel_id=1, source_target_pairs={{0,6},{1,7},{2,4},{3,5},{4,2},{5,3},{6,0},{7,1},{8,14},{9,15},{10,... | collective-permute-start | bytes 122888 | tf_op jit(solution)/shard_map/ppermute | solution.py:303
  3.3 1.5 %collective-permute-start = (bf16[128,128]{1,0:T(8,128)(2,1)S(1)}, bf16[128,128]{1,0:T(8,128)(2,1)S(1)}, u32[]{:S(2)}, u32[]{:S(2)}) collective-permute-start(bf16[128,128]{1,0:T(8,128)(2,1)S(1)} %shard_map.118.block_ref), channel_id=1, source_target_pairs={{0,1},{1,0},{2,3},{3,2},{4,5},{5,4},{6,7},{7,6},{8,9},{9,8},{10,11... | collective-permute-start | bytes 98312 | tf_op jit(solution)/shard_map/ppermute | solution.py:303
  4.8 0.3 collective-permute-start.1
  5.1 0.4 %copy-done.5 = s32[768,3]{0,1:T(4,128)S(1)} copy-done((s32[768,3]{0,1:T(4,128)S(1)}, s32[768,3]{0,1:T(4,128)}, u32[]{:S(2)}) %copy-start.5) | copy-done | bytes 9240
  5.5 0.7 %shard_map.120 = (bf16[16,768]{1,0:T(8,128)(2,1)S(1)}, bf16[256,768]{1,0:T(8,128)(2,1)S(1)}) custom-call(s32[3,768]{1,0:T(4,128)S(1)} %bitcast.10, bf16[160,128]{1,0:T(8,128)(2,1)S(1)} %pad_maximum_fusion.1.block_ref.refs_0_), custom_call_target="tpu_custom_call" | custom-call | flops 2949120000 | bytes 467968 | tf_op jit(solution)/shard_map/pallas_call | solution.py:44
  6.4 0.6 %shard_map.121.refs_1_ = bf16[256,768]{1,0:T(8,128)(2,1)S(1)} custom-call(bf16[160,128]{1,0:T(8,128)(2,1)S(1)} %collective-permute-done.2.block_ref.refs_0_, bf16[16,768]{1,0:T(8,128)(2,1)S(1)} %get-tuple-element.31.wave_ref), custom_call_target="tpu_custom_call" | custom-call | flops 1474560000 | bytes 458752 | tf_op jit(solution)/shard_map/pallas_call | solution.py:44
  7.0 0.3 collective-permute-done.refs_1_.refs_3_
  7.3 0.3 shard_map.122.refs_2_
  7.6 0.2 shard_map.123.refs_2_
  7.8 1.2 %collective-permute-done.1.refs_0_.refs_4_.refs_2_ = bf16[128,128]{1,0:T(8,128)(2,1)S(1)} collective-permute-done((bf16[128,128]{1,0:T(8,128)(2,1)S(1)}, bf16[128,128]{1,0:T(8,128)(2,1)S(1)}, u32[]{:S(2)}, u32[]{:S(2)}) %collective-permute-start.1) | collective-permute-done | bytes 32800 | tf_op jit(solution)/shard_map/ppermute | solution.py:303
  9.1 0.2 shard_map.124
  9.3 0.5 %collective-permute-start.3 = (bf16[448,128]{1,0:T(8,128)(2,1)S(1)}, bf16[448,128]{1,0:T(8,128)(2,1)S(1)}, u32[]{:S(2)}, u32[]{:S(2)}) collective-permute-start(bf16[448,128]{1,0:T(8,128)(2,1)S(1)} %get-tuple-element.34), channel_id=1, source_target_pairs={{0,2},{1,3},{2,0},{3,1},{4,6},{5,7},{6,4},{7,5},{8,10},{9,11},{10,... | collective-permute-start | bytes 344072 | tf_op jit(solution)/shard_map/ppermute | solution.py:303
  9.9 0.9 %collective-permute-done.3.refs_3_ = bf16[448,128]{1,0:T(8,128)(2,1)S(1)} collective-permute-done((bf16[448,128]{1,0:T(8,128)(2,1)S(1)}, bf16[448,128]{1,0:T(8,128)(2,1)S(1)}, u32[]{:S(2)}, u32[]{:S(2)}) %collective-permute-start.3) | collective-permute-done | bytes 114720 | tf_op jit(solution)/shard_map/ppermute | solution.py:303
  10.8 3.6 %collective-permute-start.4 = (bf16[416,128]{1,0:T(8,128)(2,1)S(1)}, bf16[416,128]{1,0:T(8,128)(2,1)S(1)}, u32[]{:S(2)}, u32[]{:S(2)}) collective-permute-start(bf16[416,128]{1,0:T(8,128)(2,1)S(1)} %add_convert_fusion), channel_id=1, source_target_pairs={{0,26},{1,27},{2,24},{3,25},{4,30},{5,31},{6,28},{7,29},{8,18},{9,... | collective-permute-start | bytes 319496 | tf_op jit(solution)/shard_map/ppermute | solution.py:303
  14.5 3.1 %collective-permute-done.4.refs_5_ = bf16[416,128]{1,0:T(8,128)(2,1)S(1)} collective-permute-done((bf16[416,128]{1,0:T(8,128)(2,1)S(1)}, bf16[416,128]{1,0:T(8,128)(2,1)S(1)}, u32[]{:S(2)}, u32[]{:S(2)}) %collective-permute-start.4) | collective-permute-done | bytes 106528 | tf_op jit(solution)/shard_map/ppermute | solution.py:303
  17.8 1.9 %collective-permute-start.5 = (bf16[416,128]{1,0:T(8,128)(2,1)S(1)}, bf16[416,128]{1,0:T(8,128)(2,1)S(1)}, u32[]{:S(2)}, u32[]{:S(2)}) collective-permute-start(bf16[416,128]{1,0:T(8,128)(2,1)S(1)} %fusion.refs_7_.a_ref), channel_id=1, source_target_pairs={{0,10},{1,11},{2,8},{3,9},{4,14},{5,15},{6,12},{7,13},{8,2},{9,3},... | collective-permute-start | bytes 319496 | tf_op jit(solution)/shard_map/ppermute | solution.py:303
  19.7 0.6 %copy-done.8 = f32[128]{0:T(128)S(1)} copy-done((f32[128]{0:T(128)S(1)}, f32[128]{0:T(128)}, u32[]{:S(2)}) %copy-start.8) | copy-done | bytes 536
  20.3 2.5 %collective-permute-done.5.refs_4_.b_ref = bf16[416,128]{1,0:T(8,128)(2,1)S(1)} collective-permute-done((bf16[416,128]{1,0:T(8,128)(2,1)S(1)}, bf16[416,128]{1,0:T(8,128)(2,1)S(1)}, u32[]{:S(2)}, u32[]{:S(2)}) %collective-permute-start.5) | collective-permute-done | bytes 106528 | tf_op jit(solution)/shard_map/ppermute | solution.py:303
  22.8 0.3 %shard_map.127.refs_2_ = bf16[128,384]{1,0:T(8,128)(2,1)S(1)} custom-call(bf16[416,128]{1,0:T(8,128)(2,1)S(1)} %fusion.refs_7_.a_ref, bf16[416,128]{1,0:T(8,128)(2,1)S(1)} %collective-permute-done.5.refs_4_.b_ref, bf16[2,128,128]{2,1,0:T(8,128)(2,1)S(1)} %copy-done.1, f32[128,384]{1,0:T(8,128)S(1)} %pad_maximum_fusion.filter_ref), custom_call_target="tpu_custom_call" | custom-call | flops 25165824 | bytes 573440 | tf_op jit(solution)/shard_map/pallas_call | solution.py:44
  23.2 0.2 collective-permute-start.6
  23.4 0.3 shard_map.128.refs_3_
  23.6 0.9 %collective-permute-done.6.refs_2_ = bf16[128,384]{1,0:T(8,128)(2,1)S(1)} collective-permute-done((bf16[128,384]{1,0:T(8,128)(2,1)S(1)}, bf16[128,384]{1,0:T(8,128)(2,1)S(1)}, u32[]{:S(2)}, u32[]{:S(2)}) %collective-permute-start.6) | collective-permute-done | bytes 98336 | tf_op jit(solution)/shard_map/ppermute | solution.py:303
  24.5 0.3 shard_map.129
  24.8 0.9 %collective-permute-start.7 = (bf16[128,128]{1,0:T(8,128)(2,1)S(1)}, bf16[128,128]{1,0:T(8,128)(2,1)S(1)}, u32[]{:S(2)}, u32[]{:S(2)}) collective-permute-start(bf16[128,128]{1,0:T(8,128)(2,1)S(1)} %get-tuple-element.49), channel_id=1, source_target_pairs={{0,7},{1,6},{2,5},{3,4},{4,3},{5,2},{6,1},{7,0},{8,15},{9,14},{10,... | collective-permute-start | bytes 98312 | tf_op jit(solution)/shard_map/ppermute | solution.py:303
  25.7 1.0 %collective-permute-start.8 = (bf16[128,128]{1,0:T(8,128)(2,1)S(1)}, bf16[128,128]{1,0:T(8,128)(2,1)S(1)}, u32[]{:S(2)}, u32[]{:S(2)}) collective-permute-start(bf16[128,128]{1,0:T(8,128)(2,1)S(1)} %get-tuple-element.50), channel_id=1, source_target_pairs={{0,1},{1,0},{2,3},{3,2},{4,5},{5,4},{6,7},{7,6},{8,9},{9,8},{10,11... | collective-permute-start | bytes 98312 | tf_op jit(solution)/shard_map/ppermute | solution.py:303
  26.7 1.1 %collective-permute-start.9 = (bf16[128,128]{1,0:T(8,128)(2,1)S(1)}, bf16[128,128]{1,0:T(8,128)(2,1)S(1)}, u32[]{:S(2)}, u32[]{:S(2)}) collective-permute-start(bf16[128,128]{1,0:T(8,128)(2,1)S(1)} %get-tuple-element.51), channel_id=1, source_target_pairs={{0,6},{1,7},{2,4},{3,5},{4,2},{5,3},{6,0},{7,1},{8,14},{9,15},{10,... | collective-permute-start | bytes 98312 | tf_op jit(solution)/shard_map/ppermute | solution.py:303
  27.8 0.7 %shard_map.126.refs_0_ = f32[128,128]{1,0:T(8,128)S(1)} custom-call(bf16[160,128]{1,0:T(8,128)(2,1)S(1)} %pad_maximum_fusion.1.block_ref.refs_0_, bf16[128,128]{1,0:T(8,128)(2,1)S(1)} %collective-permute-done.refs_1_.refs_3_, bf16[128,128]{1,0:T(8,128)(2,1)S(1)} %collective-permute-done.1.refs_0_.refs_4_.refs_2_, ...), custom_call_target="tpu_custom_call" | custom-call | flops 1966080000 | bytes 549376 | tf_op jit(solution)/shard_map/pallas_call | solution.py:44
  28.5 0.6 %collective-permute-done.7.refs_2_ = bf16[128,128]{1,0:T(8,128)(2,1)S(1)} collective-permute-done((bf16[128,128]{1,0:T(8,128)(2,1)S(1)}, bf16[128,128]{1,0:T(8,128)(2,1)S(1)}, u32[]{:S(2)}, u32[]{:S(2)}) %collective-permute-start.7) | collective-permute-done | bytes 32800 | tf_op jit(solution)/shard_map/ppermute | solution.py:303
  29.1 0.5 %collective-permute-done.8.refs_3_ = bf16[128,128]{1,0:T(8,128)(2,1)S(1)} collective-permute-done((bf16[128,128]{1,0:T(8,128)(2,1)S(1)}, bf16[128,128]{1,0:T(8,128)(2,1)S(1)}, u32[]{:S(2)}, u32[]{:S(2)}) %collective-permute-start.8) | collective-permute-done | bytes 32800 | tf_op jit(solution)/shard_map/ppermute | solution.py:303
  29.6 0.8 %collective-permute-done.9.refs_4_ = bf16[128,128]{1,0:T(8,128)(2,1)S(1)} collective-permute-done((bf16[128,128]{1,0:T(8,128)(2,1)S(1)}, bf16[128,128]{1,0:T(8,128)(2,1)S(1)}, u32[]{:S(2)}, u32[]{:S(2)}) %collective-permute-start.9) | collective-permute-done | bytes 32800 | tf_op jit(solution)/shard_map/ppermute | solution.py:303
  30.3 1.0 %shard_map.130 = bf16[128,128]{1,0:T(8,128)(2,1)} custom-call(f32[128,128]{1,0:T(8,128)S(1)} %shard_map.126.refs_0_, f32[128,128]{1,0:T(8,128)S(1)} %get-tuple-element.48.refs_1_, bf16[128,128]{1,0:T(8,128)(2,1)S(1)} %collective-permute-done.7.refs_2_, bf16[128,128]{1,0:T(8,128)(2,1)S(1)} %collective-permute-done.8.refs_3_, ...), custom_call_target="tpu_custom_call" | custom-call | flops 33554432 | bytes 524800 | tf_op jit(solution)/shard_map/pallas_call | solution.py:44
  (38 shorter events, 0.6 us)
Async XLA Ops:
  0.0 6.3 %copy-start = (f32[768,128]{1,0:T(8,128)S(1)}, f32[768,128]{1,0:T(8,128)}, u32[]{:S(2)}) copy-start(f32[768,128]{1,0:T(8,128)} %param.15) | copy-start | bytes 1179652
  0.0 0.7 %copy-start.11 = (f32[256,3]{0,1:T(4,128)S(1)}, f32[256,3]{0,1:T(4,128)}, u32[]{:S(2)}) copy-start(f32[256,3]{0,1:T(4,128)} %param.13) | copy-start | bytes 9220
  0.0 0.8 %copy-start.10 = (bf16[128,128]{1,0:T(8,128)(2,1)S(1)}, bf16[128,128]{1,0:T(8,128)(2,1)}, u32[]{:S(2)}) copy-start(bf16[128,128]{1,0:T(8,128)(2,1)} %param.12) | copy-start | bytes 98308
  0.9 5.6 %collective-permute-start.2 = (bf16[160,128]{1,0:T(8,128)(2,1)S(1)}, bf16[160,128]{1,0:T(8,128)(2,1)S(1)}, u32[]{:S(2)}, u32[]{:S(2)}) collective-permute-start(bf16[160,128]{1,0:T(8,128)(2,1)S(1)} %pad_maximum_fusion.1.block_ref.refs_0_), channel_id=1, source_target_pairs={{0,6},{1,7},{2,4},{3,5},{4,2},{5,3},{6,0},{7,1},{8,14},{9,15},{10,... | collective-permute-start | bytes 122888 | tf_op jit(solution)/shard_map/ppermute | solution.py:303
  3.3 4.0 %collective-permute-start = (bf16[128,128]{1,0:T(8,128)(2,1)S(1)}, bf16[128,128]{1,0:T(8,128)(2,1)S(1)}, u32[]{:S(2)}, u32[]{:S(2)}) collective-permute-start(bf16[128,128]{1,0:T(8,128)(2,1)S(1)} %shard_map.118.block_ref), channel_id=1, source_target_pairs={{0,1},{1,0},{2,3},{3,2},{4,5},{5,4},{6,7},{7,6},{8,9},{9,8},{10,11... | collective-permute-start | bytes 98312 | tf_op jit(solution)/shard_map/ppermute | solution.py:303
  4.8 0.7 %copy-start.5 = (s32[768,3]{0,1:T(4,128)S(1)}, s32[768,3]{0,1:T(4,128)}, u32[]{:S(2)}) copy-start(s32[768,3]{0,1:T(4,128)} %param.14) | copy-start | bytes 27652
  4.8 4.2 %collective-permute-start.1 = (bf16[128,128]{1,0:T(8,128)(2,1)S(1)}, bf16[128,128]{1,0:T(8,128)(2,1)S(1)}, u32[]{:S(2)}, u32[]{:S(2)}) collective-permute-start(bf16[128,128]{1,0:T(8,128)(2,1)S(1)} %shard_map.119), channel_id=1, source_target_pairs={{0,7},{1,6},{2,5},{3,4},{4,3},{5,2},{6,1},{7,0},{8,15},{9,14},{10,... | collective-permute-start | bytes 98312 | tf_op jit(solution)/shard_map/ppermute | solution.py:303
  9.3 1.5 %collective-permute-start.3 = (bf16[448,128]{1,0:T(8,128)(2,1)S(1)}, bf16[448,128]{1,0:T(8,128)(2,1)S(1)}, u32[]{:S(2)}, u32[]{:S(2)}) collective-permute-start(bf16[448,128]{1,0:T(8,128)(2,1)S(1)} %get-tuple-element.34), channel_id=1, source_target_pairs={{0,2},{1,3},{2,0},{3,1},{4,6},{5,7},{6,4},{7,5},{8,10},{9,11},{10,... | collective-permute-start | bytes 344072 | tf_op jit(solution)/shard_map/ppermute | solution.py:303
  10.8 6.8 %collective-permute-start.4 = (bf16[416,128]{1,0:T(8,128)(2,1)S(1)}, bf16[416,128]{1,0:T(8,128)(2,1)S(1)}, u32[]{:S(2)}, u32[]{:S(2)}) collective-permute-start(bf16[416,128]{1,0:T(8,128)(2,1)S(1)} %add_convert_fusion), channel_id=1, source_target_pairs={{0,26},{1,27},{2,24},{3,25},{4,30},{5,31},{6,28},{7,29},{8,18},{9,... | collective-permute-start | bytes 319496 | tf_op jit(solution)/shard_map/ppermute | solution.py:303
  14.4 5.2 %copy-start.2 = (bf16[128,512]{1,0:T(8,128)(2,1)S(1)}, bf16[128,512]{1,0:T(8,128)(2,1)}, u32[]{:S(2)}) copy-start(bf16[128,512]{1,0:T(8,128)(2,1)} %refs_5_.1) | copy-start | bytes 393220
  14.4 5.2 %copy-start.3 = (bf16[512,128]{1,0:T(8,128)(2,1)S(1)}, bf16[512,128]{1,0:T(8,128)(2,1)}, u32[]{:S(2)}) copy-start(bf16[512,128]{1,0:T(8,128)(2,1)} %refs_6_.1) | copy-start | bytes 393220
  14.4 5.2 %copy-start.4 = (bf16[128,128]{1,0:T(8,128)(2,1)S(1)}, bf16[128,128]{1,0:T(8,128)(2,1)}, u32[]{:S(2)}) copy-start(bf16[128,128]{1,0:T(8,128)(2,1)} %refs_0_.1) | copy-start | bytes 98308
  14.5 5.2 %copy-start.6 = (f32[128,16]{0,1:T(8,128)S(1)}, f32[128,16]{0,1:T(8,128)}, u32[]{:S(2)}) copy-start(f32[128,16]{0,1:T(8,128)} %param.19) | copy-start | bytes 24580
  14.5 5.2 %copy-start.7 = (s32[128,16]{0,1:T(8,128)S(1)}, s32[128,16]{0,1:T(8,128)}, u32[]{:S(2)}) copy-start(s32[128,16]{0,1:T(8,128)} %param.20) | copy-start | bytes 24580
  17.8 5.1 %collective-permute-start.5 = (bf16[416,128]{1,0:T(8,128)(2,1)S(1)}, bf16[416,128]{1,0:T(8,128)(2,1)S(1)}, u32[]{:S(2)}, u32[]{:S(2)}) collective-permute-start(bf16[416,128]{1,0:T(8,128)(2,1)S(1)} %fusion.refs_7_.a_ref), channel_id=1, source_target_pairs={{0,10},{1,11},{2,8},{3,9},{4,14},{5,15},{6,12},{7,13},{8,2},{9,3},... | collective-permute-start | bytes 319496 | tf_op jit(solution)/shard_map/ppermute | solution.py:303
  19.6 0.7 %copy-start.8 = (f32[128]{0:T(128)S(1)}, f32[128]{0:T(128)}, u32[]{:S(2)}) copy-start(f32[128]{0:T(128)} %param.18) | copy-start | bytes 1540
  19.6 0.7 %copy-start.9 = (f32[128]{0:T(128)S(1)}, f32[128]{0:T(128)}, u32[]{:S(2)}) copy-start(f32[128]{0:T(128)} %param.21) | copy-start | bytes 1540
  20.3 2.5 %copy-start.1 = (bf16[2,128,128]{2,1,0:T(8,128)(2,1)S(1)}, bf16[2,128,128]{2,1,0:T(8,128)(2,1)}, u32[]{:S(2)}) copy-start(bf16[2,128,128]{2,1,0:T(8,128)(2,1)} %mix_ref.1) | copy-start | bytes 196612
  23.2 1.4 %collective-permute-start.6 = (bf16[128,384]{1,0:T(8,128)(2,1)S(1)}, bf16[128,384]{1,0:T(8,128)(2,1)S(1)}, u32[]{:S(2)}, u32[]{:S(2)}) collective-permute-start(bf16[128,384]{1,0:T(8,128)(2,1)S(1)} %shard_map.127.refs_2_), channel_id=1, source_target_pairs={{0,2},{1,3},{2,0},{3,1},{4,6},{5,7},{6,4},{7,5},{8,10},{9,11},{10,... | collective-permute-start | bytes 294920 | tf_op jit(solution)/shard_map/ppermute | solution.py:303
  24.8 4.3 %collective-permute-start.7 = (bf16[128,128]{1,0:T(8,128)(2,1)S(1)}, bf16[128,128]{1,0:T(8,128)(2,1)S(1)}, u32[]{:S(2)}, u32[]{:S(2)}) collective-permute-start(bf16[128,128]{1,0:T(8,128)(2,1)S(1)} %get-tuple-element.49), channel_id=1, source_target_pairs={{0,7},{1,6},{2,5},{3,4},{4,3},{5,2},{6,1},{7,0},{8,15},{9,14},{10,... | collective-permute-start | bytes 98312 | tf_op jit(solution)/shard_map/ppermute | solution.py:303
  25.7 3.9 %collective-permute-start.8 = (bf16[128,128]{1,0:T(8,128)(2,1)S(1)}, bf16[128,128]{1,0:T(8,128)(2,1)S(1)}, u32[]{:S(2)}, u32[]{:S(2)}) collective-permute-start(bf16[128,128]{1,0:T(8,128)(2,1)S(1)} %get-tuple-element.50), channel_id=1, source_target_pairs={{0,1},{1,0},{2,3},{3,2},{4,5},{5,4},{6,7},{7,6},{8,9},{9,8},{10,11... | collective-permute-start | bytes 98312 | tf_op jit(solution)/shard_map/ppermute | solution.py:303
  26.7 3.7 %collective-permute-start.9 = (bf16[128,128]{1,0:T(8,128)(2,1)S(1)}, bf16[128,128]{1,0:T(8,128)(2,1)S(1)}, u32[]{:S(2)}, u32[]{:S(2)}) collective-permute-start(bf16[128,128]{1,0:T(8,128)(2,1)S(1)} %get-tuple-element.51), channel_id=1, source_target_pairs={{0,6},{1,7},{2,4},{3,5},{4,2},{5,3},{6,0},{7,1},{8,14},{9,15},{10,... | collective-permute-start | bytes 98312 | tf_op jit(solution)/shard_map/ppermute | solution.py:303

commit v8 on v5

--- a/solution.py
+++ b/solution.py
@@ -28,7 +28,7 @@
     return [float(c) for c in cheb.convert(kind=np.polynomial.Polynomial).coef]
 
 
-cosine = fit_cosine(6)
+cosine = fit_cosine(5)
 
 
 def dot(a, b, dims):

time: 31.5 us -> 31.5 us (level)
  no operation moved by 1% of the time
where the time goes in v8:
time: 31.5 us; the launch traced here: 31.2 us
  starting transfers between devices  13.2 us (42%)
  waiting for transfers between devices  11.2 us (36%)
  Pallas kernels  4.44 us (14%)
  local copies, waits for them, and re-layouts  1.87 us (6%)
  other arithmetic  0.37 us (1%)
    ppermute x10, starting transfers between devices, swap(): return lax.ppermute(x, both, [(i, i ^ mask) for i in range(devices)])  13.2 us
    ppermute x10, waiting for transfers between devices, swap(): return lax.ppermute(x, both, [(i, i ^ mask) for i in range(devices)])  11.2 us
    pallas_call x12, Pallas kernels, call(): pl.pallas_call(body, out_shape=outs if len(outs) > 1 else outs[0], in_spe...  4.44 us
    unnamed x25, local copies, waits for them, and re-layouts  1.86 us
  transfers between devices with their start and end apart: 10, of which 9 were waited for; matrix products, arithmetic and copies ran while one was open for 1% of the time, Pallas kernels for 8%

profile of v8, /device:TPU:0, one launch (start us, length us, event | category | flops | bytes accessed | tf_op | source)
XLA Modules:
  0.0 31.2 jit_solution(8544355549577617327)
XLA Ops:
  0.1 0.7 %copy-done.11 = f32[256,3]{0,1:T(4,128)S(1)} copy-done((f32[256,3]{0,1:T(4,128)S(1)}, f32[256,3]{0,1:T(4,128)}, u32[]{:S(2)}) %copy-start.11) | copy-done | bytes 3096
  0.9 2.5 %collective-permute-start.2 = (bf16[160,128]{1,0:T(8,128)(2,1)S(1)}, bf16[160,128]{1,0:T(8,128)(2,1)S(1)}, u32[]{:S(2)}, u32[]{:S(2)}) collective-permute-start(bf16[160,128]{1,0:T(8,128)(2,1)S(1)} %pad_maximum_fusion.1.block_ref.refs_0_), channel_id=1, source_target_pairs={{0,6},{1,7},{2,4},{3,5},{4,2},{5,3},{6,0},{7,1},{8,14},{9,15},{10,... | collective-permute-start | bytes 122888 | tf_op jit(solution)/shard_map/ppermute | solution.py:305
  3.3 1.5 %collective-permute-start = (bf16[128,128]{1,0:T(8,128)(2,1)S(1)}, bf16[128,128]{1,0:T(8,128)(2,1)S(1)}, u32[]{:S(2)}, u32[]{:S(2)}) collective-permute-start(bf16[128,128]{1,0:T(8,128)(2,1)S(1)} %shard_map.118.block_ref), channel_id=1, source_target_pairs={{0,1},{1,0},{2,3},{3,2},{4,5},{5,4},{6,7},{7,6},{8,9},{9,8},{10,11... | collective-permute-start | bytes 98312 | tf_op jit(solution)/shard_map/ppermute | solution.py:305
  4.8 0.3 collective-permute-start.1
  5.1 0.4 %copy-done.5 = s32[768,3]{0,1:T(4,128)S(1)} copy-done((s32[768,3]{0,1:T(4,128)S(1)}, s32[768,3]{0,1:T(4,128)}, u32[]{:S(2)}) %copy-start.5) | copy-done | bytes 9240
  5.5 0.7 %shard_map.120 = (bf16[16,768]{1,0:T(8,128)(2,1)S(1)}, bf16[256,768]{1,0:T(8,128)(2,1)S(1)}) custom-call(s32[3,768]{1,0:T(4,128)S(1)} %bitcast.10, bf16[160,128]{1,0:T(8,128)(2,1)S(1)} %pad_maximum_fusion.1.block_ref.refs_0_), custom_call_target="tpu_custom_call" | custom-call | flops 2949120000 | bytes 467968 | tf_op jit(solution)/shard_map/pallas_call | solution.py:44
  6.4 0.9 %collective-permute-done.refs_1_.refs_4_ = bf16[128,128]{1,0:T(8,128)(2,1)S(1)} collective-permute-done((bf16[128,128]{1,0:T(8,128)(2,1)S(1)}, bf16[128,128]{1,0:T(8,128)(2,1)S(1)}, u32[]{:S(2)}, u32[]{:S(2)}) %collective-permute-start) | collective-permute-done | bytes 32800 | tf_op jit(solution)/shard_map/ppermute | solution.py:305
  7.3 0.3 shard_map.122.refs_3_
  7.6 0.5 %shard_map.121.refs_2_.refs_1_ = bf16[256,768]{1,0:T(8,128)(2,1)S(1)} custom-call(bf16[160,128]{1,0:T(8,128)(2,1)S(1)} %collective-permute-done.2.block_ref.refs_0_, bf16[16,768]{1,0:T(8,128)(2,1)S(1)} %get-tuple-element.28.wave_ref), custom_call_target="tpu_custom_call" | custom-call | flops 1474560000 | bytes 458752 | tf_op jit(solution)/shard_map/pallas_call | solution.py:44
  8.1 0.9 %collective-permute-done.1.refs_1_.refs_5_.refs_2_ = bf16[128,128]{1,0:T(8,128)(2,1)S(1)} collective-permute-done((bf16[128,128]{1,0:T(8,128)(2,1)S(1)}, bf16[128,128]{1,0:T(8,128)(2,1)S(1)}, u32[]{:S(2)}, u32[]{:S(2)}) %collective-permute-start.1) | collective-permute-done | bytes 32800 | tf_op jit(solution)/shard_map/ppermute | solution.py:305
  9.1 0.3 shard_map.123
  9.4 0.5 %collective-permute-start.3 = (bf16[448,128]{1,0:T(8,128)(2,1)S(1)}, bf16[448,128]{1,0:T(8,128)(2,1)S(1)}, u32[]{:S(2)}, u32[]{:S(2)}) collective-permute-start(bf16[448,128]{1,0:T(8,128)(2,1)S(1)} %get-tuple-element.30), channel_id=1, source_target_pairs={{0,2},{1,3},{2,0},{3,1},{4,6},{5,7},{6,4},{7,5},{8,10},{9,11},{10,... | collective-permute-start | bytes 344072 | tf_op jit(solution)/shard_map/ppermute | solution.py:305
  10.0 0.9 %collective-permute-done.3.refs_3_ = bf16[448,128]{1,0:T(8,128)(2,1)S(1)} collective-permute-done((bf16[448,128]{1,0:T(8,128)(2,1)S(1)}, bf16[448,128]{1,0:T(8,128)(2,1)S(1)}, u32[]{:S(2)}, u32[]{:S(2)}) %collective-permute-start.3) | collective-permute-done | bytes 114720 | tf_op jit(solution)/shard_map/ppermute | solution.py:305
  10.9 1.6 %collective-permute-start.4 = (bf16[416,128]{1,0:T(8,128)(2,1)S(1)}, bf16[416,128]{1,0:T(8,128)(2,1)S(1)}, u32[]{:S(2)}, u32[]{:S(2)}) collective-permute-start(bf16[416,128]{1,0:T(8,128)(2,1)S(1)} %add_convert_fusion), channel_id=1, source_target_pairs={{0,10},{1,11},{2,8},{3,9},{4,14},{5,15},{6,12},{7,13},{8,2},{9,3},... | collective-permute-start | bytes 319496 | tf_op jit(solution)/shard_map/ppermute | solution.py:305
  12.5 3.2 %collective-permute-done.4.refs_4_ = bf16[416,128]{1,0:T(8,128)(2,1)S(1)} collective-permute-done((bf16[416,128]{1,0:T(8,128)(2,1)S(1)}, bf16[416,128]{1,0:T(8,128)(2,1)S(1)}, u32[]{:S(2)}, u32[]{:S(2)}) %collective-permute-start.4) | collective-permute-done | bytes 106528 | tf_op jit(solution)/shard_map/ppermute | solution.py:305
  15.8 0.1 fusion.refs_7_.a_ref
  15.9 3.6 %collective-permute-start.5 = (bf16[416,128]{1,0:T(8,128)(2,1)S(1)}, bf16[416,128]{1,0:T(8,128)(2,1)S(1)}, u32[]{:S(2)}, u32[]{:S(2)}) collective-permute-start(bf16[416,128]{1,0:T(8,128)(2,1)S(1)} %fusion.refs_7_.a_ref), channel_id=1, source_target_pairs={{0,26},{1,27},{2,24},{3,25},{4,30},{5,31},{6,28},{7,29},{8,18},{9,... | collective-permute-start | bytes 319496 | tf_op jit(solution)/shard_map/ppermute | solution.py:305
  19.5 0.6 %copy-done.8 = f32[128]{0:T(128)S(1)} copy-done((f32[128]{0:T(128)S(1)}, f32[128]{0:T(128)}, u32[]{:S(2)}) %copy-start.8) | copy-done | bytes 536
  20.1 2.6 %collective-permute-done.5.refs_5_.b_ref = bf16[416,128]{1,0:T(8,128)(2,1)S(1)} collective-permute-done((bf16[416,128]{1,0:T(8,128)(2,1)S(1)}, bf16[416,128]{1,0:T(8,128)(2,1)S(1)}, u32[]{:S(2)}, u32[]{:S(2)}) %collective-permute-start.5) | collective-permute-done | bytes 106528 | tf_op jit(solution)/shard_map/ppermute | solution.py:305
  22.7 0.3 %shard_map.126.refs_2_ = bf16[128,384]{1,0:T(8,128)(2,1)S(1)} custom-call(bf16[416,128]{1,0:T(8,128)(2,1)S(1)} %fusion.refs_7_.a_ref, bf16[416,128]{1,0:T(8,128)(2,1)S(1)} %collective-permute-done.5.refs_5_.b_ref, bf16[2,128,128]{2,1,0:T(8,128)(2,1)S(1)} %copy-done.1, f32[128,384]{1,0:T(8,128)S(1)} %pad_maximum_fusion.filter_ref), custom_call_target="tpu_custom_call" | custom-call | flops 25165824 | bytes 573440 | tf_op jit(solution)/shard_map/pallas_call | solution.py:44
  23.1 0.3 collective-permute-start.6
  23.3 0.3 shard_map.127.refs_3_
  23.6 0.8 %collective-permute-done.6.refs_2_ = bf16[128,384]{1,0:T(8,128)(2,1)S(1)} collective-permute-done((bf16[128,384]{1,0:T(8,128)(2,1)S(1)}, bf16[128,384]{1,0:T(8,128)(2,1)S(1)}, u32[]{:S(2)}, u32[]{:S(2)}) %collective-permute-start.6) | collective-permute-done | bytes 98336 | tf_op jit(solution)/shard_map/ppermute | solution.py:305
  24.4 0.3 shard_map.128
  24.7 1.0 %collective-permute-start.7 = (bf16[128,128]{1,0:T(8,128)(2,1)S(1)}, bf16[128,128]{1,0:T(8,128)(2,1)S(1)}, u32[]{:S(2)}, u32[]{:S(2)}) collective-permute-start(bf16[128,128]{1,0:T(8,128)(2,1)S(1)} %get-tuple-element.45), channel_id=1, source_target_pairs={{0,7},{1,6},{2,5},{3,4},{4,3},{5,2},{6,1},{7,0},{8,15},{9,14},{10,... | collective-permute-start | bytes 98312 | tf_op jit(solution)/shard_map/ppermute | solution.py:305
  25.7 1.1 %collective-permute-start.8 = (bf16[128,128]{1,0:T(8,128)(2,1)S(1)}, bf16[128,128]{1,0:T(8,128)(2,1)S(1)}, u32[]{:S(2)}, u32[]{:S(2)}) collective-permute-start(bf16[128,128]{1,0:T(8,128)(2,1)S(1)} %get-tuple-element.46), channel_id=1, source_target_pairs={{0,1},{1,0},{2,3},{3,2},{4,5},{5,4},{6,7},{7,6},{8,9},{9,8},{10,11... | collective-permute-start | bytes 98312 | tf_op jit(solution)/shard_map/ppermute | solution.py:305
  26.8 0.9 %collective-permute-start.9 = (bf16[128,128]{1,0:T(8,128)(2,1)S(1)}, bf16[128,128]{1,0:T(8,128)(2,1)S(1)}, u32[]{:S(2)}, u32[]{:S(2)}) collective-permute-start(bf16[128,128]{1,0:T(8,128)(2,1)S(1)} %get-tuple-element.47), channel_id=1, source_target_pairs={{0,6},{1,7},{2,4},{3,5},{4,2},{5,3},{6,0},{7,1},{8,14},{9,15},{10,... | collective-permute-start | bytes 98312 | tf_op jit(solution)/shard_map/ppermute | solution.py:305
  27.7 0.7 %shard_map.125.refs_0_ = f32[128,128]{1,0:T(8,128)S(1)} custom-call(bf16[160,128]{1,0:T(8,128)(2,1)S(1)} %pad_maximum_fusion.1.block_ref.refs_0_, bf16[128,128]{1,0:T(8,128)(2,1)S(1)} %collective-permute-done.refs_1_.refs_4_, bf16[128,128]{1,0:T(8,128)(2,1)S(1)} %collective-permute-done.1.refs_1_.refs_5_.refs_2_, ...), custom_call_target="tpu_custom_call" | custom-call | flops 100663296 | bytes 549376 | tf_op jit(solution)/shard_map/pallas_call | solution.py:44
  28.4 0.6 %collective-permute-done.7.refs_2_ = bf16[128,128]{1,0:T(8,128)(2,1)S(1)} collective-permute-done((bf16[128,128]{1,0:T(8,128)(2,1)S(1)}, bf16[128,128]{1,0:T(8,128)(2,1)S(1)}, u32[]{:S(2)}, u32[]{:S(2)}) %collective-permute-start.7) | collective-permute-done | bytes 32800 | tf_op jit(solution)/shard_map/ppermute | solution.py:305
  29.0 0.6 %collective-permute-done.8.refs_3_ = bf16[128,128]{1,0:T(8,128)(2,1)S(1)} collective-permute-done((bf16[128,128]{1,0:T(8,128)(2,1)S(1)}, bf16[128,128]{1,0:T(8,128)(2,1)S(1)}, u32[]{:S(2)}, u32[]{:S(2)}) %collective-permute-start.8) | collective-permute-done | bytes 32800 | tf_op jit(solution)/shard_map/ppermute | solution.py:305
  29.6 0.6 %collective-permute-done.9.refs_4_ = bf16[128,128]{1,0:T(8,128)(2,1)S(1)} collective-permute-done((bf16[128,128]{1,0:T(8,128)(2,1)S(1)}, bf16[128,128]{1,0:T(8,128)(2,1)S(1)}, u32[]{:S(2)}, u32[]{:S(2)}) %collective-permute-start.9) | collective-permute-done | bytes 32800 | tf_op jit(solution)/shard_map/ppermute | solution.py:305
  30.2 1.0 %shard_map.129 = bf16[128,128]{1,0:T(8,128)(2,1)} custom-call(f32[128,128]{1,0:T(8,128)S(1)} %shard_map.125.refs_0_, f32[128,128]{1,0:T(8,128)S(1)} %get-tuple-element.44.refs_1_, bf16[128,128]{1,0:T(8,128)(2,1)S(1)} %collective-permute-done.7.refs_2_, bf16[128,128]{1,0:T(8,128)(2,1)S(1)} %collective-permute-done.8.refs_3_, ...), custom_call_target="tpu_custom_call" | custom-call | flops 33554432 | bytes 524800 | tf_op jit(solution)/shard_map/pallas_call | solution.py:44
  (37 shorter events, 0.4 us)
Async XLA Ops:
  0.0 6.3 %copy-start = (f32[768,128]{1,0:T(8,128)S(1)}, f32[768,128]{1,0:T(8,128)}, u32[]{:S(2)}) copy-start(f32[768,128]{1,0:T(8,128)} %param.15) | copy-start | bytes 1179652
  0.0 0.7 %copy-start.11 = (f32[256,3]{0,1:T(4,128)S(1)}, f32[256,3]{0,1:T(4,128)}, u32[]{:S(2)}) copy-start(f32[256,3]{0,1:T(4,128)} %param.13) | copy-start | bytes 9220
  0.0 0.8 %copy-start.10 = (bf16[128,128]{1,0:T(8,128)(2,1)S(1)}, bf16[128,128]{1,0:T(8,128)(2,1)}, u32[]{:S(2)}) copy-start(bf16[128,128]{1,0:T(8,128)(2,1)} %param.12) | copy-start | bytes 98308
  0.9 6.7 %collective-permute-start.2 = (bf16[160,128]{1,0:T(8,128)(2,1)S(1)}, bf16[160,128]{1,0:T(8,128)(2,1)S(1)}, u32[]{:S(2)}, u32[]{:S(2)}) collective-permute-start(bf16[160,128]{1,0:T(8,128)(2,1)S(1)} %pad_maximum_fusion.1.block_ref.refs_0_), channel_id=1, source_target_pairs={{0,6},{1,7},{2,4},{3,5},{4,2},{5,3},{6,0},{7,1},{8,14},{9,15},{10,... | collective-permute-start | bytes 122888 | tf_op jit(solution)/shard_map/ppermute | solution.py:305
  3.3 4.0 %collective-permute-start = (bf16[128,128]{1,0:T(8,128)(2,1)S(1)}, bf16[128,128]{1,0:T(8,128)(2,1)S(1)}, u32[]{:S(2)}, u32[]{:S(2)}) collective-permute-start(bf16[128,128]{1,0:T(8,128)(2,1)S(1)} %shard_map.118.block_ref), channel_id=1, source_target_pairs={{0,1},{1,0},{2,3},{3,2},{4,5},{5,4},{6,7},{7,6},{8,9},{9,8},{10,11... | collective-permute-start | bytes 98312 | tf_op jit(solution)/shard_map/ppermute | solution.py:305
  4.8 0.7 %copy-start.5 = (s32[768,3]{0,1:T(4,128)S(1)}, s32[768,3]{0,1:T(4,128)}, u32[]{:S(2)}) copy-start(s32[768,3]{0,1:T(4,128)} %param.14) | copy-start | bytes 27652
  4.8 4.2 %collective-permute-start.1 = (bf16[128,128]{1,0:T(8,128)(2,1)S(1)}, bf16[128,128]{1,0:T(8,128)(2,1)S(1)}, u32[]{:S(2)}, u32[]{:S(2)}) collective-permute-start(bf16[128,128]{1,0:T(8,128)(2,1)S(1)} %shard_map.119), channel_id=1, source_target_pairs={{0,7},{1,6},{2,5},{3,4},{4,3},{5,2},{6,1},{7,0},{8,15},{9,14},{10,... | collective-permute-start | bytes 98312 | tf_op jit(solution)/shard_map/ppermute | solution.py:305
  9.4 1.5 %collective-permute-start.3 = (bf16[448,128]{1,0:T(8,128)(2,1)S(1)}, bf16[448,128]{1,0:T(8,128)(2,1)S(1)}, u32[]{:S(2)}, u32[]{:S(2)}) collective-permute-start(bf16[448,128]{1,0:T(8,128)(2,1)S(1)} %get-tuple-element.30), channel_id=1, source_target_pairs={{0,2},{1,3},{2,0},{3,1},{4,6},{5,7},{6,4},{7,5},{8,10},{9,11},{10,... | collective-permute-start | bytes 344072 | tf_op jit(solution)/shard_map/ppermute | solution.py:305
  10.9 4.9 %collective-permute-start.4 = (bf16[416,128]{1,0:T(8,128)(2,1)S(1)}, bf16[416,128]{1,0:T(8,128)(2,1)S(1)}, u32[]{:S(2)}, u32[]{:S(2)}) collective-permute-start(bf16[416,128]{1,0:T(8,128)(2,1)S(1)} %add_convert_fusion), channel_id=1, source_target_pairs={{0,10},{1,11},{2,8},{3,9},{4,14},{5,15},{6,12},{7,13},{8,2},{9,3},... | collective-permute-start | bytes 319496 | tf_op jit(solution)/shard_map/ppermute | solution.py:305
  12.5 7.0 %copy-start.2 = (bf16[128,512]{1,0:T(8,128)(2,1)S(1)}, bf16[128,512]{1,0:T(8,128)(2,1)}, u32[]{:S(2)}) copy-start(bf16[128,512]{1,0:T(8,128)(2,1)} %refs_5_.1) | copy-start | bytes 393220
  12.5 7.0 %copy-start.3 = (bf16[512,128]{1,0:T(8,128)(2,1)S(1)}, bf16[512,128]{1,0:T(8,128)(2,1)}, u32[]{:S(2)}) copy-start(bf16[512,128]{1,0:T(8,128)(2,1)} %refs_6_.1) | copy-start | bytes 393220
  12.5 7.0 %copy-start.4 = (bf16[128,128]{1,0:T(8,128)(2,1)S(1)}, bf16[128,128]{1,0:T(8,128)(2,1)}, u32[]{:S(2)}) copy-start(bf16[128,128]{1,0:T(8,128)(2,1)} %refs_0_.1) | copy-start | bytes 98308
  12.5 7.0 %copy-start.6 = (f32[128,16]{0,1:T(8,128)S(1)}, f32[128,16]{0,1:T(8,128)}, u32[]{:S(2)}) copy-start(f32[128,16]{0,1:T(8,128)} %param.19) | copy-start | bytes 24580
  12.5 7.0 %copy-start.7 = (s32[128,16]{0,1:T(8,128)S(1)}, s32[128,16]{0,1:T(8,128)}, u32[]{:S(2)}) copy-start(s32[128,16]{0,1:T(8,128)} %param.20) | copy-start | bytes 24580
  15.9 6.9 %collective-permute-start.5 = (bf16[416,128]{1,0:T(8,128)(2,1)S(1)}, bf16[416,128]{1,0:T(8,128)(2,1)S(1)}, u32[]{:S(2)}, u32[]{:S(2)}) collective-permute-start(bf16[416,128]{1,0:T(8,128)(2,1)S(1)} %fusion.refs_7_.a_ref), channel_id=1, source_target_pairs={{0,26},{1,27},{2,24},{3,25},{4,30},{5,31},{6,28},{7,29},{8,18},{9,... | collective-permute-start | bytes 319496 | tf_op jit(solution)/shard_map/ppermute | solution.py:305
  19.4 0.7 %copy-start.8 = (f32[128]{0:T(128)S(1)}, f32[128]{0:T(128)}, u32[]{:S(2)}) copy-start(f32[128]{0:T(128)} %param.18) | copy-start | bytes 1540
  19.4 0.7 %copy-start.9 = (f32[128]{0:T(128)S(1)}, f32[128]{0:T(128)}, u32[]{:S(2)}) copy-start(f32[128]{0:T(128)} %param.21) | copy-start | bytes 1540
  20.1 2.6 %copy-start.1 = (bf16[2,128,128]{2,1,0:T(8,128)(2,1)S(1)}, bf16[2,128,128]{2,1,0:T(8,128)(2,1)}, u32[]{:S(2)}) copy-start(bf16[2,128,128]{2,1,0:T(8,128)(2,1)} %mix_ref.1) | copy-start | bytes 196612
  23.1 1.4 %collective-permute-start.6 = (bf16[128,384]{1,0:T(8,128)(2,1)S(1)}, bf16[128,384]{1,0:T(8,128)(2,1)S(1)}, u32[]{:S(2)}, u32[]{:S(2)}) collective-permute-start(bf16[128,384]{1,0:T(8,128)(2,1)S(1)} %shard_map.126.refs_2_), channel_id=1, source_target_pairs={{0,2},{1,3},{2,0},{3,1},{4,6},{5,7},{6,4},{7,5},{8,10},{9,11},{10,... | collective-permute-start | bytes 294920 | tf_op jit(solution)/shard_map/ppermute | solution.py:305
  24.7 4.3 %collective-permute-start.7 = (bf16[128,128]{1,0:T(8,128)(2,1)S(1)}, bf16[128,128]{1,0:T(8,128)(2,1)S(1)}, u32[]{:S(2)}, u32[]{:S(2)}) collective-permute-start(bf16[128,128]{1,0:T(8,128)(2,1)S(1)} %get-tuple-element.45), channel_id=1, source_target_pairs={{0,7},{1,6},{2,5},{3,4},{4,3},{5,2},{6,1},{7,0},{8,15},{9,14},{10,... | collective-permute-start | bytes 98312 | tf_op jit(solution)/shard_map/ppermute | solution.py:305
  25.7 3.9 %collective-permute-start.8 = (bf16[128,128]{1,0:T(8,128)(2,1)S(1)}, bf16[128,128]{1,0:T(8,128)(2,1)S(1)}, u32[]{:S(2)}, u32[]{:S(2)}) collective-permute-start(bf16[128,128]{1,0:T(8,128)(2,1)S(1)} %get-tuple-element.46), channel_id=1, source_target_pairs={{0,1},{1,0},{2,3},{3,2},{4,5},{5,4},{6,7},{7,6},{8,9},{9,8},{10,11... | collective-permute-start | bytes 98312 | tf_op jit(solution)/shard_map/ppermute | solution.py:305
  26.8 3.4 %collective-permute-start.9 = (bf16[128,128]{1,0:T(8,128)(2,1)S(1)}, bf16[128,128]{1,0:T(8,128)(2,1)S(1)}, u32[]{:S(2)}, u32[]{:S(2)}) collective-permute-start(bf16[128,128]{1,0:T(8,128)(2,1)S(1)} %get-tuple-element.47), channel_id=1, source_target_pairs={{0,6},{1,7},{2,4},{3,5},{4,2},{5,3},{6,0},{7,1},{8,14},{9,15},{10,... | collective-permute-start | bytes 98312 | tf_op jit(solution)/shard_map/ppermute | solution.py:305
